TPU v7x, 32 devices: a whole 2x2x4 slice. The times are simulated.
32 devices in a mesh: expert: 4 (over z), seq: 4 (over x, core), fsdp: 2 (over y).
Axes of the slice: x: 2, y: 2, z: 4, core: 2. Of those that a mesh axis runs over, the one named last changes fastest.
Arguments:
- tokens: float32 [7168, 1280], P(('expert', 'seq', 'fsdp')), may hold values from -100 to 100
- slot_params: float32 [1280, 32], replicated, may hold values from -4 to 4
- w_in: float32 [8, 2560, 1280], P('expert', ('seq', 'fsdp')), may hold values from -0.15625 to 0.15625
- w_out: float32 [8, 2560, 1280], P('expert', ('seq', 'fsdp')), may hold values from -0.125 to 0.125
Outputs:
- mixed: float32 [7168, 1280], P(('expert', 'seq', 'fsdp'))
All inputs are finite; a program needn't handle non-finite values.
Results may differ from a plain program's by a relative error of at most 0.0003.
Values sent between devices are 32-bit elements; how exact they have to be, the bound alone decides.
No kernel may reach another device: no remote copies, remote signals or barrier semaphores. Data moves between devices by JAX's collectives and lax.ppermute only.
A program may use at most 64 MiB of HBM per device.

v0:
```python
import jax
import jax.numpy as jnp
from jax import lax
from jax.sharding import PartitionSpec as P

D = 1280
SLOTS = 4


def combined_all(value, axis, join):
    pieces = jax.tree.map(lambda part: lax.all_gather(part, axis), value)
    head = jax.tree.map(lambda part: part[0], pieces)
    tail = jax.tree.map(lambda part: part[1:], pieces)
    total, _ = lax.scan(lambda total, section: (join(total, section), None), head, tail)
    return total


def join_parts(left_part, right_part):
    top_value = jnp.maximum(left_part[0], right_part[0])
    left_scale = jnp.exp(left_part[0] - top_value)
    right_scale = jnp.exp(right_part[0] - top_value)
    joined_mass = left_part[1] * left_scale + right_part[1] * right_scale
    joined_sums = left_part[2] * left_scale[:, None] + right_part[2] * right_scale[:, None]
    return (top_value, joined_mass, joined_sums)


def slot_terms(logits, tokens, slot_peak):
    weights = jnp.exp(logits - slot_peak)
    slot_mass = jnp.sum(weights, axis=0)
    slot_sums = lax.dot_general(
        weights,
        tokens,
        (((0,), (0,)), ((), ())),
        precision=lax.Precision.HIGHEST,
        preferred_element_type=jnp.float32,
    )
    return (slot_mass, slot_sums)


def body(tokens, slot_params, w_in, w_out):
    highest = lax.Precision.HIGHEST
    logits = jnp.dot(tokens, slot_params, precision=highest, preferred_element_type=jnp.float32)
    row_peak = jnp.max(logits, axis=1, keepdims=True)
    row_exp = jnp.exp(logits - row_peak)
    combine = row_exp / jnp.sum(row_exp, axis=1, keepdims=True)
    own_slots = w_in.shape[0] * SLOTS
    local_peak = jnp.max(logits, axis=0)
    slot_mass, slot_sums = slot_terms(logits, tokens, local_peak)
    group_peak, group_mass, group_sums = combined_all(
        (local_peak, slot_mass, slot_sums), ("seq", "fsdp"), join_parts
    )
    overall_peak = lax.pmax(group_peak, "expert")
    rescale = jnp.exp(group_peak - overall_peak)
    sums_own, mass_own = (
        lax.psum_scatter(group_sums * rescale[:, None], "expert", scatter_dimension=0, tiled=True),
        lax.psum_scatter(group_mass * rescale, "expert", scatter_dimension=0, tiled=True),
    )
    slot_inputs = (sums_own / mass_own[:, None]).reshape(w_in.shape[0], SLOTS, D)
    hidden = jax.nn.gelu(
        jnp.einsum("esd,ehd->esh", slot_inputs, w_in, precision=highest), approximate=False
    )
    partial_out = jnp.einsum("esh,ehd->esd", hidden, w_out, precision=highest).reshape(own_slots, D)
    outputs_own = lax.psum(partial_out, ("seq", "fsdp"))
    return jnp.dot(
        combine,
        lax.all_gather(outputs_own, "expert", axis=0, tiled=True),
        precision=lax.Precision.HIGHEST,
        preferred_element_type=jnp.float32,
    )


def solution(mesh):
    placed = (
        P(("expert", "seq", "fsdp"), None),
        P(),
        P("expert", ("seq", "fsdp"), None),
        P("expert", ("seq", "fsdp"), None),
    )
    return jax.shard_map(
        body,
        mesh=mesh,
        in_specs=placed,
        out_specs=P(("expert", "seq", "fsdp"), None),
        check_vma=False,
    )
```

profile of v0, /device:TPU:0, one launch (start us, length us, event | category | flops | bytes accessed | tf_op | source)
XLA Modules:
  0.0 131.8 jit_solution(4382712439911129519)
XLA Ops:
  6.5 2.6 %fusion.130 = (f32[224]{0:T(256)S(1)}, f32[32]{0:T(128)S(1)}, f32[224,32]{0,1:T(8,128)S(1)}) fusion(f32[224,1280]{1,0:T(8,128)} %param.6, f32[1280,32]{0,1:T(8,128)} %param.7), kind=kOutput, calls=%fused_computation.151 | convolution fusion | flops 110114560 | bytes 1340416 | tf_op jit(solution)/shard_map/dot_general | solution.py:42
  9.2 1.5 %fusion.9 = f32[32,1280]{1,0:T(8,128)} fusion(f32[224,1280]{1,0:T(8,128)S(1)} %copy-done.1, f32[224,32]{0,1:T(8,128)S(1)} %get-tuple-element.76, f32[32]{0:T(128)S(1)} %get-tuple-element.50), kind=kOutput, calls=%fused_computation.17 | convolution fusion | flops 110107648 | bytes 1339520 | tf_op jit(solution)/shard_map/dot_general | solution.py:30
  12.7 15.2 %all-reduce.3 = (f32[256]{0:T(256)S(1)}, f32[256]{0:T(256)S(1)}) all-reduce(f32[256]{0:T(256)S(1)} %dynamic-update-slice, f32[256]{0:T(256)S(1)} %dynamic-update-slice.1), channel_id=2, replica_groups=mesh['expert'=4,'seq'=4,'fsdp'=2] {'seq','fsdp'}, use_global_device_ids=true, to_apply=%add | all-reduce | flops 512 | bytes 4096
  28.2 10.2 %all-gather.5.cloned.1.call-done = f32[256,1280]{1,0:T(8,128)} async-done(((f32[32,1280]{1,0:T(8,128)}), f32[256,1280]{1,0:T(8,128)}) %all-gather.5.cloned.1.call-update) | async-done | bytes 1310736 | tf_op jit(solution)/shard_map/all_gather | solution.py:11
  38.4 2.4 %slice.31 = f32[224,1280]{1,0:T(8,128)} slice(f32[256,1280]{1,0:T(8,128)} %all-gather.5.cloned.1.call-done), slice={[32:256], [0:1280]} | slice | bytes 2293760 | tf_op jit(solution)/shard_map/slice | solution.py:13
  40.7 7.4 %while.14 = (s32[]{:T(128)}, f32[32]{0:T(128)S(1)}, f32[32]{0:T(128)S(1)}, f32[32,1280]{1,0:T(8,128)S(1)}, f32[7,32]{1,0:T(8,128)S(1)}, /*index=5*/f32[7,32]{1,0:T(8,128)S(1)}, f32[7,32,1280]{2,1,0:T(8,128)}, s32[]{:T(128)}) while((s32[]{:T(128)}, f32[32]{0:T(128)S(1)}, f32[32]{0:T(128)S(1)}, f32[32,1280]{1,0:T(8,128)S(1)}, ...), condition=%wide.region_5.6_spmd, body=%wide.region_4.5_spmd.sunk | while | flops 123074 | bytes 492893 | solution.py:14
  40.8 1.0 fusion.143
  41.8 1.0 fusion.143
  42.9 1.0 fusion.143
  43.9 1.0 fusion.143
  45.0 1.0 fusion.143
  46.0 1.0 fusion.143
  47.1 1.0 fusion.143
  48.1 11.7 %pmax.7 = f32[32]{0:T(128)S(1)} all-reduce(f32[32]{0:T(128)S(1)} %get-tuple-element.45), channel_id=1, replica_groups=mesh['expert'=4,'seq'=4,'fsdp'=2] {'expert'}, use_global_device_ids=true, to_apply=%region_6.7 | all-reduce | flops 32 | bytes 256 | tf_op jit(solution)/shard_map/pmax | solution.py:52
  59.8 0.8 broadcast_multiply_fusion
  60.6 0.6 dynamic-slice.2
  61.9 8.4 %all-reduce.2 = f32[32]{0:T(128)S(1)} all-reduce(f32[32]{0:T(128)S(1)} %get-tuple-element.74), channel_id=6, replica_groups=mesh['expert'=4,'seq'=4,'fsdp'=2] {'expert'}, use_global_device_ids=true, to_apply=%region_8.9.clone | all-reduce | flops 32 | bytes 256
  70.4 6.9 %reduce-scatter.2.cloned.1.call-done = f32[8,1280]{1,0:T(8,128)} async-done(((f32[32,1280]{1,0:T(8,128)}), f32[8,1280]{1,0:T(8,128)}) %reduce-scatter.2.cloned.1.call-update) | async-done | bytes 40976 | tf_op jit(solution)/shard_map/reduce_scatter | solution.py:55
  77.3 0.9 broadcast_divide_fusion
  78.2 4.7 %fusion.100 = (u8[4,320]{1,0:T(4,128)(4,1)S(1)}, u8[4,320]{1,0:T(4,128)(4,1)S(1)}, u8[4,320]{1,0:T(4,128)(4,1)S(1)}, f32[2,4,320]{2,1,0:T(4,128)S(1)}) fusion(f32[2,4,1280]{2,1,0:T(4,128)S(1)} %reshape.13, f32[2,320,1280]{2,1,0:T(8,128)} %param.8), kind=kOutput, calls=%fused_computation.120 | convolution fusion | flops 39368960 | bytes 3331840 | tf_op jit(solution)/shard_map/esd,ehd->esh/dot_general | solution.py:60
  82.9 1.7 %fusion.17 = f32[2,4,1280]{2,1,0:T(4,128)S(1)} fusion(f32[2,320,1280]{2,1,0:T(8,128)S(1)} %copy-done, pred[2,4,320]{2,1,0:T(4,128)(4,1)S(1)} %and_convert_fusion.2, pred[2,4,320]{2,1,0:T(4,128)(4,1)S(1)} %get-tuple-element.79, pred[2,4,320]{2,1,0:T(4,128)(4,1)S(1)} %get-tuple-element.78, f32[2,4,320]{2,1,0:T(4,128)S(1)} %get-tuple-element.77), kind=kOutput, calls=%fused_computation.28 | convolution fusion | flops 39477760 | bytes 3335680 | tf_op jit(solution)/shard_map/esh,ehd->esd/dot_general | solution.py:62
  84.7 24.5 %psum.7 = f32[8,1280]{1,0:T(8,128)S(1)} all-reduce(f32[8,1280]{1,0:T(8,128)S(1)} %reshape.14), channel_id=1, replica_groups=mesh['expert'=4,'seq'=4,'fsdp'=2] {'seq','fsdp'}, use_global_device_ids=true, to_apply=%region_9.10 | all-reduce | flops 10240 | bytes 81920 | tf_op jit(solution)/shard_map/psum | solution.py:63
  109.2 13.6 %all_gather.27 = f32[32,1280]{1,0:T(8,128)S(1)} all-gather(f32[8,1280]{1,0:T(8,128)S(1)} %psum.7), channel_id=1, replica_groups=mesh['expert'=4,'seq'=4,'fsdp'=2] {'expert'}, dimensions={0}, use_global_device_ids=true | all-gather | bytes 204800 | tf_op jit(solution)/shard_map/all_gather | solution.py:66
  122.8 2.1 %fusion.6 = f32[224,1280]{1,0:T(8,128)} fusion(f32[32,1280]{1,0:T(8,128)S(1)} %all_gather.27, f32[224,32]{0,1:T(8,128)S(1)} %get-tuple-element.76, f32[224]{0:T(256)S(1)} %get-tuple-element.47, f32[224]{0:T(256)S(1)} %get-tuple-element.49), kind=kOutput, calls=%fused_computation.13 | convolution fusion | flops 110114816 | bytes 1341184 | tf_op jit(solution)/shard_map/dot_general | solution.py:64
  (39 shorter events, 2.0 us)
Async XLA Ops:
  6.5 76.4 %copy-start = (f32[2,320,1280]{2,1,0:T(8,128)S(1)}, f32[2,320,1280]{2,1,0:T(8,128)}, u32[]{:S(2)}) copy-start(f32[2,320,1280]{2,1,0:T(8,128)} %param.9) | copy-start | bytes 9830404
  6.5 4.2 %copy-start.3 = (u32[32]{0:T(128)S(1)}, u32[32]{0:T(128)}, u32[]{:S(2)}) copy-start(u32[32]{0:T(128)} %constant.79) | copy-start | bytes 388
  6.5 31.8 %all-gather.5.cloned.1.call-start = ((), (), s32[]{:S(2)}) async-start(), calls=%async_computation.2 | async-start | bytes 1474560 | tf_op jit(solution)/shard_map/all_gather | solution.py:11
  6.5 2.7 %copy-start.1 = (f32[224,1280]{1,0:T(8,128)S(1)}, f32[224,1280]{1,0:T(8,128)}, u32[]{:S(2)}) copy-start(f32[224,1280]{1,0:T(8,128)} %param.6) | copy-start | bytes 3440644
  10.7 66.6 %reduce-scatter.2.cloned.1.call-start = ((), (), s32[]{:S(2)}) async-start(), calls=%async_computation.1 | async-start | bytes 204800 | tf_op jit(solution)/shard_map/reduce_scatter | solution.py:55
  38.4 2.4 %slice-start = ((f32[256,1280]{1,0:T(8,128)}), f32[32,1280]{1,0:T(8,128)S(1)}, s32[]{:S(2)}) async-start(f32[256,1280]{1,0:T(8,128)} %all-gather.5.cloned.1.call-done), calls=%async_computation.3 | async-start | bytes 327680 | tf_op jit(solution)/shard_map/slice | solution.py:12
  40.7 19.9 %copy-start.2 = (u32[32]{0:T(128)S(1)}, u32[32]{0:T(128)}, u32[]{:S(2)}) copy-start(u32[32]{0:T(128)} %constant.91) | copy-start | bytes 388
Sparse Core Ops, SparseCore 0:
  10.8 27.5 all-gather.4
  60.7 16.5 reduce-scatter.1
where the time goes:
time: 132 us
  blocking collectives  73.4 us (56%)
  waiting for transfers between devices  17.1 us (13%)
  between operations  14.8 us (11%)
  matrix products  12.6 us (10%)
  other arithmetic  9.11 us (7%)
  local copies, waits for them, and re-layouts  4.56 us (3%)
    psum x1, blocking collectives, body(): outputs_own = lax.psum(partial_out, ('seq', 'fsdp'))  24.5 us
    unnamed x2, blocking collectives  23.6 us
    all_gather x1, blocking collectives, body(): lax.all_gather(outputs_own, 'expert', axis=0, tiled=True)  13.6 us
    pmax x1, blocking collectives, body(): overall_peak = lax.pmax(group_peak, 'expert')  11.7 us
    all_gather x1, waiting for transfers between devices, combined_all(): pieces = jax.tree.map(lambda part: lax.all_gather(part, axis), value)  10.2 us
    add x7, other arithmetic, join_parts(): left_part[2] * left_scale[:, None] + right_part[2] * right_scale[:, None]  7.1 us
    reduce_scatter x1, waiting for transfers between devices, body(): lax.psum_scatter(group_sums * rescale[:, None], 'expert', scatter_dimensi...  6.93 us
    dot_general x1, matrix products, body(): jnp.einsum('esd,ehd->esh', slot_inputs, w_in, precision=highest)  4.7 us
  transfers between devices with their start and end apart: 2, of which 2 were waited for; matrix products, arithmetic and copies ran while one was open for 2% of the time, Pallas kernels for 0%

commit v1 on v0

v1 whole, which is shorter than its diff:
```python
import functools

import jax
import jax.numpy as jnp
from jax import lax
from jax.experimental import pallas as pl
from jax.experimental.pallas import tpu as pltpu
from jax.sharding import PartitionSpec as P

SLOTS = 4
LANES = 128
AXES = ("expert", "seq", "fsdp")
VMEM = pl.BlockSpec(memory_space=pltpu.VMEM)
SMEM = pl.BlockSpec(memory_space=pltpu.SMEM)


def pieces(value, count):
    out = []
    for _ in range(count):
        part = value.astype(jnp.bfloat16)
        out.append(part)
        value = value - part.astype(jnp.float32)
    return out


def mm(left, right, contract=((1,), (0,))):
    return lax.dot_general(left, right, (contract, ((), ())), preferred_element_type=jnp.float32)


def pick(core, when_zero, when_one):
    return jnp.where(core == 0, when_zero, when_one)


def dispatch_kernel(core_ref, tokens_ref, params_ref, logits_ref, mine_ref, theirs_ref):
    core = core_ref[0]
    groups, tiles, rows, _ = mine_ref.shape
    half = tiles - 2
    slots = params_ref.shape[1]
    count = tokens_ref.shape[0]
    token_parts = pieces(tokens_ref[...], 3)
    param_parts = pieces(params_ref[...], 3)
    products = mm(jnp.concatenate(token_parts, axis=0), jnp.concatenate(param_parts, axis=1))

    def term(i, j):
        return products[i * count:(i + 1) * count, j * slots:(j + 1) * slots]

    small = term(0, 2) + term(1, 1) + term(2, 0)
    logits = (small + (term(0, 1) + term(1, 0))) + term(0, 0)
    logits = logits.T
    logits_ref[...] = logits
    peak = jnp.max(logits, axis=1, keepdims=True)
    weights = jnp.exp(logits - peak)
    mass = jnp.sum(weights, axis=1, keepdims=True)
    weight_parts = pieces(weights, 2)
    high = mm(jnp.concatenate(weight_parts, axis=0), token_parts[0])
    sums = high[:slots] + (high[slots:] + mm(weight_parts[0], token_parts[1]))
    peak = jnp.broadcast_to(peak, (slots, LANES))
    mass = jnp.broadcast_to(mass, (slots, LANES))
    for g in range(groups):
        own = slice(g * rows, (g + 1) * rows)
        for t in range(half):
            first = sums[own, t * LANES:(t + 1) * LANES]
            second = sums[own, (t + half) * LANES:(t + half + 1) * LANES]
            mine_ref[g, t] = pick(core, first, second)
            theirs_ref[g, t] = pick(core, second, first)
        for ref in (mine_ref, theirs_ref):
            ref[g, half] = mass[own]
            ref[g, half + 1] = peak[own]


def combine_kernel(logits_ref, out_ref):
    logits = logits_ref[...]
    top = jnp.max(logits, axis=0, keepdims=True)
    powers = jnp.exp(logits - top)
    combine = (powers / jnp.sum(powers, axis=0, keepdims=True)).T
    high, low = pieces(combine, 2)
    out_ref[...] = jnp.concatenate([high, low, high], axis=1)


def expert_kernel(core_ref, mine_ref, theirs_ref, w_in_ref, w_out_ref, own_ref, send_ref):
    core = core_ref[0]
    half = own_ref.shape[0]
    rows = own_ref.shape[1]
    experts, units, width = w_in_ref.shape
    mine = [mine_ref[t] / mine_ref[half] for t in range(half)]
    theirs = [theirs_ref[t] / theirs_ref[half] for t in range(half)]
    first = [pick(core, a, b) for a, b in zip(mine, theirs)]
    second = [pick(core, b, a) for a, b in zip(mine, theirs)]
    inputs = jnp.concatenate(first + second, axis=1)
    high, low = pieces(inputs, 2)
    both = jnp.concatenate([high.astype(jnp.float32), low.astype(jnp.float32)], axis=0).astype(jnp.bfloat16)
    w_high, w_low = pieces(w_in_ref[...].reshape(experts * units, width), 2)
    nt = ((1,), (1,))
    large = mm(w_high, both, nt).T
    small = mm(w_low, both, nt).T
    value = large[:rows] + (large[rows:] + small[:rows])
    value = value * (1.0 + lax.erf(value * (0.5 ** 0.5))) * 0.5
    slot = lax.broadcasted_iota(jnp.int32, value.shape, 0)
    unit = lax.broadcasted_iota(jnp.int32, value.shape, 1)
    keep = None
    for e in range(experts):
        inside = (slot // SLOTS == e) & (unit >= e * units) & (unit < (e + 1) * units)
        keep = inside if keep is None else keep | inside
    value = jnp.where(keep, value, 0.0)
    high, low = pieces(value, 2)
    both = jnp.concatenate([high.astype(jnp.float32), low.astype(jnp.float32)], axis=0).astype(jnp.bfloat16)
    w_high, w_low = pieces(w_out_ref[...].reshape(experts * units, width), 2)
    large = mm(both, w_high)
    small = mm(both, w_low)
    out = large[:rows] + (large[rows:] + small[:rows])
    for t in range(half):
        first = out[:, t * LANES:(t + 1) * LANES]
        second = out[:, (t + half) * LANES:(t + half + 1) * LANES]
        own_ref[t] = pick(core, first, second)
        send_ref[t] = pick(core, second, first)


def mix_kernel(core_ref, combine_ref, mine_ref, theirs_ref, out_ref, stack_ref):
    core, expert = core_ref[0], core_ref[1]
    groups, half, rows, _ = mine_ref.shape
    slots = groups * rows
    for k in range(groups):
        place = pl.ds(pl.multiple_of((expert ^ k) * rows, rows), rows)
        for t in range(half):
            stack_ref[place, t * LANES:(t + 1) * LANES] = pick(core, mine_ref[k, t], theirs_ref[k, t])
            stack_ref[place, (t + half) * LANES:(t + half + 1) * LANES] = pick(core, theirs_ref[k, t], mine_ref[k, t])
    high, low = pieces(stack_ref[...], 2)
    out_ref[...] = mm(combine_ref[...], jnp.concatenate([high, high, low], axis=0))


def join(parts, axis):
    size = parts[0].shape[axis] - 1
    peaks = [lax.slice_in_dim(p, size, size + 1, axis=axis) for p in parts]
    top = functools.reduce(jnp.maximum, peaks)
    total = sum(lax.slice_in_dim(p, 0, size, axis=axis) * jnp.exp(q - top) for p, q in zip(parts, peaks))
    return jnp.concatenate([total, top], axis=axis)


def solution(mesh):
    n_expert, n_seq, n_fsdp = (mesh.shape[a] for a in AXES)
    n_x = n_seq // 2

    def permute(value, target):
        pairs = []
        for e in range(n_expert):
            for s in range(n_seq):
                for f in range(n_fsdp):
                    te, tx, tc, tf = target(e, s // 2, s % 2, f)
                    pairs.append(((e * n_seq + s) * n_fsdp + f, (te * n_seq + tx * 2 + tc) * n_fsdp + tf))
        return lax.ppermute(value, AXES, pairs)

    def other_core(value):
        return permute(value, lambda e, x, c, f: (e, x, 1 - c, f))

    def along_expert(value, k):
        return permute(value, lambda e, x, c, f: (e ^ k, x, c, f))

    def plane(value):
        return [
            permute(value, lambda e, x, c, f, dx=dx, df=df: (e, (x + dx) % n_x, c, (f + df) % n_fsdp))
            for dx in range(n_x) for df in range(n_fsdp) if dx or df
        ]

    def body(tokens, slot_params, w_in, w_out):
        count, width = tokens.shape
        slots = slot_params.shape[1]
        rows = w_in.shape[0] * SLOTS
        half = width // LANES // 2
        f32 = jnp.float32
        params = pltpu.CompilerParams(vmem_limit_bytes=24 * 1024 * 1024)
        expert = lax.axis_index("expert")
        place = jnp.stack([lax.axis_index("seq") % 2, expert]).astype(jnp.int32)

        shape = jax.ShapeDtypeStruct((n_expert, half + 2, rows, LANES), f32)
        logits, mine, theirs = pl.pallas_call(
            dispatch_kernel,
            out_shape=(jax.ShapeDtypeStruct((slots, count), f32), shape, shape),
            in_specs=[SMEM, VMEM, VMEM],
            out_specs=(VMEM, VMEM, VMEM),
            compiler_params=params,
        )(place, tokens, slot_params)
        combine = pl.pallas_call(
            combine_kernel,
            out_shape=jax.ShapeDtypeStruct((count, 3 * slots), jnp.bfloat16),
            in_specs=[VMEM],
            out_specs=VMEM,
            compiler_params=params,
        )(logits)

        chip = join([mine, other_core(theirs)], 1)
        at = lambda k: lax.dynamic_index_in_dim(chip, expert ^ k, 0, keepdims=False)
        total = join([at(0)] + [along_expert(at(k), k) for k in range(1, n_expert)], 0)
        total = join([total] + plane(total), 0)
        shape = jax.ShapeDtypeStruct((half, rows, LANES), f32)
        own, send = pl.pallas_call(
            expert_kernel,
            out_shape=(shape, shape),
            in_specs=[SMEM, VMEM, VMEM, VMEM, VMEM],
            out_specs=(VMEM, VMEM),
            compiler_params=params,
        )(place, total, other_core(total), w_in, w_out)
        own = own + other_core(send)
        own = own + sum(plane(own))
        gathered = jnp.stack([own] + [along_expert(own, k) for k in range(1, n_expert)])
        block = 256 if width % 256 == 0 else width
        return pl.pallas_call(
            mix_kernel,
            out_shape=jax.ShapeDtypeStruct((count, width), f32),
            in_specs=[SMEM, VMEM, VMEM, VMEM],
            out_specs=VMEM,
            scratch_shapes=[pltpu.VMEM((slots, width), f32)],
            compiler_params=params,
        )(place, combine, gathered, other_core(gathered))

    return jax.shard_map(
        body,
        mesh=mesh,
        in_specs=(P(AXES, None), P(), P("expert", ("seq", "fsdp"), None), P("expert", ("seq", "fsdp"), None)),
        out_specs=P(AXES, None),
        check_vma=False,
    )
```

time: 132 us -> 51.2 us (0.39)
  blocking collectives: 73.4 us -> 0 us
  starting transfers between devices: 0.04 us -> 17.9 us
  between operations: 14.8 us -> 0.1 us
  matrix products: 12.6 us -> 0 us
  other arithmetic: 9.11 us -> 2.55 us
  Pallas kernels: 0 us -> 6.41 us
  local copies, waits for them, and re-layouts: 4.56 us -> 6.42 us
    psum x1 -> x0, blocking collectives: 24.5 us -> none  [body(): outputs_own = lax.psum(partial_out, ('seq', 'fsdp'))]
    unnamed x2 -> x0, blocking collectives: 23.6 us -> none
    ppermute x0 -> x16, starting transfers between devices: none -> 17.9 us  [permute(): return lax.ppermute(value, AXES, pairs)]
    ppermute x0 -> x16, waiting for transfers between devices: none -> 17.4 us  [permute(): return lax.ppermute(value, AXES, pairs)]
    all_gather x1 -> x0, blocking collectives: 13.6 us -> none  [body(): lax.all_gather(outputs_own, 'expert', axis=0, tiled=True)]
    dot_general x5 -> x0, matrix products: 12.6 us -> none  [the longest x1 4.7 us: body(): jnp.einsum('esd,ehd->esh', slot_inputs, w_in, precision=highest)]
    pmax x1 -> x0, blocking collectives: 11.7 us -> none  [body(): overall_peak = lax.pmax(group_peak, 'expert')]
    all_gather x1 -> x0, waiting for transfers between devices: 10.2 us -> none  [combined_all(): pieces = jax.tree.map(lambda part: lax.all_gather(part, axis), value)]
  transfers between devices with their start and end apart: 2 -> 16, of which waited for: 2 -> 14; matrix products, arithmetic and copies ran while one was open for 2% -> 0% of each run, Pallas kernels for 0% -> 0%
where the time goes in v1:
time: 51.2 us; the launch traced here: 50.8 us
  starting transfers between devices  17.9 us (35%)
  waiting for transfers between devices  17.4 us (34%)
  local copies, waits for them, and re-layouts  6.42 us (13%)
  Pallas kernels  6.41 us (13%)
  other arithmetic  2.55 us (5%)
    ppermute x16, starting transfers between devices, permute(): return lax.ppermute(value, AXES, pairs)  17.9 us
    ppermute x16, waiting for transfers between devices, permute(): return lax.ppermute(value, AXES, pairs)  17.4 us
    unnamed x9, local copies, waits for them, and re-layouts  6.42 us
    pallas_call x1, Pallas kernels, body(): pl.pallas_call(expert_kernel, out_shape=(shape, shape), in_specs=[SMEM, V...  2.32 us
    pallas_call x1, Pallas kernels, body(): pl.pallas_call(dispatch_kernel, out_shape=(jax.ShapeDtypeStruct((slots, c...  2.03 us
    pallas_call x1, Pallas kernels, body(): pl.pallas_call(mix_kernel, out_shape=jax.ShapeDtypeStruct((count, width),...  1.86 us
    mul x6, other arithmetic, join(): lax.slice_in_dim(p, 0, size, axis=axis) * jnp.exp(q - top)  1.49 us
  transfers between devices with their start and end apart: 16, of which 14 were waited for; matrix products, arithmetic and copies ran while one was open for 0% of the time, Pallas kernels for 0%

profile of v1, /device:TPU:0, one launch (start us, length us, event | category | flops | bytes accessed | tf_op | source)
XLA Modules:
  0.0 50.8 jit_solution(8412281653477141537)
XLA Ops:
  0.0 2.1 %copy.5.params_ref = f32[1280,32]{1,0:T(8,128)} copy(f32[1280,32]{0,1:T(8,128)} %param.5) | data formatting | bytes 327680 | tf_op args[1]
  2.2 1.1 %copy-done.2 = f32[1280,32]{1,0:T(8,128)S(1)} copy-done((f32[1280,32]{1,0:T(8,128)S(1)}, f32[1280,32]{1,0:T(8,128)}, u32[]{:S(2)}) %copy-start.2) | copy-done | bytes 163864
  3.3 1.3 %copy-done.3 = f32[224,1280]{1,0:T(8,128)S(1)} copy-done((f32[224,1280]{1,0:T(8,128)S(1)}, f32[224,1280]{1,0:T(8,128)}, u32[]{:S(2)}) %copy-start.3) | copy-done | bytes 1146904
  4.6 2.0 %shard_map.46 = (f32[32,224]{1,0:T(8,128)S(1)}, f32[4,7,8,128]{3,2,1,0:T(8,128)S(1)}, f32[4,7,8,128]{3,2,1,0:T(8,128)S(1)}) custom-call(s32[2]{0:T(128)S(1)} %pad_add_fusion.core_ref, f32[224,1280]{1,0:T(8,128)S(1)} %copy-done.3, f32[1280,32]{1,0:T(8,128)S(1)} %copy-done.2), custom_call_target="tpu_custom_call" | custom-call | tf_op jit(solution)/shard_map/pallas_call | solution.py:175
  7.1 1.1 %collective-permute-done = f32[4,7,8,128]{3,2,1,0:T(8,128)} collective-permute-done((f32[4,7,8,128]{3,2,1,0:T(8,128)S(1)}, f32[4,7,8,128]{3,2,1,0:T(8,128)}, u32[]{:S(2)}, u32[]{:S(2)}) %collective-permute-start) | collective-permute-done | bytes 114720 | tf_op jit(solution)/shard_map/ppermute | solution.py:150
  9.7 0.9 %fusion = f32[4,6,8,128]{3,2,1,0:T(8,128)S(1)} fusion(f32[4,7,8,128]{3,2,1,0:T(8,128)} %collective-permute-done, f32[4,7,8,128]{3,2,1,0:T(8,128)S(1)} %get-tuple-element.11, f32[4,8,128]{2,1,0:T(8,128)S(1)} %exponential_bitcast_fusion, f32[4,8,128]{2,1,0:T(8,128)S(1)} %get-tuple-element.19), kind=kLoop, calls=%fused_computation.9 | loop fusion | flops 73728 | bytes 327680 | tf_op jit(solution)/shard_map/add | solution.py:135
  10.6 3.0 %collective-permute-start.1 = (f32[7,8,128]{2,1,0:T(8,128)S(1)}, f32[7,8,128]{2,1,0:T(8,128)S(1)}, u32[]{:S(2)}, u32[]{:S(2)}) collective-permute-start(f32[7,8,128]{2,1,0:T(8,128)S(1)} %get-tuple-element.21), channel_id=1, source_target_pairs={{0,8},{1,9},{2,10},{3,11},{4,12},{5,13},{6,14},{7,15},{8,0},{9,1},... | collective-permute-start | bytes 86024 | tf_op jit(solution)/shard_map/ppermute | solution.py:150
  13.6 2.6 %collective-permute-start.2 = (f32[7,8,128]{2,1,0:T(8,128)S(1)}, f32[7,8,128]{2,1,0:T(8,128)S(1)}, u32[]{:S(2)}, u32[]{:S(2)}) collective-permute-start(f32[7,8,128]{2,1,0:T(8,128)S(1)} %get-tuple-element.23), channel_id=1, source_target_pairs={{0,16},{1,17},{2,18},{3,19},{4,20},{5,21},{6,22},{7,23},{8,24},{9,... | collective-permute-start | bytes 86024 | tf_op jit(solution)/shard_map/ppermute | solution.py:150
  16.2 2.6 %collective-permute-done.2 = f32[7,8,128]{2,1,0:T(8,128)S(1)} collective-permute-done((f32[7,8,128]{2,1,0:T(8,128)S(1)}, f32[7,8,128]{2,1,0:T(8,128)S(1)}, u32[]{:S(2)}, u32[]{:S(2)}) %collective-permute-start.2) | collective-permute-done | bytes 28704 | tf_op jit(solution)/shard_map/ppermute | solution.py:150
  18.8 3.0 %collective-permute-done.3 = f32[7,8,128]{2,1,0:T(8,128)S(1)} collective-permute-done((f32[7,8,128]{2,1,0:T(8,128)S(1)}, f32[7,8,128]{2,1,0:T(8,128)S(1)}, u32[]{:S(2)}, u32[]{:S(2)}) %collective-permute-start.3) | collective-permute-done | bytes 28704 | tf_op jit(solution)/shard_map/ppermute | solution.py:150
  21.9 2.5 %collective-permute-start.6 = (f32[7,8,128]{2,1,0:T(8,128)S(1)}, f32[7,8,128]{2,1,0:T(8,128)S(1)}, u32[]{:S(2)}, u32[]{:S(2)}) collective-permute-start(f32[7,8,128]{2,1,0:T(8,128)S(1)} %pad_maximum_fusion.1), channel_id=1, source_target_pairs={{0,5},{1,4},{2,7},{3,6},{4,1},{5,0},{6,3},{7,2},{8,13},{9,12},{10,... | collective-permute-start | bytes 86024 | tf_op jit(solution)/shard_map/ppermute | solution.py:150
  25.5 1.3 %collective-permute-done.6 = f32[7,8,128]{2,1,0:T(8,128)S(1)} collective-permute-done((f32[7,8,128]{2,1,0:T(8,128)S(1)}, f32[7,8,128]{2,1,0:T(8,128)S(1)}, u32[]{:S(2)}, u32[]{:S(2)}) %collective-permute-start.6) | collective-permute-done | bytes 28704 | tf_op jit(solution)/shard_map/ppermute | solution.py:150
  26.8 1.6 %collective-permute-done.5 = f32[7,8,128]{2,1,0:T(8,128)S(1)} collective-permute-done((f32[7,8,128]{2,1,0:T(8,128)S(1)}, f32[7,8,128]{2,1,0:T(8,128)S(1)}, u32[]{:S(2)}, u32[]{:S(2)}) %collective-permute-start.5) | collective-permute-done | bytes 28704 | tf_op jit(solution)/shard_map/ppermute | solution.py:150
  29.0 1.2 %collective-permute-done.7.theirs_ref = f32[7,8,128]{2,1,0:T(8,128)S(1)} collective-permute-done((f32[7,8,128]{2,1,0:T(8,128)S(1)}, f32[7,8,128]{2,1,0:T(8,128)S(1)}, u32[]{:S(2)}, u32[]{:S(2)}) %collective-permute-start.7) | collective-permute-done | bytes 28704 | tf_op jit(solution)/shard_map/ppermute | solution.py:150
  30.2 1.9 %copy-done.1 = f32[2,320,1280]{2,1,0:T(8,128)S(1)} copy-done((f32[2,320,1280]{2,1,0:T(8,128)S(1)}, f32[2,320,1280]{2,1,0:T(8,128)}, u32[]{:S(2)}) %copy-start.1) | copy-done | bytes 3276824
  32.1 2.3 %shard_map.48 = (f32[5,8,128]{2,1,0:T(8,128)S(1)}, f32[5,8,128]{2,1,0:T(8,128)S(1)}) custom-call(s32[2]{0:T(128)S(1)} %pad_add_fusion.core_ref, f32[7,8,128]{2,1,0:T(8,128)S(1)} %pad_maximum_fusion.2.mine_ref, f32[7,8,128]{2,1,0:T(8,128)S(1)} %collective-permute-done.7.theirs_ref, f32[2,320,1280]{2,1,0:T(8,128)S(1)} %copy-done, f32[2,320,1280]{2,1,0:T(8,128)S(1)} %copy-done.1), custom_call_target="tpu_custom_call" | custom-call | tf_op jit(solution)/shard_map/pallas_call | solution.py:195
  34.6 1.0 %collective-permute-done.8 = f32[5,8,128]{2,1,0:T(8,128)S(1)} collective-permute-done((f32[5,8,128]{2,1,0:T(8,128)S(1)}, f32[5,8,128]{2,1,0:T(8,128)S(1)}, u32[]{:S(2)}, u32[]{:S(2)}) %collective-permute-start.8) | collective-permute-done | bytes 20512 | tf_op jit(solution)/shard_map/ppermute | solution.py:150
  35.6 1.4 %collective-permute-start.11 = (f32[5,8,128]{2,1,0:T(8,128)S(1)}, f32[5,8,128]{2,1,0:T(8,128)S(1)}, u32[]{:S(2)}, u32[]{:S(2)}) collective-permute-start(f32[5,8,128]{2,1,0:T(8,128)S(1)} %add.62), channel_id=1, source_target_pairs={{0,5},{1,4},{2,7},{3,6},{4,1},{5,0},{6,3},{7,2},{8,13},{9,12},{10,... | collective-permute-start | bytes 61448 | tf_op jit(solution)/shard_map/ppermute | solution.py:150
  37.6 1.5 %collective-permute-start.9 = (f32[5,8,128]{2,1,0:T(8,128)S(1)}, f32[5,8,128]{2,1,0:T(8,128)S(1)}, u32[]{:S(2)}, u32[]{:S(2)}) collective-permute-start(f32[5,8,128]{2,1,0:T(8,128)S(1)} %add.62), channel_id=1, source_target_pairs={{0,1},{1,0},{2,3},{3,2},{4,5},{5,4},{6,7},{7,6},{8,9},{9,8},{10,11... | collective-permute-start | bytes 61448 | tf_op jit(solution)/shard_map/ppermute | solution.py:150
  39.1 1.2 %collective-permute-done.11 = f32[5,8,128]{2,1,0:T(8,128)S(1)} collective-permute-done((f32[5,8,128]{2,1,0:T(8,128)S(1)}, f32[5,8,128]{2,1,0:T(8,128)S(1)}, u32[]{:S(2)}, u32[]{:S(2)}) %collective-permute-start.11) | collective-permute-done | bytes 20512 | tf_op jit(solution)/shard_map/ppermute | solution.py:150
  41.8 4.0 %collective-permute-start.12 = (f32[5,8,128]{2,1,0:T(8,128)S(1)}, f32[5,8,128]{2,1,0:T(8,128)S(1)}, u32[]{:S(2)}, u32[]{:S(2)}) collective-permute-start(f32[5,8,128]{2,1,0:T(8,128)S(1)} %add_add_fusion), channel_id=1, source_target_pairs={{0,8},{1,9},{2,10},{3,11},{4,12},{5,13},{6,14},{7,15},{8,0},{9,1},... | collective-permute-start | bytes 61448 | tf_op jit(solution)/shard_map/ppermute | solution.py:150
  45.8 1.2 %collective-permute-done.14 = f32[5,8,128]{2,1,0:T(8,128)S(1)} collective-permute-done((f32[5,8,128]{2,1,0:T(8,128)S(1)}, f32[5,8,128]{2,1,0:T(8,128)S(1)}, u32[]{:S(2)}, u32[]{:S(2)}) %collective-permute-start.14) | collective-permute-done | bytes 20512 | tf_op jit(solution)/shard_map/ppermute | solution.py:150
  47.9 1.1 %collective-permute-done.15.theirs_ref = f32[4,5,8,128]{3,2,1,0:T(8,128)S(1)} collective-permute-done((f32[4,5,8,128]{3,2,1,0:T(8,128)S(1)}, f32[4,5,8,128]{3,2,1,0:T(8,128)S(1)}, u32[]{:S(2)}, u32[]{:S(2)}) %collective-permute-start.15) | collective-permute-done | bytes 81952 | tf_op jit(solution)/shard_map/ppermute | solution.py:150
  48.9 1.9 %shard_map.49 = f32[224,1280]{1,0:T(8,128)} custom-call(s32[2]{0:T(128)S(1)} %pad_add_fusion.core_ref, bf16[224,96]{1,0:T(8,128)(2,1)S(1)} %shard_map.47.combine_ref, f32[4,5,8,128]{3,2,1,0:T(8,128)S(1)} %pad_maximum_fusion.mine_ref, f32[4,5,8,128]{3,2,1,0:T(8,128)S(1)} %collective-permute-done.15.theirs_ref), custom_call_target="tpu_custom_call" | custom-call | tf_op jit(solution)/shard_map/pallas_call | solution.py:206
  (37 shorter events, 6.8 us)
Async XLA Ops:
  0.0 30.2 %copy-start = (f32[2,320,1280]{2,1,0:T(8,128)S(1)}, f32[2,320,1280]{2,1,0:T(8,128)}, u32[]{:S(2)}) copy-start(f32[2,320,1280]{2,1,0:T(8,128)} %w_in_ref.1) | copy-start | bytes 9830404
  2.2 1.1 %copy-start.2 = (f32[1280,32]{1,0:T(8,128)S(1)}, f32[1280,32]{1,0:T(8,128)}, u32[]{:S(2)}) copy-start(f32[1280,32]{1,0:T(8,128)} %copy.5.params_ref) | copy-start | bytes 491524
  3.3 1.3 %copy-start.3 = (f32[224,1280]{1,0:T(8,128)S(1)}, f32[224,1280]{1,0:T(8,128)}, u32[]{:S(2)}) copy-start(f32[224,1280]{1,0:T(8,128)} %tokens_ref.1) | copy-start | bytes 3440644
  6.6 1.6 %collective-permute-start = (f32[4,7,8,128]{3,2,1,0:T(8,128)S(1)}, f32[4,7,8,128]{3,2,1,0:T(8,128)}, u32[]{:S(2)}, u32[]{:S(2)}) collective-permute-start(f32[4,7,8,128]{3,2,1,0:T(8,128)S(1)} %get-tuple-element.12), channel_id=1, source_target_pairs={{0,2},{1,3},{2,0},{3,1},{4,6},{5,7},{6,4},{7,5},{8,10},{9,11},{10,... | collective-permute-start | bytes 344072 | tf_op jit(solution)/shard_map/ppermute | solution.py:150
  10.6 5.6 %collective-permute-start.1 = (f32[7,8,128]{2,1,0:T(8,128)S(1)}, f32[7,8,128]{2,1,0:T(8,128)S(1)}, u32[]{:S(2)}, u32[]{:S(2)}) collective-permute-start(f32[7,8,128]{2,1,0:T(8,128)S(1)} %get-tuple-element.21), channel_id=1, source_target_pairs={{0,8},{1,9},{2,10},{3,11},{4,12},{5,13},{6,14},{7,15},{8,0},{9,1},... | collective-permute-start | bytes 86024 | tf_op jit(solution)/shard_map/ppermute | solution.py:150
  13.6 5.2 %collective-permute-start.2 = (f32[7,8,128]{2,1,0:T(8,128)S(1)}, f32[7,8,128]{2,1,0:T(8,128)S(1)}, u32[]{:S(2)}, u32[]{:S(2)}) collective-permute-start(f32[7,8,128]{2,1,0:T(8,128)S(1)} %get-tuple-element.23), channel_id=1, source_target_pairs={{0,16},{1,17},{2,18},{3,19},{4,20},{5,21},{6,22},{7,23},{8,24},{9,... | collective-permute-start | bytes 86024 | tf_op jit(solution)/shard_map/ppermute | solution.py:150
  16.2 5.7 %collective-permute-start.3 = (f32[7,8,128]{2,1,0:T(8,128)S(1)}, f32[7,8,128]{2,1,0:T(8,128)S(1)}, u32[]{:S(2)}, u32[]{:S(2)}) collective-permute-start(f32[7,8,128]{2,1,0:T(8,128)S(1)} %get-tuple-element.24), channel_id=1, source_target_pairs={{0,24},{1,25},{2,26},{3,27},{4,28},{5,29},{6,30},{7,31},{8,16},{9,... | collective-permute-start | bytes 86024 | tf_op jit(solution)/shard_map/ppermute | solution.py:150
  21.9 4.8 %collective-permute-start.6 = (f32[7,8,128]{2,1,0:T(8,128)S(1)}, f32[7,8,128]{2,1,0:T(8,128)S(1)}, u32[]{:S(2)}, u32[]{:S(2)}) collective-permute-start(f32[7,8,128]{2,1,0:T(8,128)S(1)} %pad_maximum_fusion.1), channel_id=1, source_target_pairs={{0,5},{1,4},{2,7},{3,6},{4,1},{5,0},{6,3},{7,2},{8,13},{9,12},{10,... | collective-permute-start | bytes 86024 | tf_op jit(solution)/shard_map/ppermute | solution.py:150
  24.4 3.9 %collective-permute-start.5 = (f32[7,8,128]{2,1,0:T(8,128)S(1)}, f32[7,8,128]{2,1,0:T(8,128)S(1)}, u32[]{:S(2)}, u32[]{:S(2)}) collective-permute-start(f32[7,8,128]{2,1,0:T(8,128)S(1)} %pad_maximum_fusion.1), channel_id=1, source_target_pairs={{0,4},{1,5},{2,6},{3,7},{4,0},{5,1},{6,2},{7,3},{8,12},{9,13},{10,... | collective-permute-start | bytes 86024 | tf_op jit(solution)/shard_map/ppermute | solution.py:150
  25.0 3.9 %collective-permute-start.4 = (f32[7,8,128]{2,1,0:T(8,128)S(1)}, f32[7,8,128]{2,1,0:T(8,128)S(1)}, u32[]{:S(2)}, u32[]{:S(2)}) collective-permute-start(f32[7,8,128]{2,1,0:T(8,128)S(1)} %pad_maximum_fusion.1), channel_id=1, source_target_pairs={{0,1},{1,0},{2,3},{3,2},{4,5},{5,4},{6,7},{7,6},{8,9},{9,8},{10,11... | collective-permute-start | bytes 86024 | tf_op jit(solution)/shard_map/ppermute | solution.py:150
  28.9 1.3 %collective-permute-start.7 = (f32[7,8,128]{2,1,0:T(8,128)S(1)}, f32[7,8,128]{2,1,0:T(8,128)S(1)}, u32[]{:S(2)}, u32[]{:S(2)}) collective-permute-start(f32[7,8,128]{2,1,0:T(8,128)S(1)} %pad_maximum_fusion.2.mine_ref), channel_id=1, source_target_pairs={{0,2},{1,3},{2,0},{3,1},{4,6},{5,7},{6,4},{7,5},{8,10},{9,11},{10,... | collective-permute-start | bytes 86024 | tf_op jit(solution)/shard_map/ppermute | solution.py:150
  30.2 1.9 %copy-start.1 = (f32[2,320,1280]{2,1,0:T(8,128)S(1)}, f32[2,320,1280]{2,1,0:T(8,128)}, u32[]{:S(2)}) copy-start(f32[2,320,1280]{2,1,0:T(8,128)} %w_out_ref.1) | copy-start | bytes 9830404
  34.4 1.2 %collective-permute-start.8 = (f32[5,8,128]{2,1,0:T(8,128)S(1)}, f32[5,8,128]{2,1,0:T(8,128)S(1)}, u32[]{:S(2)}, u32[]{:S(2)}) collective-permute-start(f32[5,8,128]{2,1,0:T(8,128)S(1)} %get-tuple-element.14), channel_id=1, source_target_pairs={{0,2},{1,3},{2,0},{3,1},{4,6},{5,7},{6,4},{7,5},{8,10},{9,11},{10,... | collective-permute-start | bytes 61448 | tf_op jit(solution)/shard_map/ppermute | solution.py:150
  35.6 4.7 %collective-permute-start.11 = (f32[5,8,128]{2,1,0:T(8,128)S(1)}, f32[5,8,128]{2,1,0:T(8,128)S(1)}, u32[]{:S(2)}, u32[]{:S(2)}) collective-permute-start(f32[5,8,128]{2,1,0:T(8,128)S(1)} %add.62), channel_id=1, source_target_pairs={{0,5},{1,4},{2,7},{3,6},{4,1},{5,0},{6,3},{7,2},{8,13},{9,12},{10,... | collective-permute-start | bytes 61448 | tf_op jit(solution)/shard_map/ppermute | solution.py:150
  37.1 3.8 %collective-permute-start.10 = (f32[5,8,128]{2,1,0:T(8,128)S(1)}, f32[5,8,128]{2,1,0:T(8,128)S(1)}, u32[]{:S(2)}, u32[]{:S(2)}) collective-permute-start(f32[5,8,128]{2,1,0:T(8,128)S(1)} %add.62), channel_id=1, source_target_pairs={{0,4},{1,5},{2,6},{3,7},{4,0},{5,1},{6,2},{7,3},{8,12},{9,13},{10,... | collective-permute-start | bytes 61448 | tf_op jit(solution)/shard_map/ppermute | solution.py:150
  37.6 3.8 %collective-permute-start.9 = (f32[5,8,128]{2,1,0:T(8,128)S(1)}, f32[5,8,128]{2,1,0:T(8,128)S(1)}, u32[]{:S(2)}, u32[]{:S(2)}) collective-permute-start(f32[5,8,128]{2,1,0:T(8,128)S(1)} %add.62), channel_id=1, source_target_pairs={{0,1},{1,0},{2,3},{3,2},{4,5},{5,4},{6,7},{7,6},{8,9},{9,8},{10,11... | collective-permute-start | bytes 61448 | tf_op jit(solution)/shard_map/ppermute | solution.py:150
  41.4 5.6 %collective-permute-start.14 = (f32[5,8,128]{2,1,0:T(8,128)S(1)}, f32[5,8,128]{2,1,0:T(8,128)S(1)}, u32[]{:S(2)}, u32[]{:S(2)}) collective-permute-start(f32[5,8,128]{2,1,0:T(8,128)S(1)} %add_add_fusion), channel_id=1, source_target_pairs={{0,24},{1,25},{2,26},{3,27},{4,28},{5,29},{6,30},{7,31},{8,16},{9,... | collective-permute-start | bytes 61448 | tf_op jit(solution)/shard_map/ppermute | solution.py:150
  41.8 5.2 %collective-permute-start.13 = (f32[5,8,128]{2,1,0:T(8,128)S(1)}, f32[5,8,128]{2,1,0:T(8,128)S(1)}, u32[]{:S(2)}, u32[]{:S(2)}) collective-permute-start(f32[5,8,128]{2,1,0:T(8,128)S(1)} %add_add_fusion), channel_id=1, source_target_pairs={{0,16},{1,17},{2,18},{3,19},{4,20},{5,21},{6,22},{7,23},{8,24},{9,... | collective-permute-start | bytes 61448 | tf_op jit(solution)/shard_map/ppermute | solution.py:150
  41.8 5.8 %collective-permute-start.12 = (f32[5,8,128]{2,1,0:T(8,128)S(1)}, f32[5,8,128]{2,1,0:T(8,128)S(1)}, u32[]{:S(2)}, u32[]{:S(2)}) collective-permute-start(f32[5,8,128]{2,1,0:T(8,128)S(1)} %add_add_fusion), channel_id=1, source_target_pairs={{0,8},{1,9},{2,10},{3,11},{4,12},{5,13},{6,14},{7,15},{8,0},{9,1},... | collective-permute-start | bytes 61448 | tf_op jit(solution)/shard_map/ppermute | solution.py:150
  47.6 1.3 %collective-permute-start.15 = (f32[4,5,8,128]{3,2,1,0:T(8,128)S(1)}, f32[4,5,8,128]{3,2,1,0:T(8,128)S(1)}, u32[]{:S(2)}, u32[]{:S(2)}) collective-permute-start(f32[4,5,8,128]{3,2,1,0:T(8,128)S(1)} %pad_maximum_fusion.mine_ref), channel_id=1, source_target_pairs={{0,2},{1,3},{2,0},{3,1},{4,6},{5,7},{6,4},{7,5},{8,10},{9,11},{10,... | collective-permute-start | bytes 245768 | tf_op jit(solution)/shard_map/ppermute | solution.py:150

commit v2 on v1

v2 whole, which is shorter than its diff:
```python
import functools

import jax
import jax.numpy as jnp
from jax import lax
from jax.experimental import pallas as pl
from jax.experimental.pallas import tpu as pltpu
from jax.sharding import PartitionSpec as P

SLOTS = 4
LANES = 128
AXES = ("expert", "seq", "fsdp")
VMEM = pl.BlockSpec(memory_space=pltpu.VMEM)
SMEM = pl.BlockSpec(memory_space=pltpu.SMEM)
HBM = pl.BlockSpec(memory_space=pltpu.HBM)


def pieces(value, count):
    out = []
    for _ in range(count):
        part = value.astype(jnp.bfloat16)
        out.append(part)
        value = value - part.astype(jnp.float32)
    return out


def stacked(value):
    high, low = pieces(value, 2)
    return jnp.concatenate([high.astype(jnp.float32), low.astype(jnp.float32)], axis=0).astype(jnp.bfloat16)


def mm(left, right, contract=((1,), (0,))):
    return lax.dot_general(left, right, (contract, ((), ())), preferred_element_type=jnp.float32)


def pick(core, when_zero, when_one):
    return jnp.where(core == 0, when_zero, when_one)


def join(parts):
    top = functools.reduce(jnp.maximum, [p[-1] for p in parts])
    total = sum(p[:-1] * jnp.exp(p[-1] - top)[None] for p in parts)
    return jnp.concatenate([total, top[None]], axis=0)


def dispatch_kernel(chunks, place_ref, tokens_hbm, params_hbm, w_in_hbm, w_out_hbm,
                    logits_ref, mine_ref, theirs_ref, w_in_ref, w_out_ref,
                    tokens_ref, params_ref, sums_ref, sems):
    core, expert = place_ref[0], place_ref[1]
    groups, tiles, rows, _ = mine_ref.shape
    half = tiles - 2
    slots, _ = params_hbm.shape
    count = tokens_hbm.shape[0] // chunks
    params_copy = pltpu.make_async_copy(params_hbm, params_ref, sems.at[chunks])
    params_copy.start()
    copies = []
    for i in range(chunks):
        own = pl.ds(i * count, count)
        copies.append(pltpu.make_async_copy(tokens_hbm.at[own], tokens_ref.at[own], sems.at[i]))
        copies[i].start()
    weight_copies = [
        pltpu.make_async_copy(w_in_hbm, w_in_ref, sems.at[chunks + 1]),
        pltpu.make_async_copy(w_out_hbm, w_out_ref, sems.at[chunks + 2]),
    ]
    for copy in weight_copies:
        copy.start()
    params_copy.wait()
    params = jnp.concatenate(pieces(params_ref[...], 3), axis=0)
    highs, lows, logits = [], [], []
    for i in range(chunks):
        copies[i].wait()
        parts = pieces(tokens_ref[i * count:(i + 1) * count], 3)
        highs.append(parts[0])
        lows.append(parts[1])
        products = mm(jnp.concatenate(parts, axis=0), params, ((1,), (1,)))

        def term(i, j):
            return products[i * count:(i + 1) * count, j * slots:(j + 1) * slots]

        small = term(0, 2) + term(1, 1) + term(2, 0)
        logits.append((small + (term(0, 1) + term(1, 0))) + term(0, 0))
    logits = jnp.concatenate(logits, axis=0).T
    logits_ref[...] = logits
    peak = jnp.max(logits, axis=1, keepdims=True)
    weights = jnp.exp(logits - peak)
    mass = jnp.sum(weights, axis=1, keepdims=True)
    weight_high, weight_low = pieces(weights, 2)
    high = mm(jnp.concatenate([weight_high, weight_low], axis=0), jnp.concatenate(highs, axis=0))
    low = mm(weight_high, jnp.concatenate(lows, axis=0))
    width = high.shape[1]
    sums_ref[:, :width] = high[:slots] + (high[slots:] + low)
    sums_ref[:, width:width + LANES] = jnp.broadcast_to(mass, (slots, LANES))
    sums_ref[:, width + LANES:] = jnp.broadcast_to(peak, (slots, LANES))
    for k in range(groups):
        own = pl.ds(pl.multiple_of((expert ^ k) * rows, rows), rows)
        first, second = (mine_ref, theirs_ref) if k else (theirs_ref, mine_ref)
        for t in range(half):
            one = sums_ref[own, t * LANES:(t + 1) * LANES]
            two = sums_ref[own, (t + half) * LANES:(t + half + 1) * LANES]
            first[k, t] = pick(core, one, two)
            second[k, t] = pick(core, two, one)
        for t in range(2):
            value = sums_ref[own, width + t * LANES:width + (t + 1) * LANES]
            mine_ref[k, half + t] = value
            theirs_ref[k, half + t] = value
    for copy in weight_copies:
        copy.wait()


def chip_kernel(mine_ref, theirs_ref, *outs):
    for k, out_ref in enumerate(outs):
        out_ref[...] = join([mine_ref[k], theirs_ref[k]])


def combine_kernel(logits_ref, out_ref):
    logits = logits_ref[...]
    top = jnp.max(logits, axis=0, keepdims=True)
    powers = jnp.exp(logits - top)
    combine = (powers / jnp.sum(powers, axis=0, keepdims=True)).T
    high, low = pieces(combine, 2)
    out_ref[...] = jnp.concatenate([high, low, high], axis=1)


def expert_kernel(place_ref, sent_ref, got_ref, w_in_ref, w_out_ref, out_ref):
    core = place_ref[0]
    tiles, rows, _ = out_ref.shape
    half = tiles // 2
    experts, units, width = w_in_ref.shape
    near = join([sent_ref[0], got_ref[1]])
    far = join([sent_ref[1], got_ref[0]])
    near = [near[t] / near[half] for t in range(half)]
    far = [far[t] / far[half] for t in range(half)]
    first = [pick(core, a, b) for a, b in zip(near, far)]
    second = [pick(core, b, a) for a, b in zip(near, far)]
    inputs = stacked(jnp.concatenate(first + second, axis=1))
    w_high, w_low = pieces(w_in_ref[...].reshape(experts * units, width), 2)
    nt = ((1,), (1,))
    large = mm(w_high, inputs, nt).T
    small = mm(w_low, inputs, nt).T
    value = large[:rows] + (large[rows:] + small[:rows])
    value = value * (1.0 + lax.erf(value * (0.5 ** 0.5))) * 0.5
    slot = lax.broadcasted_iota(jnp.int32, value.shape, 0)
    unit = lax.broadcasted_iota(jnp.int32, value.shape, 1)
    keep = None
    for e in range(experts):
        inside = (slot // SLOTS == e) & (unit >= e * units) & (unit < (e + 1) * units)
        keep = inside if keep is None else keep | inside
    hidden = stacked(jnp.where(keep, value, 0.0))
    w_high, w_low = pieces(w_out_ref[...].reshape(experts * units, width), 2)
    large = mm(hidden, w_high)
    small = mm(hidden, w_low)
    out = large[:rows] + (large[rows:] + small[:rows])
    for t in range(tiles):
        out_ref[t] = out[:, t * LANES:(t + 1) * LANES]


def mix_kernel(near, place_ref, combine_ref, own_ref, others_ref, *refs):
    out_hbm, slots_ref, out_ref, sems = refs[-4:]
    core, expert = place_ref[0], place_ref[1]
    half, rows, _ = own_ref.shape
    groups = others_ref.shape[0] + 1
    for k in range(groups):
        place = pl.ds(pl.multiple_of((expert ^ k) * rows, rows), rows)
        for t in range(half):
            slots_ref[place, t * LANES:(t + 1) * LANES] = others_ref[k - 1, t] if k else own_ref[t]
    high, low = pieces(slots_ref[...], 2)
    out_ref[...] = mm(combine_ref[...], jnp.concatenate([high, high, low], axis=0))
    side = core if near else 1 - core
    columns = pl.ds(pl.multiple_of(side * (half * LANES), LANES), half * LANES)
    copy = pltpu.make_async_copy(out_ref, out_hbm.at[:, columns], sems)
    copy.start()
    copy.wait()


def solution(mesh):
    n_expert, n_seq, n_fsdp = (mesh.shape[a] for a in AXES)
    n_x = n_seq // 2

    def permute(value, target):
        pairs = []
        for e in range(n_expert):
            for s in range(n_seq):
                for f in range(n_fsdp):
                    te, tx, tc, tf = target(e, s // 2, s % 2, f)
                    pairs.append(((e * n_seq + s) * n_fsdp + f, (te * n_seq + tx * 2 + tc) * n_fsdp + tf))
        return lax.ppermute(value, AXES, pairs)

    def other_core(value):
        return permute(value, lambda e, x, c, f: (e, x, 1 - c, f))

    def along_expert(value, k):
        return permute(value, lambda e, x, c, f: (e ^ k, x, 1 - c, f))

    def plane(value):
        return [
            permute(value, lambda e, x, c, f, dx=dx, df=df: (e, (x + dx) % n_x, 1 - c, (f + df) % n_fsdp))
            for dx in range(n_x) for df in range(n_fsdp) if dx or df
        ]

    def body(tokens, slot_params, w_in, w_out):
        count, width = tokens.shape
        slots = slot_params.shape[1]
        rows = w_in.shape[0] * SLOTS
        half = width // LANES // 2
        f32 = jnp.float32
        params = pltpu.CompilerParams(vmem_limit_bytes=24 * 1024 * 1024)
        core = lax.axis_index("seq") % 2
        place = jnp.stack([core, lax.axis_index("expert")]).astype(jnp.int32)
        chunks = 2 if count % 32 == 0 else 1

        in_hbm = lambda value: pltpu.with_memory_space_constraint(value, pltpu.HBM)
        shape = pltpu.VMEM((n_expert, half + 2, rows, LANES), f32)
        logits, mine, theirs, w_in, w_out = pl.pallas_call(
            functools.partial(dispatch_kernel, chunks),
            out_shape=(pltpu.VMEM((slots, count), f32), shape, shape, pltpu.VMEM(w_in.shape, f32), pltpu.VMEM(w_out.shape, f32)),
            in_specs=[SMEM, HBM, HBM, HBM, HBM],
            out_specs=(VMEM,) * 5,
            scratch_shapes=[
                pltpu.VMEM((count, width), f32),
                pltpu.VMEM((slots, width), f32),
                pltpu.VMEM((slots, width + 2 * LANES), f32),
                pltpu.SemaphoreType.DMA((chunks + 3,)),
            ],
            compiler_params=params,
        )(place, in_hbm(tokens), in_hbm(slot_params.T), in_hbm(w_in), in_hbm(w_out))
        combine = pl.pallas_call(
            combine_kernel,
            out_shape=jax.ShapeDtypeStruct((count, 3 * slots), jnp.bfloat16),
            in_specs=[VMEM],
            out_specs=VMEM,
            compiler_params=params,
        )(logits)

        chip = pl.pallas_call(
            chip_kernel,
            out_shape=(pltpu.VMEM((half + 2, rows, LANES), f32),) * n_expert,
            in_specs=[VMEM, VMEM],
            out_specs=(VMEM,) * n_expert,
            compiler_params=params,
        )(mine, other_core(theirs))
        total = join([chip[0]] + [along_expert(chip[k], k) for k in range(1, n_expert)])
        sent = jnp.stack([join(plane(total)), total])
        partial = pl.pallas_call(
            expert_kernel,
            out_shape=jax.ShapeDtypeStruct((2 * half, rows, LANES), f32),
            in_specs=[SMEM, VMEM, VMEM, VMEM, VMEM],
            out_specs=VMEM,
            compiler_params=params,
        )(place, sent, other_core(sent), w_in, w_out)
        partial = partial + other_core(partial)
        first, second = partial[:half], partial[half:]
        own = pick(core, second, first) + sum(plane(pick(core, first, second)))
        others = jnp.stack([along_expert(own, k) for k in range(1, n_expert)])

        def mix(near, own, others, *out):
            return pl.pallas_call(
                functools.partial(mix_kernel, near),
                out_shape=jax.ShapeDtypeStruct((count, width), f32),
                in_specs=[SMEM, VMEM, VMEM, VMEM] + [HBM] * len(out),
                out_specs=HBM,
                scratch_shapes=[
                    pltpu.VMEM((slots, half * LANES), f32),
                    pltpu.VMEM((count, half * LANES), f32),
                    pltpu.SemaphoreType.DMA,
                ],
                input_output_aliases={4: 0} if out else {},
                compiler_params=params,
            )(place, combine, own, others, *out)

        mixed = mix(True, other_core(own), others)
        return mix(False, own, other_core(others), mixed)

    return jax.shard_map(
        body,
        mesh=mesh,
        in_specs=(P(AXES, None), P(), P("expert", ("seq", "fsdp"), None), P("expert", ("seq", "fsdp"), None)),
        out_specs=P(AXES, None),
        check_vma=False,
    )
```

time: 51.2 us -> 43.9 us (0.86)
  local copies, waits for them, and re-layouts: 6.42 us -> 0 us
  Pallas kernels: 6.41 us -> 9.56 us
  other arithmetic: 2.55 us -> 0.18 us
  starting transfers between devices: 17.9 us -> 16.7 us
    unnamed x9 -> x0, local copies, waits for them, and re-layouts: 6.42 us -> none
    pallas_call x3 -> x5, Pallas kernels: 6.21 us -> 9.36 us  [the longest x1 3.94 us: body(): pl.pallas_call(functools.partial(dispatch_kernel, chunks), out_shape=(plt...]
    mul x6 -> x4, other arithmetic: 1.49 us -> 0.03 us  [join(): total = sum((p[:-1] * jnp.exp(p[-1] - top)[None] for p in parts))]
    ppermute x16 -> x17, starting transfers between devices: 17.9 us -> 16.7 us  [permute(): return lax.ppermute(value, AXES, pairs)]
    add x5 -> x4, other arithmetic: 0.96 us -> 0.05 us  [the longest x2 0.03 us: join(): total = sum((p[:-1] * jnp.exp(p[-1] - top)[None] for p in parts))]
    ppermute x16 -> x17, waiting for transfers between devices: 17.4 us -> 17.2 us  [permute(): return lax.ppermute(value, AXES, pairs)]
  transfers between devices with their start and end apart: 16 -> 17, of which waited for: 14 -> 14; matrix products, arithmetic and copies ran while one was open for 0% -> 0% of each run, Pallas kernels for 0% -> 4%
where the time goes in v2:
time: 43.9 us; the launch traced here: 43.8 us
  waiting for transfers between devices  17.2 us (39%)
  starting transfers between devices  16.7 us (38%)
  Pallas kernels  9.56 us (22%)
    ppermute x17, waiting for transfers between devices, permute(): return lax.ppermute(value, AXES, pairs)  17.2 us
    ppermute x17, starting transfers between devices, permute(): return lax.ppermute(value, AXES, pairs)  16.7 us
    pallas_call x1, Pallas kernels, body(): pl.pallas_call(functools.partial(dispatch_kernel, chunks), out_shape=(plt...  3.94 us
    pallas_call x2, Pallas kernels, mix(): pl.pallas_call(functools.partial(mix_kernel, near), out_shape=jax.ShapeDt...  3.19 us
    pallas_call x1, Pallas kernels, body(): pl.pallas_call(expert_kernel, out_shape=jax.ShapeDtypeStruct((2 * half, r...  2.21 us
  transfers between devices with their start and end apart: 17, of which 14 were waited for; matrix products, arithmetic and copies ran while one was open for 0% of the time, Pallas kernels for 4%

profile of v2, /device:TPU:0, one launch (start us, length us, event | category | flops | bytes accessed | tf_op | source)
XLA Modules:
  0.0 43.8 jit_solution(1929850264033119132)
XLA Ops:
  0.1 3.9 %shard_map.46 = (f32[32,224]{1,0:T(8,128)S(1)}, f32[4,7,8,128]{3,2,1,0:T(8,128)S(1)}, f32[4,7,8,128]{3,2,1,0:T(8,128)S(1)}, f32[2,320,1280]{2,1,0:T(8,128)S(1)}, f32[2,320,1280]{2,1,0:T(8,128)S(1)}) custom-call(s32[2]{0:T(128)S(1)} %pad_add_fusion.place_ref, f32[224,1280]{1,0:T(8,128)} %tokens_hbm.1, f32[32,1280]{1,0:T(8,128)} %bitcast.24, ...), custom_call_target="tpu_custom_call" | custom-call | tf_op jit(solution)/shard_map/pallas_call | solution.py:213
  4.0 0.5 %collective-permute-start = (f32[4,7,8,128]{3,2,1,0:T(8,128)S(1)}, f32[4,7,8,128]{3,2,1,0:T(8,128)S(1)}, u32[]{:S(2)}, u32[]{:S(2)}) collective-permute-start(f32[4,7,8,128]{3,2,1,0:T(8,128)S(1)} %get-tuple-element.16), channel_id=1, source_target_pairs={{0,2},{1,3},{2,0},{3,1},{4,6},{5,7},{6,4},{7,5},{8,10},{9,11},{10,... | collective-permute-start | bytes 344072 | tf_op jit(solution)/shard_map/ppermute | solution.py:186
  4.5 1.0 %collective-permute-done.theirs_ref = f32[4,7,8,128]{3,2,1,0:T(8,128)S(1)} collective-permute-done((f32[4,7,8,128]{3,2,1,0:T(8,128)S(1)}, f32[4,7,8,128]{3,2,1,0:T(8,128)S(1)}, u32[]{:S(2)}, u32[]{:S(2)}) %collective-permute-start) | collective-permute-done | bytes 114720 | tf_op jit(solution)/shard_map/ppermute | solution.py:186
  5.5 2.8 %collective-permute-start.1 = (f32[7,8,128]{2,1,0:T(8,128)S(1)}, f32[7,8,128]{2,1,0:T(8,128)S(1)}, u32[]{:S(2)}, u32[]{:S(2)}) collective-permute-start(f32[7,8,128]{2,1,0:T(8,128)S(1)} %get-tuple-element.18), channel_id=1, source_target_pairs={{0,10},{1,11},{2,8},{3,9},{4,14},{5,15},{6,12},{7,13},{8,2},{9,3},... | collective-permute-start | bytes 86024 | tf_op jit(solution)/shard_map/ppermute | solution.py:186
  8.3 2.6 %collective-permute-start.2 = (f32[7,8,128]{2,1,0:T(8,128)S(1)}, f32[7,8,128]{2,1,0:T(8,128)S(1)}, u32[]{:S(2)}, u32[]{:S(2)}) collective-permute-start(f32[7,8,128]{2,1,0:T(8,128)S(1)} %get-tuple-element.19), channel_id=1, source_target_pairs={{0,18},{1,19},{2,16},{3,17},{4,22},{5,23},{6,20},{7,21},{8,26},{9,... | collective-permute-start | bytes 86024 | tf_op jit(solution)/shard_map/ppermute | solution.py:186
  10.9 1.9 %collective-permute-done.2 = f32[7,8,128]{2,1,0:T(8,128)S(1)} collective-permute-done((f32[7,8,128]{2,1,0:T(8,128)S(1)}, f32[7,8,128]{2,1,0:T(8,128)S(1)}, u32[]{:S(2)}, u32[]{:S(2)}) %collective-permute-start.2) | collective-permute-done | bytes 28704 | tf_op jit(solution)/shard_map/ppermute | solution.py:186
  12.8 3.2 %collective-permute-done.3 = f32[7,8,128]{2,1,0:T(8,128)S(1)} collective-permute-done((f32[7,8,128]{2,1,0:T(8,128)S(1)}, f32[7,8,128]{2,1,0:T(8,128)S(1)}, u32[]{:S(2)}, u32[]{:S(2)}) %collective-permute-start.3) | collective-permute-done | bytes 28704 | tf_op jit(solution)/shard_map/ppermute | solution.py:186
  16.0 1.4 %collective-permute-start.4 = (f32[7,8,128]{2,1,0:T(8,128)S(1)}, f32[7,8,128]{2,1,0:T(8,128)S(1)}, u32[]{:S(2)}, u32[]{:S(2)}) collective-permute-start(f32[7,8,128]{2,1,0:T(8,128)S(1)} %get-tuple-element.27), channel_id=1, source_target_pairs={{0,3},{1,2},{2,1},{3,0},{4,7},{5,6},{6,5},{7,4},{8,11},{9,10},{10,... | collective-permute-start | bytes 86024 | tf_op jit(solution)/shard_map/ppermute | solution.py:186
  17.3 1.4 %collective-permute-start.5 = (f32[7,8,128]{2,1,0:T(8,128)S(1)}, f32[7,8,128]{2,1,0:T(8,128)S(1)}, u32[]{:S(2)}, u32[]{:S(2)}) collective-permute-start(f32[7,8,128]{2,1,0:T(8,128)S(1)} %get-tuple-element.27), channel_id=1, source_target_pairs={{0,6},{1,7},{2,4},{3,5},{4,2},{5,3},{6,0},{7,1},{8,14},{9,15},{10,... | collective-permute-start | bytes 86024 | tf_op jit(solution)/shard_map/ppermute | solution.py:186
  19.4 1.3 %collective-permute-done.5 = f32[7,8,128]{2,1,0:T(8,128)S(1)} collective-permute-done((f32[7,8,128]{2,1,0:T(8,128)S(1)}, f32[7,8,128]{2,1,0:T(8,128)S(1)}, u32[]{:S(2)}, u32[]{:S(2)}) %collective-permute-start.5) | collective-permute-done | bytes 28704 | tf_op jit(solution)/shard_map/ppermute | solution.py:186
  20.6 2.3 %collective-permute-done.6 = f32[7,8,128]{2,1,0:T(8,128)S(1)} collective-permute-done((f32[7,8,128]{2,1,0:T(8,128)S(1)}, f32[7,8,128]{2,1,0:T(8,128)S(1)}, u32[]{:S(2)}, u32[]{:S(2)}) %collective-permute-start.6) | collective-permute-done | bytes 28704 | tf_op jit(solution)/shard_map/ppermute | solution.py:186
  23.3 1.1 %collective-permute-done.7.got_ref = f32[2,7,8,128]{3,2,1,0:T(8,128)S(1)} collective-permute-done((f32[2,7,8,128]{3,2,1,0:T(8,128)S(1)}, f32[2,7,8,128]{3,2,1,0:T(8,128)S(1)}, u32[]{:S(2)}, u32[]{:S(2)}) %collective-permute-start.7) | collective-permute-done | bytes 57376 | tf_op jit(solution)/shard_map/ppermute | solution.py:186
  24.4 2.2 %shard_map.49 = f32[10,8,128]{2,1,0:T(8,128)S(1)} custom-call(s32[2]{0:T(128)S(1)} %pad_add_fusion.place_ref, f32[2,7,8,128]{3,2,1,0:T(8,128)S(1)} %pad_maximum_fusion.1.sent_ref, f32[2,7,8,128]{3,2,1,0:T(8,128)S(1)} %collective-permute-done.7.got_ref, f32[2,320,1280]{2,1,0:T(8,128)S(1)} %get-tuple-element.21.w_in_ref, ...), custom_call_target="tpu_custom_call" | custom-call | tf_op jit(solution)/shard_map/pallas_call | solution.py:243
  26.7 1.1 %collective-permute-done.8 = f32[10,8,128]{2,1,0:T(8,128)S(1)} collective-permute-done((f32[10,8,128]{2,1,0:T(8,128)S(1)}, f32[10,8,128]{2,1,0:T(8,128)S(1)}, u32[]{:S(2)}, u32[]{:S(2)}) %collective-permute-start.8) | collective-permute-done | bytes 40992 | tf_op jit(solution)/shard_map/ppermute | solution.py:186
  28.2 1.4 %collective-permute-start.11 = (f32[5,8,128]{2,1,0:T(8,128)S(1)}, f32[5,8,128]{2,1,0:T(8,128)S(1)}, u32[]{:S(2)}, u32[]{:S(2)}) collective-permute-start(f32[5,8,128]{2,1,0:T(8,128)S(1)} %slice_select_fusion), channel_id=1, source_target_pairs={{0,7},{1,6},{2,5},{3,4},{4,3},{5,2},{6,1},{7,0},{8,15},{9,14},{10,... | collective-permute-start | bytes 61448 | tf_op jit(solution)/shard_map/ppermute | solution.py:186
  29.6 1.3 %collective-permute-start.9 = (f32[5,8,128]{2,1,0:T(8,128)S(1)}, f32[5,8,128]{2,1,0:T(8,128)S(1)}, u32[]{:S(2)}, u32[]{:S(2)}) collective-permute-start(f32[5,8,128]{2,1,0:T(8,128)S(1)} %slice_select_fusion), channel_id=1, source_target_pairs={{0,3},{1,2},{2,1},{3,0},{4,7},{5,6},{6,5},{7,4},{8,11},{9,10},{10,... | collective-permute-start | bytes 61448 | tf_op jit(solution)/shard_map/ppermute | solution.py:186
  31.1 1.2 %collective-permute-done.11 = f32[5,8,128]{2,1,0:T(8,128)S(1)} collective-permute-done((f32[5,8,128]{2,1,0:T(8,128)S(1)}, f32[5,8,128]{2,1,0:T(8,128)S(1)}, u32[]{:S(2)}, u32[]{:S(2)}) %collective-permute-start.11) | collective-permute-done | bytes 20512 | tf_op jit(solution)/shard_map/ppermute | solution.py:186
  32.3 0.8 %collective-permute-done.9 = f32[5,8,128]{2,1,0:T(8,128)S(1)} collective-permute-done((f32[5,8,128]{2,1,0:T(8,128)S(1)}, f32[5,8,128]{2,1,0:T(8,128)S(1)}, u32[]{:S(2)}, u32[]{:S(2)}) %collective-permute-start.9) | collective-permute-done | bytes 20512 | tf_op jit(solution)/shard_map/ppermute | solution.py:186
  33.2 0.8 %collective-permute-start.13 = (f32[5,8,128]{2,1,0:T(8,128)S(1)}, f32[5,8,128]{2,1,0:T(8,128)S(1)}, u32[]{:S(2)}, u32[]{:S(2)}) collective-permute-start(f32[5,8,128]{2,1,0:T(8,128)S(1)} %add_add_fusion.own_ref), channel_id=1, source_target_pairs={{0,18},{1,19},{2,16},{3,17},{4,22},{5,23},{6,20},{7,21},{8,26},{9,... | collective-permute-start | bytes 61448 | tf_op jit(solution)/shard_map/ppermute | solution.py:186
  34.0 3.0 %collective-permute-start.14 = (f32[5,8,128]{2,1,0:T(8,128)S(1)}, f32[5,8,128]{2,1,0:T(8,128)S(1)}, u32[]{:S(2)}, u32[]{:S(2)}) collective-permute-start(f32[5,8,128]{2,1,0:T(8,128)S(1)} %add_add_fusion.own_ref), channel_id=1, source_target_pairs={{0,26},{1,27},{2,24},{3,25},{4,30},{5,31},{6,28},{7,29},{8,18},{9,... | collective-permute-start | bytes 61448 | tf_op jit(solution)/shard_map/ppermute | solution.py:186
  37.3 1.9 %collective-permute-done.14 = f32[5,8,128]{2,1,0:T(8,128)S(1)} collective-permute-done((f32[5,8,128]{2,1,0:T(8,128)S(1)}, f32[5,8,128]{2,1,0:T(8,128)S(1)}, u32[]{:S(2)}, u32[]{:S(2)}) %collective-permute-start.14) | collective-permute-done | bytes 20512 | tf_op jit(solution)/shard_map/ppermute | solution.py:186
  39.9 0.6 %collective-permute-done.16.own_ref = f32[5,8,128]{2,1,0:T(8,128)S(1)} collective-permute-done((f32[5,8,128]{2,1,0:T(8,128)S(1)}, f32[5,8,128]{2,1,0:T(8,128)S(1)}, u32[]{:S(2)}, u32[]{:S(2)}) %collective-permute-start.16) | collective-permute-done | bytes 20512 | tf_op jit(solution)/shard_map/ppermute | solution.py:186
  40.5 1.6 %shard_map.50.refs_0_ = f32[224,1280]{1,0:T(8,128)} custom-call(s32[2]{0:T(128)S(1)} %pad_add_fusion.place_ref, bf16[224,96]{1,0:T(8,128)(2,1)S(1)} %shard_map.47.combine_ref, f32[5,8,128]{2,1,0:T(8,128)S(1)} %collective-permute-done.16.own_ref, f32[3,5,8,128]{3,2,1,0:T(8,128)S(1)} %pad_maximum_fusion.others_ref), custom_call_target="tpu_custom_call" | custom-call | tf_op jit(solution)/shard_map/pallas_call | solution.py:256
  42.2 1.6 %shard_map.51 = f32[224,1280]{1,0:T(8,128)} custom-call(s32[2]{0:T(128)S(1)} %pad_add_fusion.place_ref, bf16[224,96]{1,0:T(8,128)(2,1)S(1)} %shard_map.47.combine_ref, f32[5,8,128]{2,1,0:T(8,128)S(1)} %add_add_fusion.own_ref, f32[3,5,8,128]{3,2,1,0:T(8,128)S(1)} %collective-permute-done.15.others_ref, ...), custom_call_target="tpu_custom_call", output_to_operand_aliasing={{}: (4, {})} | custom-call | tf_op jit(solution)/shard_map/pallas_call | solution.py:256
  (30 shorter events, 2.9 us)
Async XLA Ops:
  4.0 1.5 %collective-permute-start = (f32[4,7,8,128]{3,2,1,0:T(8,128)S(1)}, f32[4,7,8,128]{3,2,1,0:T(8,128)S(1)}, u32[]{:S(2)}, u32[]{:S(2)}) collective-permute-start(f32[4,7,8,128]{3,2,1,0:T(8,128)S(1)} %get-tuple-element.16), channel_id=1, source_target_pairs={{0,2},{1,3},{2,0},{3,1},{4,6},{5,7},{6,4},{7,5},{8,10},{9,11},{10,... | collective-permute-start | bytes 344072 | tf_op jit(solution)/shard_map/ppermute | solution.py:186
  5.5 5.3 %collective-permute-start.1 = (f32[7,8,128]{2,1,0:T(8,128)S(1)}, f32[7,8,128]{2,1,0:T(8,128)S(1)}, u32[]{:S(2)}, u32[]{:S(2)}) collective-permute-start(f32[7,8,128]{2,1,0:T(8,128)S(1)} %get-tuple-element.18), channel_id=1, source_target_pairs={{0,10},{1,11},{2,8},{3,9},{4,14},{5,15},{6,12},{7,13},{8,2},{9,3},... | collective-permute-start | bytes 86024 | tf_op jit(solution)/shard_map/ppermute | solution.py:186
  8.3 4.5 %collective-permute-start.2 = (f32[7,8,128]{2,1,0:T(8,128)S(1)}, f32[7,8,128]{2,1,0:T(8,128)S(1)}, u32[]{:S(2)}, u32[]{:S(2)}) collective-permute-start(f32[7,8,128]{2,1,0:T(8,128)S(1)} %get-tuple-element.19), channel_id=1, source_target_pairs={{0,18},{1,19},{2,16},{3,17},{4,22},{5,23},{6,20},{7,21},{8,26},{9,... | collective-permute-start | bytes 86024 | tf_op jit(solution)/shard_map/ppermute | solution.py:186
  10.8 5.1 %collective-permute-start.3 = (f32[7,8,128]{2,1,0:T(8,128)S(1)}, f32[7,8,128]{2,1,0:T(8,128)S(1)}, u32[]{:S(2)}, u32[]{:S(2)}) collective-permute-start(f32[7,8,128]{2,1,0:T(8,128)S(1)} %get-tuple-element.20), channel_id=1, source_target_pairs={{0,26},{1,27},{2,24},{3,25},{4,30},{5,31},{6,28},{7,29},{8,18},{9,... | collective-permute-start | bytes 86024 | tf_op jit(solution)/shard_map/ppermute | solution.py:186
  16.0 3.4 %collective-permute-start.4 = (f32[7,8,128]{2,1,0:T(8,128)S(1)}, f32[7,8,128]{2,1,0:T(8,128)S(1)}, u32[]{:S(2)}, u32[]{:S(2)}) collective-permute-start(f32[7,8,128]{2,1,0:T(8,128)S(1)} %get-tuple-element.27), channel_id=1, source_target_pairs={{0,3},{1,2},{2,1},{3,0},{4,7},{5,6},{6,5},{7,4},{8,11},{9,10},{10,... | collective-permute-start | bytes 86024 | tf_op jit(solution)/shard_map/ppermute | solution.py:186
  17.3 3.3 %collective-permute-start.5 = (f32[7,8,128]{2,1,0:T(8,128)S(1)}, f32[7,8,128]{2,1,0:T(8,128)S(1)}, u32[]{:S(2)}, u32[]{:S(2)}) collective-permute-start(f32[7,8,128]{2,1,0:T(8,128)S(1)} %get-tuple-element.27), channel_id=1, source_target_pairs={{0,6},{1,7},{2,4},{3,5},{4,2},{5,3},{6,0},{7,1},{8,14},{9,15},{10,... | collective-permute-start | bytes 86024 | tf_op jit(solution)/shard_map/ppermute | solution.py:186
  18.8 4.2 %collective-permute-start.6 = (f32[7,8,128]{2,1,0:T(8,128)S(1)}, f32[7,8,128]{2,1,0:T(8,128)S(1)}, u32[]{:S(2)}, u32[]{:S(2)}) collective-permute-start(f32[7,8,128]{2,1,0:T(8,128)S(1)} %get-tuple-element.27), channel_id=1, source_target_pairs={{0,7},{1,6},{2,5},{3,4},{4,3},{5,2},{6,1},{7,0},{8,15},{9,14},{10,... | collective-permute-start | bytes 86024 | tf_op jit(solution)/shard_map/ppermute | solution.py:186
  23.0 1.3 %collective-permute-start.7 = (f32[2,7,8,128]{3,2,1,0:T(8,128)S(1)}, f32[2,7,8,128]{3,2,1,0:T(8,128)S(1)}, u32[]{:S(2)}, u32[]{:S(2)}) collective-permute-start(f32[2,7,8,128]{3,2,1,0:T(8,128)S(1)} %pad_maximum_fusion.1.sent_ref), channel_id=1, source_target_pairs={{0,2},{1,3},{2,0},{3,1},{4,6},{5,7},{6,4},{7,5},{8,10},{9,11},{10,... | collective-permute-start | bytes 172040 | tf_op jit(solution)/shard_map/ppermute | solution.py:186
  26.6 1.2 %collective-permute-start.8 = (f32[10,8,128]{2,1,0:T(8,128)S(1)}, f32[10,8,128]{2,1,0:T(8,128)S(1)}, u32[]{:S(2)}, u32[]{:S(2)}) collective-permute-start(f32[10,8,128]{2,1,0:T(8,128)S(1)} %shard_map.49), channel_id=1, source_target_pairs={{0,2},{1,3},{2,0},{3,1},{4,6},{5,7},{6,4},{7,5},{8,10},{9,11},{10,... | collective-permute-start | bytes 122888 | tf_op jit(solution)/shard_map/ppermute | solution.py:186
  27.8 3.3 %collective-permute-start.10 = (f32[5,8,128]{2,1,0:T(8,128)S(1)}, f32[5,8,128]{2,1,0:T(8,128)S(1)}, u32[]{:S(2)}, u32[]{:S(2)}) collective-permute-start(f32[5,8,128]{2,1,0:T(8,128)S(1)} %slice_select_fusion), channel_id=1, source_target_pairs={{0,6},{1,7},{2,4},{3,5},{4,2},{5,3},{6,0},{7,1},{8,14},{9,15},{10,... | collective-permute-start | bytes 61448 | tf_op jit(solution)/shard_map/ppermute | solution.py:186
  28.2 4.1 %collective-permute-start.11 = (f32[5,8,128]{2,1,0:T(8,128)S(1)}, f32[5,8,128]{2,1,0:T(8,128)S(1)}, u32[]{:S(2)}, u32[]{:S(2)}) collective-permute-start(f32[5,8,128]{2,1,0:T(8,128)S(1)} %slice_select_fusion), channel_id=1, source_target_pairs={{0,7},{1,6},{2,5},{3,4},{4,3},{5,2},{6,1},{7,0},{8,15},{9,14},{10,... | collective-permute-start | bytes 61448 | tf_op jit(solution)/shard_map/ppermute | solution.py:186
  29.6 3.5 %collective-permute-start.9 = (f32[5,8,128]{2,1,0:T(8,128)S(1)}, f32[5,8,128]{2,1,0:T(8,128)S(1)}, u32[]{:S(2)}, u32[]{:S(2)}) collective-permute-start(f32[5,8,128]{2,1,0:T(8,128)S(1)} %slice_select_fusion), channel_id=1, source_target_pairs={{0,3},{1,2},{2,1},{3,0},{4,7},{5,6},{6,5},{7,4},{8,11},{9,10},{10,... | collective-permute-start | bytes 61448 | tf_op jit(solution)/shard_map/ppermute | solution.py:186
  33.1 3.9 %collective-permute-start.12 = (f32[5,8,128]{2,1,0:T(8,128)S(1)}, f32[5,8,128]{2,1,0:T(8,128)S(1)}, u32[]{:S(2)}, u32[]{:S(2)}) collective-permute-start(f32[5,8,128]{2,1,0:T(8,128)S(1)} %add_add_fusion.own_ref), channel_id=1, source_target_pairs={{0,10},{1,11},{2,8},{3,9},{4,14},{5,15},{6,12},{7,13},{8,2},{9,3},... | collective-permute-start | bytes 61448 | tf_op jit(solution)/shard_map/ppermute | solution.py:186
  33.2 4.2 %collective-permute-start.13 = (f32[5,8,128]{2,1,0:T(8,128)S(1)}, f32[5,8,128]{2,1,0:T(8,128)S(1)}, u32[]{:S(2)}, u32[]{:S(2)}) collective-permute-start(f32[5,8,128]{2,1,0:T(8,128)S(1)} %add_add_fusion.own_ref), channel_id=1, source_target_pairs={{0,18},{1,19},{2,16},{3,17},{4,22},{5,23},{6,20},{7,21},{8,26},{9,... | collective-permute-start | bytes 61448 | tf_op jit(solution)/shard_map/ppermute | solution.py:186
  34.0 5.2 %collective-permute-start.14 = (f32[5,8,128]{2,1,0:T(8,128)S(1)}, f32[5,8,128]{2,1,0:T(8,128)S(1)}, u32[]{:S(2)}, u32[]{:S(2)}) collective-permute-start(f32[5,8,128]{2,1,0:T(8,128)S(1)} %add_add_fusion.own_ref), channel_id=1, source_target_pairs={{0,26},{1,27},{2,24},{3,25},{4,30},{5,31},{6,28},{7,29},{8,18},{9,... | collective-permute-start | bytes 61448 | tf_op jit(solution)/shard_map/ppermute | solution.py:186
  39.2 3.0 %collective-permute-start.15 = (f32[3,5,8,128]{3,2,1,0:T(8,128)S(1)}, f32[3,5,8,128]{3,2,1,0:T(8,128)S(1)}, u32[]{:S(2)}, u32[]{:S(2)}) collective-permute-start(f32[3,5,8,128]{3,2,1,0:T(8,128)S(1)} %pad_maximum_fusion.others_ref), channel_id=1, source_target_pairs={{0,2},{1,3},{2,0},{3,1},{4,6},{5,7},{6,4},{7,5},{8,10},{9,11},{10,... | collective-permute-start | bytes 184328 | tf_op jit(solution)/shard_map/ppermute | solution.py:186
  39.3 1.2 %collective-permute-start.16 = (f32[5,8,128]{2,1,0:T(8,128)S(1)}, f32[5,8,128]{2,1,0:T(8,128)S(1)}, u32[]{:S(2)}, u32[]{:S(2)}) collective-permute-start(f32[5,8,128]{2,1,0:T(8,128)S(1)} %add_add_fusion.own_ref), channel_id=1, source_target_pairs={{0,2},{1,3},{2,0},{3,1},{4,6},{5,7},{6,4},{7,5},{8,10},{9,11},{10,... | collective-permute-start | bytes 61448 | tf_op jit(solution)/shard_map/ppermute | solution.py:186

commit v3 on v2

v3 whole, which is shorter than its diff:
```python
import functools

import jax
import jax.numpy as jnp
from jax import lax
from jax.experimental import pallas as pl
from jax.experimental.pallas import tpu as pltpu
from jax.sharding import PartitionSpec as P

SLOTS = 4
LANES = 128
AXES = ("expert", "seq", "fsdp")
VMEM = pl.BlockSpec(memory_space=pltpu.VMEM)
HBM = pl.BlockSpec(memory_space=pltpu.HBM)


def pieces(value, count):
    out = []
    for _ in range(count):
        part = value.astype(jnp.bfloat16)
        out.append(part)
        value = value - part.astype(jnp.float32)
    return out


def stacked(value):
    high, low = pieces(value, 2)
    return jnp.concatenate([high.astype(jnp.float32), low.astype(jnp.float32)], axis=0).astype(jnp.bfloat16)


def mm(left, right, contract=((1,), (0,))):
    return lax.dot_general(left, right, (contract, ((), ())), preferred_element_type=jnp.float32)


def pick(core, when_zero, when_one):
    return jnp.where(core == 0, when_zero, when_one)


def join(parts):
    top = functools.reduce(jnp.maximum, [p[-1] for p in parts])
    total = sum(p[:-1] * jnp.exp(p[-1] - top)[None] for p in parts)
    return jnp.concatenate([total, top[None]], axis=0)


def dispatch_kernel(chunks, tokens_hbm, params_hbm, w_in_hbm, logits_ref, mine_ref, theirs_ref, w_in_ref,
                    tokens_ref, params_ref, sums_ref, sems):
    core, expert = lax.axis_index("seq") % 2, lax.axis_index("expert")
    groups, tiles, rows, _ = mine_ref.shape
    half = tiles - 2
    slots, width = params_hbm.shape
    copies = [pltpu.make_async_copy(params_hbm, params_ref, sems.at[0])]
    for start, stop in chunks:
        own = pl.ds(start, stop - start)
        copies.append(pltpu.make_async_copy(tokens_hbm.at[own], tokens_ref.at[own], sems.at[len(copies)]))
    copies.append(pltpu.make_async_copy(w_in_hbm, w_in_ref, sems.at[len(copies)]))
    for copy in copies:
        copy.start()
    copies[0].wait()
    params = jnp.concatenate(pieces(params_ref[...], 3), axis=0)
    highs, lows, logits = [], [], []
    nt = ((1,), (1,))
    for (start, stop), copy in zip(chunks, copies[1:]):
        copy.wait()
        high, low, rest = pieces(tokens_ref[start:stop], 3)
        highs.append(high)
        lows.append(low)
        a = mm(params, high, nt)
        b = mm(params[:2 * slots], low, nt)
        c = mm(params[:slots], rest, nt)
        small = a[2 * slots:] + b[slots:] + c
        logits.append((small + (a[slots:2 * slots] + b[:slots])) + a[:slots])
    logits = jnp.concatenate(logits, axis=1)
    logits_ref[...] = logits
    peak = jnp.max(logits, axis=1, keepdims=True)
    weights = jnp.exp(logits - peak)
    mass = jnp.sum(weights, axis=1, keepdims=True)
    weight_high, weight_low = pieces(weights, 2)
    high = mm(jnp.concatenate([weight_high, weight_low], axis=0), jnp.concatenate(highs, axis=0))
    low = mm(weight_high, jnp.concatenate(lows, axis=0))
    sums_ref[:, :width] = high[:slots] + (high[slots:] + low)
    sums_ref[:, width:width + LANES] = jnp.broadcast_to(mass, (slots, LANES))
    sums_ref[:, width + LANES:] = jnp.broadcast_to(peak, (slots, LANES))
    for k in range(groups):
        own = pl.ds(pl.multiple_of((expert ^ k) * rows, rows), rows)
        sides = (core, 1 - core) if k else (1 - core, core)
        for ref, side in zip((mine_ref, theirs_ref), sides):
            for t in range(half):
                place = pl.ds(pl.multiple_of((side * half + t) * LANES, LANES), LANES)
                ref[k, t] = sums_ref[own, place]
            for t in range(2):
                ref[k, half + t] = sums_ref[own, width + t * LANES:width + (t + 1) * LANES]
    copies[-1].wait()


def chip_kernel(mine_ref, theirs_ref, *outs):
    for k, out_ref in enumerate(outs):
        out_ref[...] = join([mine_ref[k], theirs_ref[k]])


def split_out_kernel(_, w_hbm, high_ref, low_ref, flag_ref, w_ref, sems):
    experts, units, _ = w_hbm.shape
    parts = sems.shape[0] // experts
    count = units // parts
    copies = []
    for e in range(experts):
        for i in range(parts):
            own = pl.ds(i * count, count)
            copies.append(pltpu.make_async_copy(w_hbm.at[e, own], w_ref.at[e, own], sems.at[len(copies)]))
            copies[-1].start()
    for e in range(experts):
        for i in range(parts):
            copies[e * parts + i].wait()
            start = e * units + i * count
            own = slice(start, start + count)
            high_ref[own], low_ref[own] = pieces(w_ref[e, i * count:(i + 1) * count], 2)
    flag_ref[...] = jnp.zeros_like(flag_ref)


def split_in_kernel(_, w_ref, high_ref, low_ref, flag_ref):
    experts, units, width = w_ref.shape
    high, low = pieces(w_ref[...].reshape(experts * units, width), 2)
    high_ref[...] = high.T
    low_ref[...] = low.T
    flag_ref[...] = jnp.zeros_like(flag_ref)


def total_kernel(own_ref, *refs):
    *others, _, out_ref = refs
    out_ref[...] = join([own_ref[...]] + [r[...] for r in others])


def plane_kernel(own_ref, *refs):
    *others, _, out_ref = refs
    out_ref[0] = join([r[...] for r in others])
    out_ref[1] = own_ref[...]


def stack_kernel(_, *refs):
    *others, out_ref = refs
    for k, r in enumerate(others):
        out_ref[k] = r[...]


def combine_kernel(logits_ref, out_ref):
    logits = logits_ref[...]
    top = jnp.max(logits, axis=0, keepdims=True)
    powers = jnp.exp(logits - top)
    combine = (powers / jnp.sum(powers, axis=0, keepdims=True)).T
    high, low = pieces(combine, 2)
    out_ref[...] = jnp.concatenate([high, low, high], axis=1)


def expert_kernel(sent_ref, got_ref, in_high_ref, in_low_ref, out_high_ref, out_low_ref, out_ref):
    core = lax.axis_index("seq") % 2
    tiles, rows, _ = out_ref.shape
    half = tiles // 2
    experts = rows // SLOTS
    units = in_high_ref.shape[1] // experts
    near = join([sent_ref[0], got_ref[1]])
    far = join([sent_ref[1], got_ref[0]])
    near = [near[t] / near[half] for t in range(half)]
    far = [far[t] / far[half] for t in range(half)]
    first = [pick(core, a, b) for a, b in zip(near, far)]
    second = [pick(core, b, a) for a, b in zip(near, far)]
    inputs = stacked(jnp.concatenate(first + second, axis=1))
    large = mm(inputs, in_high_ref[...])
    small = mm(inputs, in_low_ref[...])
    value = large[:rows] + (large[rows:] + small[:rows])
    value = value * (1.0 + lax.erf(value * (0.5 ** 0.5))) * 0.5
    slot = lax.broadcasted_iota(jnp.int32, value.shape, 0)
    unit = lax.broadcasted_iota(jnp.int32, value.shape, 1)
    keep = None
    for e in range(experts):
        inside = (slot // SLOTS == e) & (unit >= e * units) & (unit < (e + 1) * units)
        keep = inside if keep is None else keep | inside
    hidden = stacked(jnp.where(keep, value, 0.0))
    large = mm(hidden, out_high_ref[...])
    small = mm(hidden, out_low_ref[...])
    out = large[:rows] + (large[rows:] + small[:rows])
    for t in range(tiles):
        out_ref[t] = out[:, t * LANES:(t + 1) * LANES]


def mix_kernel(near, combine_ref, own_ref, others_ref, *refs):
    out_hbm, slots_ref, out_ref, sems = refs[-4:]
    core, expert = lax.axis_index("seq") % 2, lax.axis_index("expert")
    half, rows, _ = own_ref.shape
    groups = others_ref.shape[0] + 1
    for k in range(groups):
        place = pl.ds(pl.multiple_of((expert ^ k) * rows, rows), rows)
        for t in range(half):
            slots_ref[place, t * LANES:(t + 1) * LANES] = others_ref[k - 1, t] if k else own_ref[t]
    high, low = pieces(slots_ref[...], 2)
    slots = jnp.concatenate([high, high, low], axis=0)
    side = core if near else 1 - core
    columns = pl.ds(pl.multiple_of(side * (half * LANES), LANES), half * LANES)
    parts = sems.shape[0]
    count = combine_ref.shape[0] // parts
    copies = []
    for i in range(parts):
        own = slice(i * count, (i + 1) * count)
        out_ref[own] = mm(combine_ref[own], slots)
        place = pl.ds(i * count, count)
        copies.append(pltpu.make_async_copy(out_ref.at[place], out_hbm.at[place, columns], sems.at[i]))
        copies[i].start()
    for copy in copies:
        copy.wait()


def solution(mesh):
    n_expert, n_seq, n_fsdp = (mesh.shape[a] for a in AXES)
    n_x = n_seq // 2

    def permute(value, target):
        pairs = []
        for e in range(n_expert):
            for s in range(n_seq):
                for f in range(n_fsdp):
                    te, tx, tc, tf = target(e, s // 2, s % 2, f)
                    pairs.append(((e * n_seq + s) * n_fsdp + f, (te * n_seq + tx * 2 + tc) * n_fsdp + tf))
        return lax.ppermute(value, AXES, pairs)

    def other_core(value):
        return permute(value, lambda e, x, c, f: (e, x, 1 - c, f))

    def along_expert(value, k):
        return permute(value, lambda e, x, c, f: (e ^ k, x, 1 - c, f))

    def plane(value):
        return [
            permute(value, lambda e, x, c, f, dx=dx, df=df: (e, (x + dx) % n_x, 1 - c, (f + df) % n_fsdp))
            for dx in range(n_x) for df in range(n_fsdp) if dx or df
        ]

    def body(tokens, slot_params, w_in, w_out):
        count, width = tokens.shape
        slots = slot_params.shape[1]
        rows = w_in.shape[0] * SLOTS
        half = width // LANES // 2
        f32 = jnp.float32
        params = pltpu.CompilerParams(vmem_limit_bytes=24 * 1024 * 1024)
        core = lax.axis_index("seq") % 2
        chunks = [(i, min(i + LANES, count)) for i in range(0, count, LANES)]

        in_hbm = lambda value: pltpu.with_memory_space_constraint(value, pltpu.HBM)
        shape = pltpu.VMEM((n_expert, half + 2, rows, LANES), f32)
        logits, mine, theirs, w_in = pl.pallas_call(
            functools.partial(dispatch_kernel, chunks),
            out_shape=(pltpu.VMEM((slots, count), f32), shape, shape, pltpu.VMEM(w_in.shape, f32)),
            in_specs=[HBM, HBM, HBM],
            out_specs=(VMEM,) * 4,
            scratch_shapes=[
                pltpu.VMEM((count, width), f32),
                pltpu.VMEM((slots, width), f32),
                pltpu.VMEM((slots, width + 2 * LANES), f32),
                pltpu.SemaphoreType.DMA((len(chunks) + 2,)),
            ],
            compiler_params=params,
        )(in_hbm(tokens), in_hbm(slot_params.T), in_hbm(w_in))
        combine = pl.pallas_call(
            combine_kernel,
            out_shape=jax.ShapeDtypeStruct((count, 3 * slots), jnp.bfloat16),
            in_specs=[VMEM],
            out_specs=VMEM,
            compiler_params=params,
        )(logits)

        chip = pl.pallas_call(
            chip_kernel,
            out_shape=(pltpu.VMEM((half + 2, rows, LANES), f32),) * n_expert,
            in_specs=[VMEM, VMEM],
            out_specs=(VMEM,) * n_expert,
            compiler_params=params,
        )(mine, other_core(theirs))
        order = list(range(n_expert - 1, 0, -1))
        flag = pltpu.VMEM((8, LANES), f32)
        experts, units, _ = w_in.shape
        cost = pl.CostEstimate(flops=8 * w_in.size, bytes_accessed=8 * w_in.size, transcendentals=0)

        def local(kernel, out, *args):
            return pl.pallas_call(
                kernel, out_shape=out, in_specs=[VMEM] * len(args), out_specs=VMEM, compiler_params=params
            )(*args)

        part = pltpu.VMEM((experts * units, width), jnp.bfloat16)
        parts = 4 if units % 64 == 0 else 1
        out_high, out_low, ready = pl.pallas_call(
            split_out_kernel,
            out_shape=(part, part, flag),
            in_specs=[VMEM, HBM],
            out_specs=(VMEM,) * 3,
            scratch_shapes=[pltpu.VMEM(w_out.shape, f32), pltpu.SemaphoreType.DMA((experts * parts,))],
            cost_estimate=cost,
            compiler_params=params,
        )(chip[0], in_hbm(w_out))
        shape = pltpu.VMEM((half + 2, rows, LANES), f32)
        total = local(total_kernel, shape, chip[0], *[along_expert(chip[k], k) for k in order], ready)
        part = pltpu.VMEM((width, experts * units), jnp.bfloat16)
        in_high, in_low, ready = pl.pallas_call(
            split_in_kernel,
            out_shape=(part, part, flag),
            in_specs=[VMEM, VMEM],
            out_specs=(VMEM,) * 3,
            cost_estimate=cost,
            compiler_params=params,
        )(total, w_in)
        shape = pltpu.VMEM((2, half + 2, rows, LANES), f32)
        sent = local(plane_kernel, shape, total, *plane(total), ready)
        shape = pltpu.VMEM((2 * half, rows, LANES), f32)
        partial = local(expert_kernel, shape, sent, other_core(sent), in_high, in_low, out_high, out_low)
        partial = partial + other_core(partial)
        first, second = partial[:half], partial[half:]
        own = pick(core, second, first) + sum(plane(pick(core, first, second)))
        arrived = {k: along_expert(own, k) for k in order}
        own_near = other_core(own)
        shape = pltpu.VMEM((n_expert - 1, half, rows, LANES), f32)
        others = local(stack_kernel, shape, own_near, *[arrived[k] for k in range(1, n_expert)])

        def mix(near, own, others, *out):
            return pl.pallas_call(
                functools.partial(mix_kernel, near),
                out_shape=jax.ShapeDtypeStruct((count, width), f32),
                in_specs=[VMEM, VMEM, VMEM] + [HBM] * len(out),
                out_specs=HBM,
                scratch_shapes=[
                    pltpu.VMEM((slots, half * LANES), f32),
                    pltpu.VMEM((count, half * LANES), f32),
                    pltpu.SemaphoreType.DMA((2 if count % 32 == 0 else 1,)),
                ],
                input_output_aliases={3: 0} if out else {},
                compiler_params=params,
            )(combine, own, others, *out)

        mixed = mix(True, own_near, others)
        return mix(False, own, other_core(others), mixed)

    return jax.shard_map(
        body,
        mesh=mesh,
        in_specs=(P(AXES, None), P(), P("expert", ("seq", "fsdp"), None), P("expert", ("seq", "fsdp"), None)),
        out_specs=P(AXES, None),
        check_vma=False,
    )
```

time: 43.9 us -> 39.4 us (0.90)
  waiting for transfers between devices: 17.2 us -> 12.3 us
  starting transfers between devices: 16.7 us -> 17.8 us
  Pallas kernels: 9.56 us -> 9.07 us
    ppermute x17, waiting for transfers between devices: 17.2 us -> 12.3 us  [permute(): return lax.ppermute(value, AXES, pairs)]
    pallas_call x1 -> x6, Pallas kernels: 2.21 us -> 3.95 us  [the longest x1 2 us: body(): pl.pallas_call(split_out_kernel, out_shape=(part, part, flag), in_specs=[...]
    pallas_call x1, Pallas kernels: 3.94 us -> 2.79 us  [body(): pl.pallas_call(functools.partial(dispatch_kernel, chunks), out_shape=(plt...]
    pallas_call x2, Pallas kernels: 3.19 us -> 2.1 us  [mix(): pl.pallas_call(functools.partial(mix_kernel, near), out_shape=jax.ShapeDt...]
    ppermute x17, starting transfers between devices: 16.7 us -> 17.8 us  [permute(): return lax.ppermute(value, AXES, pairs)]
  transfers between devices with their start and end apart: 17 -> 17, of which waited for: 14 -> 10; matrix products, arithmetic and copies ran while one was open for 0% -> 0% of each run, Pallas kernels for 4% -> 11%
where the time goes in v3:
time: 39.4 us; the launch traced here: 39.3 us
  starting transfers between devices  17.8 us (45%)
  waiting for transfers between devices  12.3 us (31%)
  Pallas kernels  9.07 us (23%)
    ppermute x17, starting transfers between devices, permute(): return lax.ppermute(value, AXES, pairs)  17.8 us
    ppermute x17, waiting for transfers between devices, permute(): return lax.ppermute(value, AXES, pairs)  12.3 us
    pallas_call x1, Pallas kernels, body(): pl.pallas_call(functools.partial(dispatch_kernel, chunks), out_shape=(plt...  2.79 us
    pallas_call x2, Pallas kernels, mix(): pl.pallas_call(functools.partial(mix_kernel, near), out_shape=jax.ShapeDt...  2.1 us
    pallas_call x1, Pallas kernels, body(): pl.pallas_call(split_out_kernel, out_shape=(part, part, flag), in_specs=[...  2 us
    pallas_call x4, Pallas kernels, local(): pl.pallas_call(kernel, out_shape=out, in_specs=[VMEM] * len(args), out_sp...  1.05 us
    pallas_call x1, Pallas kernels, body(): pl.pallas_call(split_in_kernel, out_shape=(part, part, flag), in_specs=[V...  0.89 us
  transfers between devices with their start and end apart: 17, of which 10 were waited for; matrix products, arithmetic and copies ran while one was open for 0% of the time, Pallas kernels for 11%

profile of v3, /device:TPU:0, one launch (start us, length us, event | category | flops | bytes accessed | tf_op | source)
XLA Modules:
  0.0 39.3 jit_solution(7709735712434196467)
XLA Ops:
  0.0 2.8 %shard_map.46 = (f32[32,224]{1,0:T(8,128)S(1)}, f32[4,7,8,128]{3,2,1,0:T(8,128)S(1)}, f32[4,7,8,128]{3,2,1,0:T(8,128)S(1)}, f32[2,320,1280]{2,1,0:T(8,128)S(1)}) custom-call(f32[224,1280]{1,0:T(8,128)} %tokens_hbm.1, f32[32,1280]{1,0:T(8,128)} %bitcast.1, f32[2,320,1280]{2,1,0:T(8,128)} %w_in_hbm.1), custom_call_target="tpu_custom_call" | custom-call | tf_op jit(solution)/shard_map/pallas_call | solution.py:247
  3.3 1.0 %collective-permute-done.theirs_ref = f32[4,7,8,128]{3,2,1,0:T(8,128)S(1)} collective-permute-done((f32[4,7,8,128]{3,2,1,0:T(8,128)S(1)}, f32[4,7,8,128]{3,2,1,0:T(8,128)S(1)}, u32[]{:S(2)}, u32[]{:S(2)}) %collective-permute-start) | collective-permute-done | bytes 114720 | tf_op jit(solution)/shard_map/ppermute | solution.py:221
  4.3 4.8 %collective-permute-start.1 = (f32[7,8,128]{2,1,0:T(8,128)S(1)}, f32[7,8,128]{2,1,0:T(8,128)S(1)}, u32[]{:S(2)}, u32[]{:S(2)}) collective-permute-start(f32[7,8,128]{2,1,0:T(8,128)S(1)} %get-tuple-element.23), channel_id=1, source_target_pairs={{0,26},{1,27},{2,24},{3,25},{4,30},{5,31},{6,28},{7,29},{8,18},{9,... | collective-permute-start | bytes 86024 | tf_op jit(solution)/shard_map/ppermute | solution.py:221
  9.1 0.6 %collective-permute-start.3 = (f32[7,8,128]{2,1,0:T(8,128)S(1)}, f32[7,8,128]{2,1,0:T(8,128)S(1)}, u32[]{:S(2)}, u32[]{:S(2)}) collective-permute-start(f32[7,8,128]{2,1,0:T(8,128)S(1)} %get-tuple-element.25), channel_id=1, source_target_pairs={{0,10},{1,11},{2,8},{3,9},{4,14},{5,15},{6,12},{7,13},{8,2},{9,3},... | collective-permute-start | bytes 86024 | tf_op jit(solution)/shard_map/ppermute | solution.py:221
  9.7 2.0 %shard_map.49 = (bf16[640,1280]{1,0:T(8,128)(2,1)S(1)}, bf16[640,1280]{1,0:T(8,128)(2,1)S(1)}, f32[8,128]{1,0:T(8,128)S(1)}) custom-call(f32[7,8,128]{2,1,0:T(8,128)S(1)} %get-tuple-element.22._.own_ref, f32[2,320,1280]{2,1,0:T(8,128)} %w_hbm.1), custom_call_target="tpu_custom_call" | custom-call | flops 6553600 | bytes 6553600 | tf_op jit(solution)/shard_map/pallas_call | solution.py:287
  11.7 1.6 %collective-permute-done.2.refs_1_ = f32[7,8,128]{2,1,0:T(8,128)S(1)} collective-permute-done((f32[7,8,128]{2,1,0:T(8,128)S(1)}, f32[7,8,128]{2,1,0:T(8,128)S(1)}, u32[]{:S(2)}, u32[]{:S(2)}) %collective-permute-start.2) | collective-permute-done | bytes 28704 | tf_op jit(solution)/shard_map/ppermute | solution.py:221
  13.3 1.5 %collective-permute-start.4 = (f32[7,8,128]{2,1,0:T(8,128)S(1)}, f32[7,8,128]{2,1,0:T(8,128)S(1)}, u32[]{:S(2)}, u32[]{:S(2)}) collective-permute-start(f32[7,8,128]{2,1,0:T(8,128)S(1)} %shard_map.50._.own_ref), channel_id=1, source_target_pairs={{0,3},{1,2},{2,1},{3,0},{4,7},{5,6},{6,5},{7,4},{8,11},{9,10},{10,... | collective-permute-start | bytes 86024 | tf_op jit(solution)/shard_map/ppermute | solution.py:221
  14.9 1.3 %collective-permute-start.5 = (f32[7,8,128]{2,1,0:T(8,128)S(1)}, f32[7,8,128]{2,1,0:T(8,128)S(1)}, u32[]{:S(2)}, u32[]{:S(2)}) collective-permute-start(f32[7,8,128]{2,1,0:T(8,128)S(1)} %shard_map.50._.own_ref), channel_id=1, source_target_pairs={{0,6},{1,7},{2,4},{3,5},{4,2},{5,3},{6,0},{7,1},{8,14},{9,15},{10,... | collective-permute-start | bytes 86024 | tf_op jit(solution)/shard_map/ppermute | solution.py:221
  16.6 0.9 %shard_map.51 = (bf16[1280,640]{1,0:T(8,128)(2,1)S(1)}, bf16[1280,640]{1,0:T(8,128)(2,1)S(1)}, f32[8,128]{1,0:T(8,128)S(1)}) custom-call(f32[7,8,128]{2,1,0:T(8,128)S(1)} %shard_map.50._.own_ref, f32[2,320,1280]{2,1,0:T(8,128)S(1)} %get-tuple-element.27.w_ref), custom_call_target="tpu_custom_call" | custom-call | flops 6553600 | bytes 6553600 | tf_op jit(solution)/shard_map/pallas_call | solution.py:299
  17.5 0.7 %collective-permute-done.5.refs_1_ = f32[7,8,128]{2,1,0:T(8,128)S(1)} collective-permute-done((f32[7,8,128]{2,1,0:T(8,128)S(1)}, f32[7,8,128]{2,1,0:T(8,128)S(1)}, u32[]{:S(2)}, u32[]{:S(2)}) %collective-permute-start.5) | collective-permute-done | bytes 28704 | tf_op jit(solution)/shard_map/ppermute | solution.py:221
  18.2 2.2 %collective-permute-done.6.refs_2_ = f32[7,8,128]{2,1,0:T(8,128)S(1)} collective-permute-done((f32[7,8,128]{2,1,0:T(8,128)S(1)}, f32[7,8,128]{2,1,0:T(8,128)S(1)}, u32[]{:S(2)}, u32[]{:S(2)}) %collective-permute-start.6) | collective-permute-done | bytes 28704 | tf_op jit(solution)/shard_map/ppermute | solution.py:221
  20.8 0.9 %collective-permute-done.7.got_ref = f32[2,7,8,128]{3,2,1,0:T(8,128)S(1)} collective-permute-done((f32[2,7,8,128]{3,2,1,0:T(8,128)S(1)}, f32[2,7,8,128]{3,2,1,0:T(8,128)S(1)}, u32[]{:S(2)}, u32[]{:S(2)}) %collective-permute-start.7) | collective-permute-done | bytes 57376 | tf_op jit(solution)/shard_map/ppermute | solution.py:221
  21.7 1.0 %shard_map.53 = f32[10,8,128]{2,1,0:T(8,128)S(1)} custom-call(f32[2,7,8,128]{3,2,1,0:T(8,128)S(1)} %shard_map.52.sent_ref, f32[2,7,8,128]{3,2,1,0:T(8,128)S(1)} %collective-permute-done.7.got_ref, bf16[1280,640]{1,0:T(8,128)(2,1)S(1)} %get-tuple-element.29.in_high_ref, bf16[1280,640]{1,0:T(8,128)(2,1)S(1)} %get-tuple-element.30.in_low_ref, ...), custom_call_target="tpu_custom_call" | custom-call | tf_op jit(solution)/shard_map/pallas_call | solution.py:281
  23.0 0.9 %collective-permute-done.8 = f32[10,8,128]{2,1,0:T(8,128)S(1)} collective-permute-done((f32[10,8,128]{2,1,0:T(8,128)S(1)}, f32[10,8,128]{2,1,0:T(8,128)S(1)}, u32[]{:S(2)}, u32[]{:S(2)}) %collective-permute-start.8) | collective-permute-done | bytes 40992 | tf_op jit(solution)/shard_map/ppermute | solution.py:221
  24.5 1.2 %collective-permute-start.11 = (f32[5,8,128]{2,1,0:T(8,128)S(1)}, f32[5,8,128]{2,1,0:T(8,128)S(1)}, u32[]{:S(2)}, u32[]{:S(2)}) collective-permute-start(f32[5,8,128]{2,1,0:T(8,128)S(1)} %slice_select_fusion), channel_id=1, source_target_pairs={{0,7},{1,6},{2,5},{3,4},{4,3},{5,2},{6,1},{7,0},{8,15},{9,14},{10,... | collective-permute-start | bytes 61448 | tf_op jit(solution)/shard_map/ppermute | solution.py:221
  25.7 1.5 %collective-permute-start.9 = (f32[5,8,128]{2,1,0:T(8,128)S(1)}, f32[5,8,128]{2,1,0:T(8,128)S(1)}, u32[]{:S(2)}, u32[]{:S(2)}) collective-permute-start(f32[5,8,128]{2,1,0:T(8,128)S(1)} %slice_select_fusion), channel_id=1, source_target_pairs={{0,3},{1,2},{2,1},{3,0},{4,7},{5,6},{6,5},{7,4},{8,11},{9,10},{10,... | collective-permute-start | bytes 61448 | tf_op jit(solution)/shard_map/ppermute | solution.py:221
  27.2 1.4 %collective-permute-done.11 = f32[5,8,128]{2,1,0:T(8,128)S(1)} collective-permute-done((f32[5,8,128]{2,1,0:T(8,128)S(1)}, f32[5,8,128]{2,1,0:T(8,128)S(1)}, u32[]{:S(2)}, u32[]{:S(2)}) %collective-permute-start.11) | collective-permute-done | bytes 20512 | tf_op jit(solution)/shard_map/ppermute | solution.py:221
  29.3 0.6 %collective-permute-start.13 = (f32[5,8,128]{2,1,0:T(8,128)S(1)}, f32[5,8,128]{2,1,0:T(8,128)S(1)}, u32[]{:S(2)}, u32[]{:S(2)}) collective-permute-start(f32[5,8,128]{2,1,0:T(8,128)S(1)} %add_add_fusion.own_ref), channel_id=1, source_target_pairs={{0,10},{1,11},{2,8},{3,9},{4,14},{5,15},{6,12},{7,13},{8,2},{9,3},... | collective-permute-start | bytes 61448 | tf_op jit(solution)/shard_map/ppermute | solution.py:221
  29.9 1.7 %collective-permute-start.14 = (f32[5,8,128]{2,1,0:T(8,128)S(1)}, f32[5,8,128]{2,1,0:T(8,128)S(1)}, u32[]{:S(2)}, u32[]{:S(2)}) collective-permute-start(f32[5,8,128]{2,1,0:T(8,128)S(1)} %add_add_fusion.own_ref), channel_id=1, source_target_pairs={{0,18},{1,19},{2,16},{3,17},{4,22},{5,23},{6,20},{7,21},{8,26},{9,... | collective-permute-start | bytes 61448 | tf_op jit(solution)/shard_map/ppermute | solution.py:221
  31.6 1.8 %collective-permute-start.15 = (f32[5,8,128]{2,1,0:T(8,128)S(1)}, f32[5,8,128]{2,1,0:T(8,128)S(1)}, u32[]{:S(2)}, u32[]{:S(2)}) collective-permute-start(f32[5,8,128]{2,1,0:T(8,128)S(1)} %add_add_fusion.own_ref), channel_id=1, source_target_pairs={{0,26},{1,27},{2,24},{3,25},{4,30},{5,31},{6,28},{7,29},{8,18},{9,... | collective-permute-start | bytes 61448 | tf_op jit(solution)/shard_map/ppermute | solution.py:221
  33.4 0.6 %collective-permute-done.14.refs_1_ = f32[5,8,128]{2,1,0:T(8,128)S(1)} collective-permute-done((f32[5,8,128]{2,1,0:T(8,128)S(1)}, f32[5,8,128]{2,1,0:T(8,128)S(1)}, u32[]{:S(2)}, u32[]{:S(2)}) %collective-permute-start.14) | collective-permute-done | bytes 20512 | tf_op jit(solution)/shard_map/ppermute | solution.py:221
  34.0 2.6 %collective-permute-done.15.refs_2_ = f32[5,8,128]{2,1,0:T(8,128)S(1)} collective-permute-done((f32[5,8,128]{2,1,0:T(8,128)S(1)}, f32[5,8,128]{2,1,0:T(8,128)S(1)}, u32[]{:S(2)}, u32[]{:S(2)}) %collective-permute-start.15) | collective-permute-done | bytes 20512 | tf_op jit(solution)/shard_map/ppermute | solution.py:221
  37.1 1.0 %shard_map.55.refs_0_ = f32[224,1280]{1,0:T(8,128)} custom-call(bf16[224,96]{1,0:T(8,128)(2,1)S(1)} %shard_map.47.combine_ref, f32[5,8,128]{2,1,0:T(8,128)S(1)} %collective-permute-done.12._.own_ref, f32[3,5,8,128]{3,2,1,0:T(8,128)S(1)} %shard_map.54.others_ref), custom_call_target="tpu_custom_call" | custom-call | tf_op jit(solution)/shard_map/pallas_call | solution.py:320
  38.2 1.1 %shard_map.56 = f32[224,1280]{1,0:T(8,128)} custom-call(bf16[224,96]{1,0:T(8,128)(2,1)S(1)} %shard_map.47.combine_ref, f32[5,8,128]{2,1,0:T(8,128)S(1)} %add_add_fusion.own_ref, f32[3,5,8,128]{3,2,1,0:T(8,128)S(1)} %collective-permute-done.16.others_ref, f32[224,1280]{1,0:T(8,128)} %shard_map.55.refs_0_), custom_call_target="tpu_custom_call", output_to_operand_aliasing={{}: (3, {})} | custom-call | tf_op jit(solution)/shard_map/pallas_call | solution.py:320
  (24 shorter events, 3.7 us)
Async XLA Ops:
  2.8 1.5 %collective-permute-start = (f32[4,7,8,128]{3,2,1,0:T(8,128)S(1)}, f32[4,7,8,128]{3,2,1,0:T(8,128)S(1)}, u32[]{:S(2)}, u32[]{:S(2)}) collective-permute-start(f32[4,7,8,128]{3,2,1,0:T(8,128)S(1)} %get-tuple-element.21), channel_id=1, source_target_pairs={{0,2},{1,3},{2,0},{3,1},{4,6},{5,7},{6,4},{7,5},{8,10},{9,11},{10,... | collective-permute-start | bytes 344072 | tf_op jit(solution)/shard_map/ppermute | solution.py:221
  4.3 7.4 %collective-permute-start.1 = (f32[7,8,128]{2,1,0:T(8,128)S(1)}, f32[7,8,128]{2,1,0:T(8,128)S(1)}, u32[]{:S(2)}, u32[]{:S(2)}) collective-permute-start(f32[7,8,128]{2,1,0:T(8,128)S(1)} %get-tuple-element.23), channel_id=1, source_target_pairs={{0,26},{1,27},{2,24},{3,25},{4,30},{5,31},{6,28},{7,29},{8,18},{9,... | collective-permute-start | bytes 86024 | tf_op jit(solution)/shard_map/ppermute | solution.py:221
  9.1 4.2 %collective-permute-start.2 = (f32[7,8,128]{2,1,0:T(8,128)S(1)}, f32[7,8,128]{2,1,0:T(8,128)S(1)}, u32[]{:S(2)}, u32[]{:S(2)}) collective-permute-start(f32[7,8,128]{2,1,0:T(8,128)S(1)} %get-tuple-element.24), channel_id=1, source_target_pairs={{0,18},{1,19},{2,16},{3,17},{4,22},{5,23},{6,20},{7,21},{8,26},{9,... | collective-permute-start | bytes 86024 | tf_op jit(solution)/shard_map/ppermute | solution.py:221
  9.1 4.2 %collective-permute-start.3 = (f32[7,8,128]{2,1,0:T(8,128)S(1)}, f32[7,8,128]{2,1,0:T(8,128)S(1)}, u32[]{:S(2)}, u32[]{:S(2)}) collective-permute-start(f32[7,8,128]{2,1,0:T(8,128)S(1)} %get-tuple-element.25), channel_id=1, source_target_pairs={{0,10},{1,11},{2,8},{3,9},{4,14},{5,15},{6,12},{7,13},{8,2},{9,3},... | collective-permute-start | bytes 86024 | tf_op jit(solution)/shard_map/ppermute | solution.py:221
  13.3 4.1 %collective-permute-start.4 = (f32[7,8,128]{2,1,0:T(8,128)S(1)}, f32[7,8,128]{2,1,0:T(8,128)S(1)}, u32[]{:S(2)}, u32[]{:S(2)}) collective-permute-start(f32[7,8,128]{2,1,0:T(8,128)S(1)} %shard_map.50._.own_ref), channel_id=1, source_target_pairs={{0,3},{1,2},{2,1},{3,0},{4,7},{5,6},{6,5},{7,4},{8,11},{9,10},{10,... | collective-permute-start | bytes 86024 | tf_op jit(solution)/shard_map/ppermute | solution.py:221
  14.9 3.3 %collective-permute-start.5 = (f32[7,8,128]{2,1,0:T(8,128)S(1)}, f32[7,8,128]{2,1,0:T(8,128)S(1)}, u32[]{:S(2)}, u32[]{:S(2)}) collective-permute-start(f32[7,8,128]{2,1,0:T(8,128)S(1)} %shard_map.50._.own_ref), channel_id=1, source_target_pairs={{0,6},{1,7},{2,4},{3,5},{4,2},{5,3},{6,0},{7,1},{8,14},{9,15},{10,... | collective-permute-start | bytes 86024 | tf_op jit(solution)/shard_map/ppermute | solution.py:221
  16.1 4.2 %collective-permute-start.6 = (f32[7,8,128]{2,1,0:T(8,128)S(1)}, f32[7,8,128]{2,1,0:T(8,128)S(1)}, u32[]{:S(2)}, u32[]{:S(2)}) collective-permute-start(f32[7,8,128]{2,1,0:T(8,128)S(1)} %shard_map.50._.own_ref), channel_id=1, source_target_pairs={{0,7},{1,6},{2,5},{3,4},{4,3},{5,2},{6,1},{7,0},{8,15},{9,14},{10,... | collective-permute-start | bytes 86024 | tf_op jit(solution)/shard_map/ppermute | solution.py:221
  20.3 1.3 %collective-permute-start.7 = (f32[2,7,8,128]{3,2,1,0:T(8,128)S(1)}, f32[2,7,8,128]{3,2,1,0:T(8,128)S(1)}, u32[]{:S(2)}, u32[]{:S(2)}) collective-permute-start(f32[2,7,8,128]{3,2,1,0:T(8,128)S(1)} %shard_map.52.sent_ref), channel_id=1, source_target_pairs={{0,2},{1,3},{2,0},{3,1},{4,6},{5,7},{6,4},{7,5},{8,10},{9,11},{10,... | collective-permute-start | bytes 172040 | tf_op jit(solution)/shard_map/ppermute | solution.py:221
  22.7 1.2 %collective-permute-start.8 = (f32[10,8,128]{2,1,0:T(8,128)S(1)}, f32[10,8,128]{2,1,0:T(8,128)S(1)}, u32[]{:S(2)}, u32[]{:S(2)}) collective-permute-start(f32[10,8,128]{2,1,0:T(8,128)S(1)} %shard_map.53), channel_id=1, source_target_pairs={{0,2},{1,3},{2,0},{3,1},{4,6},{5,7},{6,4},{7,5},{8,10},{9,11},{10,... | collective-permute-start | bytes 122888 | tf_op jit(solution)/shard_map/ppermute | solution.py:221
  23.9 3.3 %collective-permute-start.10 = (f32[5,8,128]{2,1,0:T(8,128)S(1)}, f32[5,8,128]{2,1,0:T(8,128)S(1)}, u32[]{:S(2)}, u32[]{:S(2)}) collective-permute-start(f32[5,8,128]{2,1,0:T(8,128)S(1)} %slice_select_fusion), channel_id=1, source_target_pairs={{0,6},{1,7},{2,4},{3,5},{4,2},{5,3},{6,0},{7,1},{8,14},{9,15},{10,... | collective-permute-start | bytes 61448 | tf_op jit(solution)/shard_map/ppermute | solution.py:221
  24.5 4.1 %collective-permute-start.11 = (f32[5,8,128]{2,1,0:T(8,128)S(1)}, f32[5,8,128]{2,1,0:T(8,128)S(1)}, u32[]{:S(2)}, u32[]{:S(2)}) collective-permute-start(f32[5,8,128]{2,1,0:T(8,128)S(1)} %slice_select_fusion), channel_id=1, source_target_pairs={{0,7},{1,6},{2,5},{3,4},{4,3},{5,2},{6,1},{7,0},{8,15},{9,14},{10,... | collective-permute-start | bytes 61448 | tf_op jit(solution)/shard_map/ppermute | solution.py:221
  25.7 3.4 %collective-permute-start.9 = (f32[5,8,128]{2,1,0:T(8,128)S(1)}, f32[5,8,128]{2,1,0:T(8,128)S(1)}, u32[]{:S(2)}, u32[]{:S(2)}) collective-permute-start(f32[5,8,128]{2,1,0:T(8,128)S(1)} %slice_select_fusion), channel_id=1, source_target_pairs={{0,3},{1,2},{2,1},{3,0},{4,7},{5,6},{6,5},{7,4},{8,11},{9,10},{10,... | collective-permute-start | bytes 61448 | tf_op jit(solution)/shard_map/ppermute | solution.py:221
  29.1 4.3 %collective-permute-start.12 = (f32[5,8,128]{2,1,0:T(8,128)S(1)}, f32[5,8,128]{2,1,0:T(8,128)S(1)}, u32[]{:S(2)}, u32[]{:S(2)}) collective-permute-start(f32[5,8,128]{2,1,0:T(8,128)S(1)} %add_add_fusion.own_ref), channel_id=1, source_target_pairs={{0,2},{1,3},{2,0},{3,1},{4,6},{5,7},{6,4},{7,5},{8,10},{9,11},{10,... | collective-permute-start | bytes 61448 | tf_op jit(solution)/shard_map/ppermute | solution.py:221
  29.3 4.1 %collective-permute-start.13 = (f32[5,8,128]{2,1,0:T(8,128)S(1)}, f32[5,8,128]{2,1,0:T(8,128)S(1)}, u32[]{:S(2)}, u32[]{:S(2)}) collective-permute-start(f32[5,8,128]{2,1,0:T(8,128)S(1)} %add_add_fusion.own_ref), channel_id=1, source_target_pairs={{0,10},{1,11},{2,8},{3,9},{4,14},{5,15},{6,12},{7,13},{8,2},{9,3},... | collective-permute-start | bytes 61448 | tf_op jit(solution)/shard_map/ppermute | solution.py:221
  29.9 4.1 %collective-permute-start.14 = (f32[5,8,128]{2,1,0:T(8,128)S(1)}, f32[5,8,128]{2,1,0:T(8,128)S(1)}, u32[]{:S(2)}, u32[]{:S(2)}) collective-permute-start(f32[5,8,128]{2,1,0:T(8,128)S(1)} %add_add_fusion.own_ref), channel_id=1, source_target_pairs={{0,18},{1,19},{2,16},{3,17},{4,22},{5,23},{6,20},{7,21},{8,26},{9,... | collective-permute-start | bytes 61448 | tf_op jit(solution)/shard_map/ppermute | solution.py:221
  31.6 5.0 %collective-permute-start.15 = (f32[5,8,128]{2,1,0:T(8,128)S(1)}, f32[5,8,128]{2,1,0:T(8,128)S(1)}, u32[]{:S(2)}, u32[]{:S(2)}) collective-permute-start(f32[5,8,128]{2,1,0:T(8,128)S(1)} %add_add_fusion.own_ref), channel_id=1, source_target_pairs={{0,26},{1,27},{2,24},{3,25},{4,30},{5,31},{6,28},{7,29},{8,18},{9,... | collective-permute-start | bytes 61448 | tf_op jit(solution)/shard_map/ppermute | solution.py:221
  36.6 1.6 %collective-permute-start.16 = (f32[3,5,8,128]{3,2,1,0:T(8,128)S(1)}, f32[3,5,8,128]{3,2,1,0:T(8,128)S(1)}, u32[]{:S(2)}, u32[]{:S(2)}) collective-permute-start(f32[3,5,8,128]{3,2,1,0:T(8,128)S(1)} %shard_map.54.others_ref), channel_id=1, source_target_pairs={{0,2},{1,3},{2,0},{3,1},{4,6},{5,7},{6,4},{7,5},{8,10},{9,11},{10,... | collective-permute-start | bytes 184328 | tf_op jit(solution)/shard_map/ppermute | solution.py:221

commit v4 on v3

--- a/solution.py
+++ b/solution.py
@@ -135,9 +135,9 @@
     out_ref[1] = own_ref[...]
 
 
-def stack_kernel(_, *refs):
-    *others, out_ref = refs
-    for k, r in enumerate(others):
+def stack_kernel(*refs):
+    _, _, *others, out_ref = refs
+    for k, r in enumerate(reversed(others)):
         out_ref[k] = r[...]
 
 
@@ -240,8 +240,7 @@
         f32 = jnp.float32
         params = pltpu.CompilerParams(vmem_limit_bytes=24 * 1024 * 1024)
         core = lax.axis_index("seq") % 2
-        chunks = [(i, min(i + LANES, count)) for i in range(0, count, LANES)]
-
+        chunks = [(0, count)]
         in_hbm = lambda value: pltpu.with_memory_space_constraint(value, pltpu.HBM)
         shape = pltpu.VMEM((n_expert, half + 2, rows, LANES), f32)
         logits, mine, theirs, w_in = pl.pallas_call(
@@ -311,10 +310,10 @@
         partial = partial + other_core(partial)
         first, second = partial[:half], partial[half:]
         own = pick(core, second, first) + sum(plane(pick(core, first, second)))
-        arrived = {k: along_expert(own, k) for k in order}
+        arrived = [along_expert(own, k) for k in order]
         own_near = other_core(own)
         shape = pltpu.VMEM((n_expert - 1, half, rows, LANES), f32)
-        others = local(stack_kernel, shape, own_near, *[arrived[k] for k in range(1, n_expert)])
+        others = local(stack_kernel, shape, combine, own_near, *arrived)
 
         def mix(near, own, others, *out):
             return pl.pallas_call(

time: 39.4 us -> 38.2 us (0.970)
  waiting for transfers between devices: 12.3 us -> 11.4 us
    ppermute x17, waiting for transfers between devices: 12.3 us -> 11.4 us  [permute(): return lax.ppermute(value, AXES, pairs)]
  transfers between devices with their start and end apart: 17 -> 17, of which waited for: 10 -> 11; matrix products, arithmetic and copies ran while one was open for 0% -> 0% of each run, Pallas kernels for 11% -> 11%
where the time goes in v4:
time: 38.2 us; the launch traced here: 38 us
  starting transfers between devices  17.6 us (46%)
  waiting for transfers between devices  11.4 us (30%)
  Pallas kernels  8.91 us (23%)
    ppermute x17, starting transfers between devices, permute(): return lax.ppermute(value, AXES, pairs)  17.6 us
    ppermute x17, waiting for transfers between devices, permute(): return lax.ppermute(value, AXES, pairs)  11.4 us
    pallas_call x1, Pallas kernels, body(): pl.pallas_call(functools.partial(dispatch_kernel, chunks), out_shape=(plt...  2.65 us
    pallas_call x2, Pallas kernels, mix(): pl.pallas_call(functools.partial(mix_kernel, near), out_shape=jax.ShapeDt...  2.08 us
    pallas_call x1, Pallas kernels, body(): pl.pallas_call(split_out_kernel, out_shape=(part, part, flag), in_specs=[...  2 us
    pallas_call x4, Pallas kernels, local(): pl.pallas_call(kernel, out_shape=out, in_specs=[VMEM] * len(args), out_sp...  1.05 us
    pallas_call x1, Pallas kernels, body(): pl.pallas_call(split_in_kernel, out_shape=(part, part, flag), in_specs=[V...  0.89 us
  transfers between devices with their start and end apart: 17, of which 11 were waited for; matrix products, arithmetic and copies ran while one was open for 0% of the time, Pallas kernels for 11%

profile of v4, /device:TPU:0, one launch (start us, length us, event | category | flops | bytes accessed | tf_op | source)
XLA Modules:
  0.0 38.0 jit_solution(105870074595443772)
XLA Ops:
  0.0 2.7 %shard_map.46 = (f32[32,224]{1,0:T(8,128)S(1)}, f32[4,7,8,128]{3,2,1,0:T(8,128)S(1)}, f32[4,7,8,128]{3,2,1,0:T(8,128)S(1)}, f32[2,320,1280]{2,1,0:T(8,128)S(1)}) custom-call(f32[224,1280]{1,0:T(8,128)} %tokens_hbm.1, f32[32,1280]{1,0:T(8,128)} %bitcast.1, f32[2,320,1280]{2,1,0:T(8,128)} %w_in_hbm.1), custom_call_target="tpu_custom_call" | custom-call | tf_op jit(solution)/shard_map/pallas_call | solution.py:246
  3.2 1.0 %collective-permute-done.theirs_ref = f32[4,7,8,128]{3,2,1,0:T(8,128)S(1)} collective-permute-done((f32[4,7,8,128]{3,2,1,0:T(8,128)S(1)}, f32[4,7,8,128]{3,2,1,0:T(8,128)S(1)}, u32[]{:S(2)}, u32[]{:S(2)}) %collective-permute-start) | collective-permute-done | bytes 114720 | tf_op jit(solution)/shard_map/ppermute | solution.py:221
  4.2 4.8 %collective-permute-start.1 = (f32[7,8,128]{2,1,0:T(8,128)S(1)}, f32[7,8,128]{2,1,0:T(8,128)S(1)}, u32[]{:S(2)}, u32[]{:S(2)}) collective-permute-start(f32[7,8,128]{2,1,0:T(8,128)S(1)} %get-tuple-element.23), channel_id=1, source_target_pairs={{0,26},{1,27},{2,24},{3,25},{4,30},{5,31},{6,28},{7,29},{8,18},{9,... | collective-permute-start | bytes 86024 | tf_op jit(solution)/shard_map/ppermute | solution.py:221
  9.0 0.6 %collective-permute-start.3 = (f32[7,8,128]{2,1,0:T(8,128)S(1)}, f32[7,8,128]{2,1,0:T(8,128)S(1)}, u32[]{:S(2)}, u32[]{:S(2)}) collective-permute-start(f32[7,8,128]{2,1,0:T(8,128)S(1)} %get-tuple-element.25), channel_id=1, source_target_pairs={{0,10},{1,11},{2,8},{3,9},{4,14},{5,15},{6,12},{7,13},{8,2},{9,3},... | collective-permute-start | bytes 86024 | tf_op jit(solution)/shard_map/ppermute | solution.py:221
  9.6 2.0 %shard_map.49 = (bf16[640,1280]{1,0:T(8,128)(2,1)S(1)}, bf16[640,1280]{1,0:T(8,128)(2,1)S(1)}, f32[8,128]{1,0:T(8,128)S(1)}) custom-call(f32[7,8,128]{2,1,0:T(8,128)S(1)} %get-tuple-element.22._.own_ref, f32[2,320,1280]{2,1,0:T(8,128)} %w_hbm.1), custom_call_target="tpu_custom_call" | custom-call | flops 6553600 | bytes 6553600 | tf_op jit(solution)/shard_map/pallas_call | solution.py:286
  11.6 1.6 %collective-permute-done.2.refs_1_ = f32[7,8,128]{2,1,0:T(8,128)S(1)} collective-permute-done((f32[7,8,128]{2,1,0:T(8,128)S(1)}, f32[7,8,128]{2,1,0:T(8,128)S(1)}, u32[]{:S(2)}, u32[]{:S(2)}) %collective-permute-start.2) | collective-permute-done | bytes 28704 | tf_op jit(solution)/shard_map/ppermute | solution.py:221
  13.2 1.5 %collective-permute-start.4 = (f32[7,8,128]{2,1,0:T(8,128)S(1)}, f32[7,8,128]{2,1,0:T(8,128)S(1)}, u32[]{:S(2)}, u32[]{:S(2)}) collective-permute-start(f32[7,8,128]{2,1,0:T(8,128)S(1)} %shard_map.50._.own_ref), channel_id=1, source_target_pairs={{0,3},{1,2},{2,1},{3,0},{4,7},{5,6},{6,5},{7,4},{8,11},{9,10},{10,... | collective-permute-start | bytes 86024 | tf_op jit(solution)/shard_map/ppermute | solution.py:221
  14.7 1.3 %collective-permute-start.5 = (f32[7,8,128]{2,1,0:T(8,128)S(1)}, f32[7,8,128]{2,1,0:T(8,128)S(1)}, u32[]{:S(2)}, u32[]{:S(2)}) collective-permute-start(f32[7,8,128]{2,1,0:T(8,128)S(1)} %shard_map.50._.own_ref), channel_id=1, source_target_pairs={{0,6},{1,7},{2,4},{3,5},{4,2},{5,3},{6,0},{7,1},{8,14},{9,15},{10,... | collective-permute-start | bytes 86024 | tf_op jit(solution)/shard_map/ppermute | solution.py:221
  16.4 0.9 %shard_map.51 = (bf16[1280,640]{1,0:T(8,128)(2,1)S(1)}, bf16[1280,640]{1,0:T(8,128)(2,1)S(1)}, f32[8,128]{1,0:T(8,128)S(1)}) custom-call(f32[7,8,128]{2,1,0:T(8,128)S(1)} %shard_map.50._.own_ref, f32[2,320,1280]{2,1,0:T(8,128)S(1)} %get-tuple-element.27.w_ref), custom_call_target="tpu_custom_call" | custom-call | flops 6553600 | bytes 6553600 | tf_op jit(solution)/shard_map/pallas_call | solution.py:298
  17.3 0.7 %collective-permute-done.5.refs_1_ = f32[7,8,128]{2,1,0:T(8,128)S(1)} collective-permute-done((f32[7,8,128]{2,1,0:T(8,128)S(1)}, f32[7,8,128]{2,1,0:T(8,128)S(1)}, u32[]{:S(2)}, u32[]{:S(2)}) %collective-permute-start.5) | collective-permute-done | bytes 28704 | tf_op jit(solution)/shard_map/ppermute | solution.py:221
  18.0 2.2 %collective-permute-done.6.refs_2_ = f32[7,8,128]{2,1,0:T(8,128)S(1)} collective-permute-done((f32[7,8,128]{2,1,0:T(8,128)S(1)}, f32[7,8,128]{2,1,0:T(8,128)S(1)}, u32[]{:S(2)}, u32[]{:S(2)}) %collective-permute-start.6) | collective-permute-done | bytes 28704 | tf_op jit(solution)/shard_map/ppermute | solution.py:221
  20.6 0.9 %collective-permute-done.7.got_ref = f32[2,7,8,128]{3,2,1,0:T(8,128)S(1)} collective-permute-done((f32[2,7,8,128]{3,2,1,0:T(8,128)S(1)}, f32[2,7,8,128]{3,2,1,0:T(8,128)S(1)}, u32[]{:S(2)}, u32[]{:S(2)}) %collective-permute-start.7) | collective-permute-done | bytes 57376 | tf_op jit(solution)/shard_map/ppermute | solution.py:221
  21.5 1.0 %shard_map.53 = f32[10,8,128]{2,1,0:T(8,128)S(1)} custom-call(f32[2,7,8,128]{3,2,1,0:T(8,128)S(1)} %shard_map.52.sent_ref, f32[2,7,8,128]{3,2,1,0:T(8,128)S(1)} %collective-permute-done.7.got_ref, bf16[1280,640]{1,0:T(8,128)(2,1)S(1)} %get-tuple-element.29.in_high_ref, bf16[1280,640]{1,0:T(8,128)(2,1)S(1)} %get-tuple-element.30.in_low_ref, ...), custom_call_target="tpu_custom_call" | custom-call | tf_op jit(solution)/shard_map/pallas_call | solution.py:280
  22.9 0.9 %collective-permute-done.8 = f32[10,8,128]{2,1,0:T(8,128)S(1)} collective-permute-done((f32[10,8,128]{2,1,0:T(8,128)S(1)}, f32[10,8,128]{2,1,0:T(8,128)S(1)}, u32[]{:S(2)}, u32[]{:S(2)}) %collective-permute-start.8) | collective-permute-done | bytes 40992 | tf_op jit(solution)/shard_map/ppermute | solution.py:221
  23.8 0.6 %collective-permute-start.10 = (f32[5,8,128]{2,1,0:T(8,128)S(1)}, f32[5,8,128]{2,1,0:T(8,128)S(1)}, u32[]{:S(2)}, u32[]{:S(2)}) collective-permute-start(f32[5,8,128]{2,1,0:T(8,128)S(1)} %slice_select_fusion), channel_id=1, source_target_pairs={{0,6},{1,7},{2,4},{3,5},{4,2},{5,3},{6,0},{7,1},{8,14},{9,15},{10,... | collective-permute-start | bytes 61448 | tf_op jit(solution)/shard_map/ppermute | solution.py:221
  24.3 1.2 %collective-permute-start.11 = (f32[5,8,128]{2,1,0:T(8,128)S(1)}, f32[5,8,128]{2,1,0:T(8,128)S(1)}, u32[]{:S(2)}, u32[]{:S(2)}) collective-permute-start(f32[5,8,128]{2,1,0:T(8,128)S(1)} %slice_select_fusion), channel_id=1, source_target_pairs={{0,7},{1,6},{2,5},{3,4},{4,3},{5,2},{6,1},{7,0},{8,15},{9,14},{10,... | collective-permute-start | bytes 61448 | tf_op jit(solution)/shard_map/ppermute | solution.py:221
  25.5 1.5 %collective-permute-start.9 = (f32[5,8,128]{2,1,0:T(8,128)S(1)}, f32[5,8,128]{2,1,0:T(8,128)S(1)}, u32[]{:S(2)}, u32[]{:S(2)}) collective-permute-start(f32[5,8,128]{2,1,0:T(8,128)S(1)} %slice_select_fusion), channel_id=1, source_target_pairs={{0,3},{1,2},{2,1},{3,0},{4,7},{5,6},{6,5},{7,4},{8,11},{9,10},{10,... | collective-permute-start | bytes 61448 | tf_op jit(solution)/shard_map/ppermute | solution.py:221
  27.0 1.4 %collective-permute-done.11 = f32[5,8,128]{2,1,0:T(8,128)S(1)} collective-permute-done((f32[5,8,128]{2,1,0:T(8,128)S(1)}, f32[5,8,128]{2,1,0:T(8,128)S(1)}, u32[]{:S(2)}, u32[]{:S(2)}) %collective-permute-start.11) | collective-permute-done | bytes 20512 | tf_op jit(solution)/shard_map/ppermute | solution.py:221
  29.2 1.9 %collective-permute-start.13 = (f32[5,8,128]{2,1,0:T(8,128)S(1)}, f32[5,8,128]{2,1,0:T(8,128)S(1)}, u32[]{:S(2)}, u32[]{:S(2)}) collective-permute-start(f32[5,8,128]{2,1,0:T(8,128)S(1)} %add_add_fusion.own_ref), channel_id=1, source_target_pairs={{0,26},{1,27},{2,24},{3,25},{4,30},{5,31},{6,28},{7,29},{8,18},{9,... | collective-permute-start | bytes 61448 | tf_op jit(solution)/shard_map/ppermute | solution.py:221
  31.2 2.1 %collective-permute-start.15 = (f32[5,8,128]{2,1,0:T(8,128)S(1)}, f32[5,8,128]{2,1,0:T(8,128)S(1)}, u32[]{:S(2)}, u32[]{:S(2)}) collective-permute-start(f32[5,8,128]{2,1,0:T(8,128)S(1)} %add_add_fusion.own_ref), channel_id=1, source_target_pairs={{0,10},{1,11},{2,8},{3,9},{4,14},{5,15},{6,12},{7,13},{8,2},{9,3},... | collective-permute-start | bytes 61448 | tf_op jit(solution)/shard_map/ppermute | solution.py:221
  33.5 0.7 %collective-permute-done.13.refs_2_ = f32[5,8,128]{2,1,0:T(8,128)S(1)} collective-permute-done((f32[5,8,128]{2,1,0:T(8,128)S(1)}, f32[5,8,128]{2,1,0:T(8,128)S(1)}, u32[]{:S(2)}, u32[]{:S(2)}) %collective-permute-start.13) | collective-permute-done | bytes 20512 | tf_op jit(solution)/shard_map/ppermute | solution.py:221
  34.2 1.5 %collective-permute-done.14.refs_3_ = f32[5,8,128]{2,1,0:T(8,128)S(1)} collective-permute-done((f32[5,8,128]{2,1,0:T(8,128)S(1)}, f32[5,8,128]{2,1,0:T(8,128)S(1)}, u32[]{:S(2)}, u32[]{:S(2)}) %collective-permute-start.14) | collective-permute-done | bytes 20512 | tf_op jit(solution)/shard_map/ppermute | solution.py:221
  35.9 1.0 %shard_map.55.refs_0_ = f32[224,1280]{1,0:T(8,128)} custom-call(bf16[224,96]{1,0:T(8,128)(2,1)S(1)} %shard_map.47.refs_0_.combine_ref, f32[5,8,128]{2,1,0:T(8,128)S(1)} %collective-permute-done.12.refs_1_.own_ref, f32[3,5,8,128]{3,2,1,0:T(8,128)S(1)} %shard_map.54.others_ref), custom_call_target="tpu_custom_call" | custom-call | tf_op jit(solution)/shard_map/pallas_call | solution.py:319
  37.0 1.0 %shard_map.56 = f32[224,1280]{1,0:T(8,128)} custom-call(bf16[224,96]{1,0:T(8,128)(2,1)S(1)} %shard_map.47.refs_0_.combine_ref, f32[5,8,128]{2,1,0:T(8,128)S(1)} %add_add_fusion.own_ref, f32[3,5,8,128]{3,2,1,0:T(8,128)S(1)} %collective-permute-done.16.others_ref, f32[224,1280]{1,0:T(8,128)} %shard_map.55.refs_0_), custom_call_target="tpu_custom_call", output_to_operand_aliasing={{}: (3, {})} | custom-call | tf_op jit(solution)/shard_map/pallas_call | solution.py:319
  (24 shorter events, 3.1 us)
Async XLA Ops:
  2.7 1.5 %collective-permute-start = (f32[4,7,8,128]{3,2,1,0:T(8,128)S(1)}, f32[4,7,8,128]{3,2,1,0:T(8,128)S(1)}, u32[]{:S(2)}, u32[]{:S(2)}) collective-permute-start(f32[4,7,8,128]{3,2,1,0:T(8,128)S(1)} %get-tuple-element.21), channel_id=1, source_target_pairs={{0,2},{1,3},{2,0},{3,1},{4,6},{5,7},{6,4},{7,5},{8,10},{9,11},{10,... | collective-permute-start | bytes 344072 | tf_op jit(solution)/shard_map/ppermute | solution.py:221
  4.2 7.4 %collective-permute-start.1 = (f32[7,8,128]{2,1,0:T(8,128)S(1)}, f32[7,8,128]{2,1,0:T(8,128)S(1)}, u32[]{:S(2)}, u32[]{:S(2)}) collective-permute-start(f32[7,8,128]{2,1,0:T(8,128)S(1)} %get-tuple-element.23), channel_id=1, source_target_pairs={{0,26},{1,27},{2,24},{3,25},{4,30},{5,31},{6,28},{7,29},{8,18},{9,... | collective-permute-start | bytes 86024 | tf_op jit(solution)/shard_map/ppermute | solution.py:221
  9.0 4.2 %collective-permute-start.2 = (f32[7,8,128]{2,1,0:T(8,128)S(1)}, f32[7,8,128]{2,1,0:T(8,128)S(1)}, u32[]{:S(2)}, u32[]{:S(2)}) collective-permute-start(f32[7,8,128]{2,1,0:T(8,128)S(1)} %get-tuple-element.24), channel_id=1, source_target_pairs={{0,18},{1,19},{2,16},{3,17},{4,22},{5,23},{6,20},{7,21},{8,26},{9,... | collective-permute-start | bytes 86024 | tf_op jit(solution)/shard_map/ppermute | solution.py:221
  9.0 4.2 %collective-permute-start.3 = (f32[7,8,128]{2,1,0:T(8,128)S(1)}, f32[7,8,128]{2,1,0:T(8,128)S(1)}, u32[]{:S(2)}, u32[]{:S(2)}) collective-permute-start(f32[7,8,128]{2,1,0:T(8,128)S(1)} %get-tuple-element.25), channel_id=1, source_target_pairs={{0,10},{1,11},{2,8},{3,9},{4,14},{5,15},{6,12},{7,13},{8,2},{9,3},... | collective-permute-start | bytes 86024 | tf_op jit(solution)/shard_map/ppermute | solution.py:221
  13.2 4.1 %collective-permute-start.4 = (f32[7,8,128]{2,1,0:T(8,128)S(1)}, f32[7,8,128]{2,1,0:T(8,128)S(1)}, u32[]{:S(2)}, u32[]{:S(2)}) collective-permute-start(f32[7,8,128]{2,1,0:T(8,128)S(1)} %shard_map.50._.own_ref), channel_id=1, source_target_pairs={{0,3},{1,2},{2,1},{3,0},{4,7},{5,6},{6,5},{7,4},{8,11},{9,10},{10,... | collective-permute-start | bytes 86024 | tf_op jit(solution)/shard_map/ppermute | solution.py:221
  14.7 3.3 %collective-permute-start.5 = (f32[7,8,128]{2,1,0:T(8,128)S(1)}, f32[7,8,128]{2,1,0:T(8,128)S(1)}, u32[]{:S(2)}, u32[]{:S(2)}) collective-permute-start(f32[7,8,128]{2,1,0:T(8,128)S(1)} %shard_map.50._.own_ref), channel_id=1, source_target_pairs={{0,6},{1,7},{2,4},{3,5},{4,2},{5,3},{6,0},{7,1},{8,14},{9,15},{10,... | collective-permute-start | bytes 86024 | tf_op jit(solution)/shard_map/ppermute | solution.py:221
  16.0 4.2 %collective-permute-start.6 = (f32[7,8,128]{2,1,0:T(8,128)S(1)}, f32[7,8,128]{2,1,0:T(8,128)S(1)}, u32[]{:S(2)}, u32[]{:S(2)}) collective-permute-start(f32[7,8,128]{2,1,0:T(8,128)S(1)} %shard_map.50._.own_ref), channel_id=1, source_target_pairs={{0,7},{1,6},{2,5},{3,4},{4,3},{5,2},{6,1},{7,0},{8,15},{9,14},{10,... | collective-permute-start | bytes 86024 | tf_op jit(solution)/shard_map/ppermute | solution.py:221
  20.2 1.3 %collective-permute-start.7 = (f32[2,7,8,128]{3,2,1,0:T(8,128)S(1)}, f32[2,7,8,128]{3,2,1,0:T(8,128)S(1)}, u32[]{:S(2)}, u32[]{:S(2)}) collective-permute-start(f32[2,7,8,128]{3,2,1,0:T(8,128)S(1)} %shard_map.52.sent_ref), channel_id=1, source_target_pairs={{0,2},{1,3},{2,0},{3,1},{4,6},{5,7},{6,4},{7,5},{8,10},{9,11},{10,... | collective-permute-start | bytes 172040 | tf_op jit(solution)/shard_map/ppermute | solution.py:221
  22.5 1.2 %collective-permute-start.8 = (f32[10,8,128]{2,1,0:T(8,128)S(1)}, f32[10,8,128]{2,1,0:T(8,128)S(1)}, u32[]{:S(2)}, u32[]{:S(2)}) collective-permute-start(f32[10,8,128]{2,1,0:T(8,128)S(1)} %shard_map.53), channel_id=1, source_target_pairs={{0,2},{1,3},{2,0},{3,1},{4,6},{5,7},{6,4},{7,5},{8,10},{9,11},{10,... | collective-permute-start | bytes 122888 | tf_op jit(solution)/shard_map/ppermute | solution.py:221
  23.8 3.3 %collective-permute-start.10 = (f32[5,8,128]{2,1,0:T(8,128)S(1)}, f32[5,8,128]{2,1,0:T(8,128)S(1)}, u32[]{:S(2)}, u32[]{:S(2)}) collective-permute-start(f32[5,8,128]{2,1,0:T(8,128)S(1)} %slice_select_fusion), channel_id=1, source_target_pairs={{0,6},{1,7},{2,4},{3,5},{4,2},{5,3},{6,0},{7,1},{8,14},{9,15},{10,... | collective-permute-start | bytes 61448 | tf_op jit(solution)/shard_map/ppermute | solution.py:221
  24.3 4.1 %collective-permute-start.11 = (f32[5,8,128]{2,1,0:T(8,128)S(1)}, f32[5,8,128]{2,1,0:T(8,128)S(1)}, u32[]{:S(2)}, u32[]{:S(2)}) collective-permute-start(f32[5,8,128]{2,1,0:T(8,128)S(1)} %slice_select_fusion), channel_id=1, source_target_pairs={{0,7},{1,6},{2,5},{3,4},{4,3},{5,2},{6,1},{7,0},{8,15},{9,14},{10,... | collective-permute-start | bytes 61448 | tf_op jit(solution)/shard_map/ppermute | solution.py:221
  25.5 3.4 %collective-permute-start.9 = (f32[5,8,128]{2,1,0:T(8,128)S(1)}, f32[5,8,128]{2,1,0:T(8,128)S(1)}, u32[]{:S(2)}, u32[]{:S(2)}) collective-permute-start(f32[5,8,128]{2,1,0:T(8,128)S(1)} %slice_select_fusion), channel_id=1, source_target_pairs={{0,3},{1,2},{2,1},{3,0},{4,7},{5,6},{6,5},{7,4},{8,11},{9,10},{10,... | collective-permute-start | bytes 61448 | tf_op jit(solution)/shard_map/ppermute | solution.py:221
  29.0 4.5 %collective-permute-start.12 = (f32[5,8,128]{2,1,0:T(8,128)S(1)}, f32[5,8,128]{2,1,0:T(8,128)S(1)}, u32[]{:S(2)}, u32[]{:S(2)}) collective-permute-start(f32[5,8,128]{2,1,0:T(8,128)S(1)} %add_add_fusion.own_ref), channel_id=1, source_target_pairs={{0,2},{1,3},{2,0},{3,1},{4,6},{5,7},{6,4},{7,5},{8,10},{9,11},{10,... | collective-permute-start | bytes 61448 | tf_op jit(solution)/shard_map/ppermute | solution.py:221
  29.2 5.0 %collective-permute-start.13 = (f32[5,8,128]{2,1,0:T(8,128)S(1)}, f32[5,8,128]{2,1,0:T(8,128)S(1)}, u32[]{:S(2)}, u32[]{:S(2)}) collective-permute-start(f32[5,8,128]{2,1,0:T(8,128)S(1)} %add_add_fusion.own_ref), channel_id=1, source_target_pairs={{0,26},{1,27},{2,24},{3,25},{4,30},{5,31},{6,28},{7,29},{8,18},{9,... | collective-permute-start | bytes 61448 | tf_op jit(solution)/shard_map/ppermute | solution.py:221
  31.1 4.6 %collective-permute-start.14 = (f32[5,8,128]{2,1,0:T(8,128)S(1)}, f32[5,8,128]{2,1,0:T(8,128)S(1)}, u32[]{:S(2)}, u32[]{:S(2)}) collective-permute-start(f32[5,8,128]{2,1,0:T(8,128)S(1)} %add_add_fusion.own_ref), channel_id=1, source_target_pairs={{0,18},{1,19},{2,16},{3,17},{4,22},{5,23},{6,20},{7,21},{8,26},{9,... | collective-permute-start | bytes 61448 | tf_op jit(solution)/shard_map/ppermute | solution.py:221
  31.2 4.5 %collective-permute-start.15 = (f32[5,8,128]{2,1,0:T(8,128)S(1)}, f32[5,8,128]{2,1,0:T(8,128)S(1)}, u32[]{:S(2)}, u32[]{:S(2)}) collective-permute-start(f32[5,8,128]{2,1,0:T(8,128)S(1)} %add_add_fusion.own_ref), channel_id=1, source_target_pairs={{0,10},{1,11},{2,8},{3,9},{4,14},{5,15},{6,12},{7,13},{8,2},{9,3},... | collective-permute-start | bytes 61448 | tf_op jit(solution)/shard_map/ppermute | solution.py:221
  35.7 1.3 %collective-permute-start.16 = (f32[3,5,8,128]{3,2,1,0:T(8,128)S(1)}, f32[3,5,8,128]{3,2,1,0:T(8,128)S(1)}, u32[]{:S(2)}, u32[]{:S(2)}) collective-permute-start(f32[3,5,8,128]{3,2,1,0:T(8,128)S(1)} %shard_map.54.others_ref), channel_id=1, source_target_pairs={{0,2},{1,3},{2,0},{3,1},{4,6},{5,7},{6,4},{7,5},{8,10},{9,11},{10,... | collective-permute-start | bytes 184328 | tf_op jit(solution)/shard_map/ppermute | solution.py:221

commit v5 on v4

--- a/solution.py
+++ b/solution.py
@@ -136,7 +136,7 @@
 
 
 def stack_kernel(*refs):
-    _, _, *others, out_ref = refs
+    _, *others, _, out_ref = refs
     for k, r in enumerate(reversed(others)):
         out_ref[k] = r[...]
 
@@ -194,13 +194,13 @@
     slots = jnp.concatenate([high, high, low], axis=0)
     side = core if near else 1 - core
     columns = pl.ds(pl.multiple_of(side * (half * LANES), LANES), half * LANES)
-    parts = sems.shape[0]
-    count = combine_ref.shape[0] // parts
+    count = combine_ref.shape[0]
+    step = pl.cdiv(count, 16 * sems.shape[0]) * 16
     copies = []
-    for i in range(parts):
-        own = slice(i * count, (i + 1) * count)
-        out_ref[own] = mm(combine_ref[own], slots)
-        place = pl.ds(i * count, count)
+    for i, start in enumerate(range(0, count, step)):
+        size = min(step, count - start)
+        out_ref[start:start + size] = mm(combine_ref[start:start + size], slots)
+        place = pl.ds(start, size)
         copies.append(pltpu.make_async_copy(out_ref.at[place], out_hbm.at[place, columns], sems.at[i]))
         copies[i].start()
     for copy in copies:
@@ -229,7 +229,7 @@
     def plane(value):
         return [
             permute(value, lambda e, x, c, f, dx=dx, df=df: (e, (x + dx) % n_x, 1 - c, (f + df) % n_fsdp))
-            for dx in range(n_x) for df in range(n_fsdp) if dx or df
+            for dx in range(n_x)[::-1] for df in range(n_fsdp)[::-1] if dx or df
         ]
 
     def body(tokens, slot_params, w_in, w_out):
@@ -313,7 +313,7 @@
         arrived = [along_expert(own, k) for k in order]
         own_near = other_core(own)
         shape = pltpu.VMEM((n_expert - 1, half, rows, LANES), f32)
-        others = local(stack_kernel, shape, combine, own_near, *arrived)
+        others = local(stack_kernel, shape, combine, *arrived, own_near)
 
         def mix(near, own, others, *out):
             return pl.pallas_call(
@@ -324,7 +324,7 @@
                 scratch_shapes=[
                     pltpu.VMEM((slots, half * LANES), f32),
                     pltpu.VMEM((count, half * LANES), f32),
-                    pltpu.SemaphoreType.DMA((2 if count % 32 == 0 else 1,)),
+                    pltpu.SemaphoreType.DMA((4,)),
                 ],
                 input_output_aliases={3: 0} if out else {},
                 compiler_params=params,

time: 38.2 us -> 37.6 us (0.984)
  waiting for transfers between devices: 11.4 us -> 10.7 us
    ppermute x17, waiting for transfers between devices: 11.4 us -> 10.7 us  [permute(): return lax.ppermute(value, AXES, pairs)]
where the time goes in v5:
time: 37.6 us; the launch traced here: 37.5 us
  starting transfers between devices  17.8 us (47%)
  waiting for transfers between devices  10.7 us (28%)
  Pallas kernels  8.86 us (24%)
    ppermute x17, starting transfers between devices, permute(): return lax.ppermute(value, AXES, pairs)  17.8 us
    ppermute x17, waiting for transfers between devices, permute(): return lax.ppermute(value, AXES, pairs)  10.7 us
    pallas_call x1, Pallas kernels, body(): pl.pallas_call(functools.partial(dispatch_kernel, chunks), out_shape=(plt...  2.65 us
    pallas_call x2, Pallas kernels, mix(): pl.pallas_call(functools.partial(mix_kernel, near), out_shape=jax.ShapeDt...  2.03 us
    pallas_call x1, Pallas kernels, body(): pl.pallas_call(split_out_kernel, out_shape=(part, part, flag), in_specs=[...  2 us
    pallas_call x4, Pallas kernels, local(): pl.pallas_call(kernel, out_shape=out, in_specs=[VMEM] * len(args), out_sp...  1.05 us
    pallas_call x1, Pallas kernels, body(): pl.pallas_call(split_in_kernel, out_shape=(part, part, flag), in_specs=[V...  0.89 us
  transfers between devices with their start and end apart: 17, of which 11 were waited for; matrix products, arithmetic and copies ran while one was open for 0% of the time, Pallas kernels for 11%

profile of v5, /device:TPU:0, one launch (start us, length us, event | category | flops | bytes accessed | tf_op | source)
XLA Modules:
  0.0 37.5 jit_solution(6581861167906441085)
XLA Ops:
  0.0 2.7 %shard_map.46 = (f32[32,224]{1,0:T(8,128)S(1)}, f32[4,7,8,128]{3,2,1,0:T(8,128)S(1)}, f32[4,7,8,128]{3,2,1,0:T(8,128)S(1)}, f32[2,320,1280]{2,1,0:T(8,128)S(1)}) custom-call(f32[224,1280]{1,0:T(8,128)} %tokens_hbm.1, f32[32,1280]{1,0:T(8,128)} %bitcast.1, f32[2,320,1280]{2,1,0:T(8,128)} %w_in_hbm.1), custom_call_target="tpu_custom_call" | custom-call | tf_op jit(solution)/shard_map/pallas_call | solution.py:246
  2.7 0.5 %collective-permute-start = (f32[4,7,8,128]{3,2,1,0:T(8,128)S(1)}, f32[4,7,8,128]{3,2,1,0:T(8,128)S(1)}, u32[]{:S(2)}, u32[]{:S(2)}) collective-permute-start(f32[4,7,8,128]{3,2,1,0:T(8,128)S(1)} %get-tuple-element.21), channel_id=1, source_target_pairs={{0,2},{1,3},{2,0},{3,1},{4,6},{5,7},{6,4},{7,5},{8,10},{9,11},{10,... | collective-permute-start | bytes 344072 | tf_op jit(solution)/shard_map/ppermute | solution.py:221
  3.2 1.0 %collective-permute-done.theirs_ref = f32[4,7,8,128]{3,2,1,0:T(8,128)S(1)} collective-permute-done((f32[4,7,8,128]{3,2,1,0:T(8,128)S(1)}, f32[4,7,8,128]{3,2,1,0:T(8,128)S(1)}, u32[]{:S(2)}, u32[]{:S(2)}) %collective-permute-start) | collective-permute-done | bytes 114720 | tf_op jit(solution)/shard_map/ppermute | solution.py:221
  4.2 4.8 %collective-permute-start.1 = (f32[7,8,128]{2,1,0:T(8,128)S(1)}, f32[7,8,128]{2,1,0:T(8,128)S(1)}, u32[]{:S(2)}, u32[]{:S(2)}) collective-permute-start(f32[7,8,128]{2,1,0:T(8,128)S(1)} %get-tuple-element.23), channel_id=1, source_target_pairs={{0,26},{1,27},{2,24},{3,25},{4,30},{5,31},{6,28},{7,29},{8,18},{9,... | collective-permute-start | bytes 86024 | tf_op jit(solution)/shard_map/ppermute | solution.py:221
  9.0 0.6 %collective-permute-start.3 = (f32[7,8,128]{2,1,0:T(8,128)S(1)}, f32[7,8,128]{2,1,0:T(8,128)S(1)}, u32[]{:S(2)}, u32[]{:S(2)}) collective-permute-start(f32[7,8,128]{2,1,0:T(8,128)S(1)} %get-tuple-element.25), channel_id=1, source_target_pairs={{0,10},{1,11},{2,8},{3,9},{4,14},{5,15},{6,12},{7,13},{8,2},{9,3},... | collective-permute-start | bytes 86024 | tf_op jit(solution)/shard_map/ppermute | solution.py:221
  9.6 2.0 %shard_map.49 = (bf16[640,1280]{1,0:T(8,128)(2,1)S(1)}, bf16[640,1280]{1,0:T(8,128)(2,1)S(1)}, f32[8,128]{1,0:T(8,128)S(1)}) custom-call(f32[7,8,128]{2,1,0:T(8,128)S(1)} %get-tuple-element.22._.own_ref, f32[2,320,1280]{2,1,0:T(8,128)} %w_hbm.1), custom_call_target="tpu_custom_call" | custom-call | flops 6553600 | bytes 6553600 | tf_op jit(solution)/shard_map/pallas_call | solution.py:286
  11.6 1.6 %collective-permute-done.2.refs_1_ = f32[7,8,128]{2,1,0:T(8,128)S(1)} collective-permute-done((f32[7,8,128]{2,1,0:T(8,128)S(1)}, f32[7,8,128]{2,1,0:T(8,128)S(1)}, u32[]{:S(2)}, u32[]{:S(2)}) %collective-permute-start.2) | collective-permute-done | bytes 28704 | tf_op jit(solution)/shard_map/ppermute | solution.py:221
  13.2 2.4 %collective-permute-start.4 = (f32[7,8,128]{2,1,0:T(8,128)S(1)}, f32[7,8,128]{2,1,0:T(8,128)S(1)}, u32[]{:S(2)}, u32[]{:S(2)}) collective-permute-start(f32[7,8,128]{2,1,0:T(8,128)S(1)} %shard_map.50._.own_ref), channel_id=1, source_target_pairs={{0,7},{1,6},{2,5},{3,4},{4,3},{5,2},{6,1},{7,0},{8,15},{9,14},{10,... | collective-permute-start | bytes 86024 | tf_op jit(solution)/shard_map/ppermute | solution.py:221
  16.0 0.5 %collective-permute-start.6 = (f32[7,8,128]{2,1,0:T(8,128)S(1)}, f32[7,8,128]{2,1,0:T(8,128)S(1)}, u32[]{:S(2)}, u32[]{:S(2)}) collective-permute-start(f32[7,8,128]{2,1,0:T(8,128)S(1)} %shard_map.50._.own_ref), channel_id=1, source_target_pairs={{0,3},{1,2},{2,1},{3,0},{4,7},{5,6},{6,5},{7,4},{8,11},{9,10},{10,... | collective-permute-start | bytes 86024 | tf_op jit(solution)/shard_map/ppermute | solution.py:221
  16.4 0.9 %shard_map.51 = (bf16[1280,640]{1,0:T(8,128)(2,1)S(1)}, bf16[1280,640]{1,0:T(8,128)(2,1)S(1)}, f32[8,128]{1,0:T(8,128)S(1)}) custom-call(f32[7,8,128]{2,1,0:T(8,128)S(1)} %shard_map.50._.own_ref, f32[2,320,1280]{2,1,0:T(8,128)S(1)} %get-tuple-element.27.w_ref), custom_call_target="tpu_custom_call" | custom-call | flops 6553600 | bytes 6553600 | tf_op jit(solution)/shard_map/pallas_call | solution.py:298
  17.5 1.5 %collective-permute-done.5.refs_1_ = f32[7,8,128]{2,1,0:T(8,128)S(1)} collective-permute-done((f32[7,8,128]{2,1,0:T(8,128)S(1)}, f32[7,8,128]{2,1,0:T(8,128)S(1)}, u32[]{:S(2)}, u32[]{:S(2)}) %collective-permute-start.5) | collective-permute-done | bytes 28704 | tf_op jit(solution)/shard_map/ppermute | solution.py:221
  19.7 0.9 %collective-permute-done.7.got_ref = f32[2,7,8,128]{3,2,1,0:T(8,128)S(1)} collective-permute-done((f32[2,7,8,128]{3,2,1,0:T(8,128)S(1)}, f32[2,7,8,128]{3,2,1,0:T(8,128)S(1)}, u32[]{:S(2)}, u32[]{:S(2)}) %collective-permute-start.7) | collective-permute-done | bytes 57376 | tf_op jit(solution)/shard_map/ppermute | solution.py:221
  20.6 1.0 %shard_map.53 = f32[10,8,128]{2,1,0:T(8,128)S(1)} custom-call(f32[2,7,8,128]{3,2,1,0:T(8,128)S(1)} %shard_map.52.sent_ref, f32[2,7,8,128]{3,2,1,0:T(8,128)S(1)} %collective-permute-done.7.got_ref, bf16[1280,640]{1,0:T(8,128)(2,1)S(1)} %get-tuple-element.29.in_high_ref, bf16[1280,640]{1,0:T(8,128)(2,1)S(1)} %get-tuple-element.30.in_low_ref, ...), custom_call_target="tpu_custom_call" | custom-call | tf_op jit(solution)/shard_map/pallas_call | solution.py:280
  22.0 0.9 %collective-permute-done.8 = f32[10,8,128]{2,1,0:T(8,128)S(1)} collective-permute-done((f32[10,8,128]{2,1,0:T(8,128)S(1)}, f32[10,8,128]{2,1,0:T(8,128)S(1)}, u32[]{:S(2)}, u32[]{:S(2)}) %collective-permute-start.8) | collective-permute-done | bytes 40992 | tf_op jit(solution)/shard_map/ppermute | solution.py:221
  22.8 1.5 %collective-permute-start.10 = (f32[5,8,128]{2,1,0:T(8,128)S(1)}, f32[5,8,128]{2,1,0:T(8,128)S(1)}, u32[]{:S(2)}, u32[]{:S(2)}) collective-permute-start(f32[5,8,128]{2,1,0:T(8,128)S(1)} %slice_select_fusion), channel_id=1, source_target_pairs={{0,6},{1,7},{2,4},{3,5},{4,2},{5,3},{6,0},{7,1},{8,14},{9,15},{10,... | collective-permute-start | bytes 61448 | tf_op jit(solution)/shard_map/ppermute | solution.py:221
  24.8 1.3 %collective-permute-start.9 = (f32[5,8,128]{2,1,0:T(8,128)S(1)}, f32[5,8,128]{2,1,0:T(8,128)S(1)}, u32[]{:S(2)}, u32[]{:S(2)}) collective-permute-start(f32[5,8,128]{2,1,0:T(8,128)S(1)} %slice_select_fusion), channel_id=1, source_target_pairs={{0,7},{1,6},{2,5},{3,4},{4,3},{5,2},{6,1},{7,0},{8,15},{9,14},{10,... | collective-permute-start | bytes 61448 | tf_op jit(solution)/shard_map/ppermute | solution.py:221
  26.1 1.4 %collective-permute-done.11 = f32[5,8,128]{2,1,0:T(8,128)S(1)} collective-permute-done((f32[5,8,128]{2,1,0:T(8,128)S(1)}, f32[5,8,128]{2,1,0:T(8,128)S(1)}, u32[]{:S(2)}, u32[]{:S(2)}) %collective-permute-start.11) | collective-permute-done | bytes 20512 | tf_op jit(solution)/shard_map/ppermute | solution.py:221
  27.6 1.3 %collective-permute-done.9 = f32[5,8,128]{2,1,0:T(8,128)S(1)} collective-permute-done((f32[5,8,128]{2,1,0:T(8,128)S(1)}, f32[5,8,128]{2,1,0:T(8,128)S(1)}, u32[]{:S(2)}, u32[]{:S(2)}) %collective-permute-start.9) | collective-permute-done | bytes 20512 | tf_op jit(solution)/shard_map/ppermute | solution.py:221
  28.9 1.8 %collective-permute-start.12 = (f32[5,8,128]{2,1,0:T(8,128)S(1)}, f32[5,8,128]{2,1,0:T(8,128)S(1)}, u32[]{:S(2)}, u32[]{:S(2)}) collective-permute-start(f32[5,8,128]{2,1,0:T(8,128)S(1)} %add_add_fusion.own_ref), channel_id=1, source_target_pairs={{0,26},{1,27},{2,24},{3,25},{4,30},{5,31},{6,28},{7,29},{8,18},{9,... | collective-permute-start | bytes 61448 | tf_op jit(solution)/shard_map/ppermute | solution.py:221
  30.8 2.1 %collective-permute-start.14 = (f32[5,8,128]{2,1,0:T(8,128)S(1)}, f32[5,8,128]{2,1,0:T(8,128)S(1)}, u32[]{:S(2)}, u32[]{:S(2)}) collective-permute-start(f32[5,8,128]{2,1,0:T(8,128)S(1)} %add_add_fusion.own_ref), channel_id=1, source_target_pairs={{0,10},{1,11},{2,8},{3,9},{4,14},{5,15},{6,12},{7,13},{8,2},{9,3},... | collective-permute-start | bytes 61448 | tf_op jit(solution)/shard_map/ppermute | solution.py:221
  33.4 0.6 %collective-permute-done.12.refs_1_ = f32[5,8,128]{2,1,0:T(8,128)S(1)} collective-permute-done((f32[5,8,128]{2,1,0:T(8,128)S(1)}, f32[5,8,128]{2,1,0:T(8,128)S(1)}, u32[]{:S(2)}, u32[]{:S(2)}) %collective-permute-start.12) | collective-permute-done | bytes 20512 | tf_op jit(solution)/shard_map/ppermute | solution.py:221
  34.0 1.0 %collective-permute-done.13.refs_2_ = f32[5,8,128]{2,1,0:T(8,128)S(1)} collective-permute-done((f32[5,8,128]{2,1,0:T(8,128)S(1)}, f32[5,8,128]{2,1,0:T(8,128)S(1)}, u32[]{:S(2)}, u32[]{:S(2)}) %collective-permute-start.13) | collective-permute-done | bytes 20512 | tf_op jit(solution)/shard_map/ppermute | solution.py:221
  35.4 1.0 %shard_map.55.refs_0_ = f32[224,1280]{1,0:T(8,128)} custom-call(bf16[224,96]{1,0:T(8,128)(2,1)S(1)} %shard_map.47.refs_0_.combine_ref, f32[5,8,128]{2,1,0:T(8,128)S(1)} %collective-permute-done.15.refs_4_.own_ref, f32[3,5,8,128]{3,2,1,0:T(8,128)S(1)} %shard_map.54.others_ref), custom_call_target="tpu_custom_call" | custom-call | tf_op jit(solution)/shard_map/pallas_call | solution.py:319
  36.5 1.0 %shard_map.56 = f32[224,1280]{1,0:T(8,128)} custom-call(bf16[224,96]{1,0:T(8,128)(2,1)S(1)} %shard_map.47.refs_0_.combine_ref, f32[5,8,128]{2,1,0:T(8,128)S(1)} %add_add_fusion.own_ref, f32[3,5,8,128]{3,2,1,0:T(8,128)S(1)} %collective-permute-done.16.others_ref, f32[224,1280]{1,0:T(8,128)} %shard_map.55.refs_0_), custom_call_target="tpu_custom_call", output_to_operand_aliasing={{}: (3, {})} | custom-call | tf_op jit(solution)/shard_map/pallas_call | solution.py:319
  (24 shorter events, 3.1 us)
Async XLA Ops:
  2.7 1.5 %collective-permute-start = (f32[4,7,8,128]{3,2,1,0:T(8,128)S(1)}, f32[4,7,8,128]{3,2,1,0:T(8,128)S(1)}, u32[]{:S(2)}, u32[]{:S(2)}) collective-permute-start(f32[4,7,8,128]{3,2,1,0:T(8,128)S(1)} %get-tuple-element.21), channel_id=1, source_target_pairs={{0,2},{1,3},{2,0},{3,1},{4,6},{5,7},{6,4},{7,5},{8,10},{9,11},{10,... | collective-permute-start | bytes 344072 | tf_op jit(solution)/shard_map/ppermute | solution.py:221
  4.2 7.4 %collective-permute-start.1 = (f32[7,8,128]{2,1,0:T(8,128)S(1)}, f32[7,8,128]{2,1,0:T(8,128)S(1)}, u32[]{:S(2)}, u32[]{:S(2)}) collective-permute-start(f32[7,8,128]{2,1,0:T(8,128)S(1)} %get-tuple-element.23), channel_id=1, source_target_pairs={{0,26},{1,27},{2,24},{3,25},{4,30},{5,31},{6,28},{7,29},{8,18},{9,... | collective-permute-start | bytes 86024 | tf_op jit(solution)/shard_map/ppermute | solution.py:221
  9.0 4.2 %collective-permute-start.2 = (f32[7,8,128]{2,1,0:T(8,128)S(1)}, f32[7,8,128]{2,1,0:T(8,128)S(1)}, u32[]{:S(2)}, u32[]{:S(2)}) collective-permute-start(f32[7,8,128]{2,1,0:T(8,128)S(1)} %get-tuple-element.24), channel_id=1, source_target_pairs={{0,18},{1,19},{2,16},{3,17},{4,22},{5,23},{6,20},{7,21},{8,26},{9,... | collective-permute-start | bytes 86024 | tf_op jit(solution)/shard_map/ppermute | solution.py:221
  9.0 4.2 %collective-permute-start.3 = (f32[7,8,128]{2,1,0:T(8,128)S(1)}, f32[7,8,128]{2,1,0:T(8,128)S(1)}, u32[]{:S(2)}, u32[]{:S(2)}) collective-permute-start(f32[7,8,128]{2,1,0:T(8,128)S(1)} %get-tuple-element.25), channel_id=1, source_target_pairs={{0,10},{1,11},{2,8},{3,9},{4,14},{5,15},{6,12},{7,13},{8,2},{9,3},... | collective-permute-start | bytes 86024 | tf_op jit(solution)/shard_map/ppermute | solution.py:221
  13.2 4.3 %collective-permute-start.4 = (f32[7,8,128]{2,1,0:T(8,128)S(1)}, f32[7,8,128]{2,1,0:T(8,128)S(1)}, u32[]{:S(2)}, u32[]{:S(2)}) collective-permute-start(f32[7,8,128]{2,1,0:T(8,128)S(1)} %shard_map.50._.own_ref), channel_id=1, source_target_pairs={{0,7},{1,6},{2,5},{3,4},{4,3},{5,2},{6,1},{7,0},{8,15},{9,14},{10,... | collective-permute-start | bytes 86024 | tf_op jit(solution)/shard_map/ppermute | solution.py:221
  15.7 3.3 %collective-permute-start.5 = (f32[7,8,128]{2,1,0:T(8,128)S(1)}, f32[7,8,128]{2,1,0:T(8,128)S(1)}, u32[]{:S(2)}, u32[]{:S(2)}) collective-permute-start(f32[7,8,128]{2,1,0:T(8,128)S(1)} %shard_map.50._.own_ref), channel_id=1, source_target_pairs={{0,6},{1,7},{2,4},{3,5},{4,2},{5,3},{6,0},{7,1},{8,14},{9,15},{10,... | collective-permute-start | bytes 86024 | tf_op jit(solution)/shard_map/ppermute | solution.py:221
  16.0 3.3 %collective-permute-start.6 = (f32[7,8,128]{2,1,0:T(8,128)S(1)}, f32[7,8,128]{2,1,0:T(8,128)S(1)}, u32[]{:S(2)}, u32[]{:S(2)}) collective-permute-start(f32[7,8,128]{2,1,0:T(8,128)S(1)} %shard_map.50._.own_ref), channel_id=1, source_target_pairs={{0,3},{1,2},{2,1},{3,0},{4,7},{5,6},{6,5},{7,4},{8,11},{9,10},{10,... | collective-permute-start | bytes 86024 | tf_op jit(solution)/shard_map/ppermute | solution.py:221
  19.3 1.3 %collective-permute-start.7 = (f32[2,7,8,128]{3,2,1,0:T(8,128)S(1)}, f32[2,7,8,128]{3,2,1,0:T(8,128)S(1)}, u32[]{:S(2)}, u32[]{:S(2)}) collective-permute-start(f32[2,7,8,128]{3,2,1,0:T(8,128)S(1)} %shard_map.52.sent_ref), channel_id=1, source_target_pairs={{0,2},{1,3},{2,0},{3,1},{4,6},{5,7},{6,4},{7,5},{8,10},{9,11},{10,... | collective-permute-start | bytes 172040 | tf_op jit(solution)/shard_map/ppermute | solution.py:221
  21.6 1.2 %collective-permute-start.8 = (f32[10,8,128]{2,1,0:T(8,128)S(1)}, f32[10,8,128]{2,1,0:T(8,128)S(1)}, u32[]{:S(2)}, u32[]{:S(2)}) collective-permute-start(f32[10,8,128]{2,1,0:T(8,128)S(1)} %shard_map.53), channel_id=1, source_target_pairs={{0,2},{1,3},{2,0},{3,1},{4,6},{5,7},{6,4},{7,5},{8,10},{9,11},{10,... | collective-permute-start | bytes 122888 | tf_op jit(solution)/shard_map/ppermute | solution.py:221
  22.8 3.3 %collective-permute-start.10 = (f32[5,8,128]{2,1,0:T(8,128)S(1)}, f32[5,8,128]{2,1,0:T(8,128)S(1)}, u32[]{:S(2)}, u32[]{:S(2)}) collective-permute-start(f32[5,8,128]{2,1,0:T(8,128)S(1)} %slice_select_fusion), channel_id=1, source_target_pairs={{0,6},{1,7},{2,4},{3,5},{4,2},{5,3},{6,0},{7,1},{8,14},{9,15},{10,... | collective-permute-start | bytes 61448 | tf_op jit(solution)/shard_map/ppermute | solution.py:221
  24.3 3.2 %collective-permute-start.11 = (f32[5,8,128]{2,1,0:T(8,128)S(1)}, f32[5,8,128]{2,1,0:T(8,128)S(1)}, u32[]{:S(2)}, u32[]{:S(2)}) collective-permute-start(f32[5,8,128]{2,1,0:T(8,128)S(1)} %slice_select_fusion), channel_id=1, source_target_pairs={{0,3},{1,2},{2,1},{3,0},{4,7},{5,6},{6,5},{7,4},{8,11},{9,10},{10,... | collective-permute-start | bytes 61448 | tf_op jit(solution)/shard_map/ppermute | solution.py:221
  24.8 4.1 %collective-permute-start.9 = (f32[5,8,128]{2,1,0:T(8,128)S(1)}, f32[5,8,128]{2,1,0:T(8,128)S(1)}, u32[]{:S(2)}, u32[]{:S(2)}) collective-permute-start(f32[5,8,128]{2,1,0:T(8,128)S(1)} %slice_select_fusion), channel_id=1, source_target_pairs={{0,7},{1,6},{2,5},{3,4},{4,3},{5,2},{6,1},{7,0},{8,15},{9,14},{10,... | collective-permute-start | bytes 61448 | tf_op jit(solution)/shard_map/ppermute | solution.py:221
  28.9 5.1 %collective-permute-start.12 = (f32[5,8,128]{2,1,0:T(8,128)S(1)}, f32[5,8,128]{2,1,0:T(8,128)S(1)}, u32[]{:S(2)}, u32[]{:S(2)}) collective-permute-start(f32[5,8,128]{2,1,0:T(8,128)S(1)} %add_add_fusion.own_ref), channel_id=1, source_target_pairs={{0,26},{1,27},{2,24},{3,25},{4,30},{5,31},{6,28},{7,29},{8,18},{9,... | collective-permute-start | bytes 61448 | tf_op jit(solution)/shard_map/ppermute | solution.py:221
  30.7 4.3 %collective-permute-start.13 = (f32[5,8,128]{2,1,0:T(8,128)S(1)}, f32[5,8,128]{2,1,0:T(8,128)S(1)}, u32[]{:S(2)}, u32[]{:S(2)}) collective-permute-start(f32[5,8,128]{2,1,0:T(8,128)S(1)} %add_add_fusion.own_ref), channel_id=1, source_target_pairs={{0,18},{1,19},{2,16},{3,17},{4,22},{5,23},{6,20},{7,21},{8,26},{9,... | collective-permute-start | bytes 61448 | tf_op jit(solution)/shard_map/ppermute | solution.py:221
  30.8 4.3 %collective-permute-start.14 = (f32[5,8,128]{2,1,0:T(8,128)S(1)}, f32[5,8,128]{2,1,0:T(8,128)S(1)}, u32[]{:S(2)}, u32[]{:S(2)}) collective-permute-start(f32[5,8,128]{2,1,0:T(8,128)S(1)} %add_add_fusion.own_ref), channel_id=1, source_target_pairs={{0,10},{1,11},{2,8},{3,9},{4,14},{5,15},{6,12},{7,13},{8,2},{9,3},... | collective-permute-start | bytes 61448 | tf_op jit(solution)/shard_map/ppermute | solution.py:221
  32.9 2.2 %collective-permute-start.15 = (f32[5,8,128]{2,1,0:T(8,128)S(1)}, f32[5,8,128]{2,1,0:T(8,128)S(1)}, u32[]{:S(2)}, u32[]{:S(2)}) collective-permute-start(f32[5,8,128]{2,1,0:T(8,128)S(1)} %add_add_fusion.own_ref), channel_id=1, source_target_pairs={{0,2},{1,3},{2,0},{3,1},{4,6},{5,7},{6,4},{7,5},{8,10},{9,11},{10,... | collective-permute-start | bytes 61448 | tf_op jit(solution)/shard_map/ppermute | solution.py:221
  35.0 1.4 %collective-permute-start.16 = (f32[3,5,8,128]{3,2,1,0:T(8,128)S(1)}, f32[3,5,8,128]{3,2,1,0:T(8,128)S(1)}, u32[]{:S(2)}, u32[]{:S(2)}) collective-permute-start(f32[3,5,8,128]{3,2,1,0:T(8,128)S(1)} %shard_map.54.others_ref), channel_id=1, source_target_pairs={{0,2},{1,3},{2,0},{3,1},{4,6},{5,7},{6,4},{7,5},{8,10},{9,11},{10,... | collective-permute-start | bytes 184328 | tf_op jit(solution)/shard_map/ppermute | solution.py:221

commit v6 on v5

--- a/solution.py
+++ b/solution.py
@@ -135,6 +135,19 @@
     out_ref[1] = own_ref[...]
 
 
+def halves_kernel(mine_ref, theirs_ref, keep_ref, send_ref):
+    core = lax.axis_index("seq") % 2
+    half = keep_ref.shape[0]
+    for ref, side in ((send_ref, core), (keep_ref, 1 - core)):
+        own = pl.ds(side * half, half)
+        ref[...] = mine_ref[own] + theirs_ref[own]
+
+
+def add_kernel(own_ref, *refs):
+    *others, out_ref = refs
+    out_ref[...] = own_ref[...] + sum(r[...] for r in others)
+
+
 def stack_kernel(*refs):
     _, *others, _, out_ref = refs
     for k, r in enumerate(reversed(others)):
@@ -278,7 +291,11 @@
 
         def local(kernel, out, *args):
             return pl.pallas_call(
-                kernel, out_shape=out, in_specs=[VMEM] * len(args), out_specs=VMEM, compiler_params=params
+                kernel,
+                out_shape=out,
+                in_specs=[VMEM] * len(args),
+                out_specs=jax.tree.map(lambda _: VMEM, out),
+                compiler_params=params,
             )(*args)
 
         part = pltpu.VMEM((experts * units, width), jnp.bfloat16)
@@ -307,9 +324,10 @@
         sent = local(plane_kernel, shape, total, *plane(total), ready)
         shape = pltpu.VMEM((2 * half, rows, LANES), f32)
         partial = local(expert_kernel, shape, sent, other_core(sent), in_high, in_low, out_high, out_low)
-        partial = partial + other_core(partial)
-        first, second = partial[:half], partial[half:]
-        own = pick(core, second, first) + sum(plane(pick(core, first, second)))
+        shape = pltpu.VMEM((half, rows, LANES), f32)
+        keep, send = local(halves_kernel, (shape, shape), partial, other_core(partial))
+        around = plane(send)
+        own = local(add_kernel, shape, keep, *around[-1:], *around[:-1])
         arrived = [along_expert(own, k) for k in order]
         own_near = other_core(own)
         shape = pltpu.VMEM((n_expert - 1, half, rows, LANES), f32)

time: 37.6 us -> 36.5 us (0.971)
  waiting for transfers between devices: 10.7 us -> 9.66 us
    ppermute x17, waiting for transfers between devices: 10.7 us -> 9.66 us  [permute(): return lax.ppermute(value, AXES, pairs)]
    pallas_call x4 -> x6, Pallas kernels: 1.05 us -> 1.07 us  [local(): pl.pallas_call(kernel, out_shape=out, in_specs=[VMEM] * len(args), out_sp...]
  transfers between devices with their start and end apart: 17 -> 17, of which waited for: 11 -> 12; matrix products, arithmetic and copies ran while one was open for 0% -> 0% of each run, Pallas kernels for 11% -> 11%
where the time goes in v6:
time: 36.5 us; the launch traced here: 36.4 us
  starting transfers between devices  17.7 us (48%)
  waiting for transfers between devices  9.66 us (26%)
  Pallas kernels  8.87 us (24%)
    ppermute x17, starting transfers between devices, permute(): return lax.ppermute(value, AXES, pairs)  17.7 us
    ppermute x17, waiting for transfers between devices, permute(): return lax.ppermute(value, AXES, pairs)  9.66 us
    pallas_call x1, Pallas kernels, body(): pl.pallas_call(functools.partial(dispatch_kernel, chunks), out_shape=(plt...  2.65 us
    pallas_call x2, Pallas kernels, mix(): pl.pallas_call(functools.partial(mix_kernel, near), out_shape=jax.ShapeDt...  2.03 us
    pallas_call x1, Pallas kernels, body(): pl.pallas_call(split_out_kernel, out_shape=(part, part, flag), in_specs=[...  2 us
    pallas_call x6, Pallas kernels, local(): pl.pallas_call(kernel, out_shape=out, in_specs=[VMEM] * len(args), out_sp...  1.07 us
    pallas_call x1, Pallas kernels, body(): pl.pallas_call(split_in_kernel, out_shape=(part, part, flag), in_specs=[V...  0.89 us
  transfers between devices with their start and end apart: 17, of which 12 were waited for; matrix products, arithmetic and copies ran while one was open for 0% of the time, Pallas kernels for 11%

profile of v6, /device:TPU:0, one launch (start us, length us, event | category | flops | bytes accessed | tf_op | source)
XLA Modules:
  0.0 36.4 jit_solution(13898061313839244309)
XLA Ops:
  0.0 2.7 %shard_map.46 = (f32[32,224]{1,0:T(8,128)S(1)}, f32[4,7,8,128]{3,2,1,0:T(8,128)S(1)}, f32[4,7,8,128]{3,2,1,0:T(8,128)S(1)}, f32[2,320,1280]{2,1,0:T(8,128)S(1)}) custom-call(f32[224,1280]{1,0:T(8,128)} %tokens_hbm.1, f32[32,1280]{1,0:T(8,128)} %bitcast.1, f32[2,320,1280]{2,1,0:T(8,128)} %w_in_hbm.1), custom_call_target="tpu_custom_call" | custom-call | tf_op jit(solution)/shard_map/pallas_call | solution.py:259
  2.7 0.5 %collective-permute-start = (f32[4,7,8,128]{3,2,1,0:T(8,128)S(1)}, f32[4,7,8,128]{3,2,1,0:T(8,128)S(1)}, u32[]{:S(2)}, u32[]{:S(2)}) collective-permute-start(f32[4,7,8,128]{3,2,1,0:T(8,128)S(1)} %get-tuple-element.23), channel_id=1, source_target_pairs={{0,2},{1,3},{2,0},{3,1},{4,6},{5,7},{6,4},{7,5},{8,10},{9,11},{10,... | collective-permute-start | bytes 344072 | tf_op jit(solution)/shard_map/ppermute | solution.py:234
  3.2 1.0 %collective-permute-done.theirs_ref = f32[4,7,8,128]{3,2,1,0:T(8,128)S(1)} collective-permute-done((f32[4,7,8,128]{3,2,1,0:T(8,128)S(1)}, f32[4,7,8,128]{3,2,1,0:T(8,128)S(1)}, u32[]{:S(2)}, u32[]{:S(2)}) %collective-permute-start) | collective-permute-done | bytes 114720 | tf_op jit(solution)/shard_map/ppermute | solution.py:234
  4.2 4.8 %collective-permute-start.1 = (f32[7,8,128]{2,1,0:T(8,128)S(1)}, f32[7,8,128]{2,1,0:T(8,128)S(1)}, u32[]{:S(2)}, u32[]{:S(2)}) collective-permute-start(f32[7,8,128]{2,1,0:T(8,128)S(1)} %get-tuple-element.25), channel_id=1, source_target_pairs={{0,26},{1,27},{2,24},{3,25},{4,30},{5,31},{6,28},{7,29},{8,18},{9,... | collective-permute-start | bytes 86024 | tf_op jit(solution)/shard_map/ppermute | solution.py:234
  9.0 0.6 %collective-permute-start.3 = (f32[7,8,128]{2,1,0:T(8,128)S(1)}, f32[7,8,128]{2,1,0:T(8,128)S(1)}, u32[]{:S(2)}, u32[]{:S(2)}) collective-permute-start(f32[7,8,128]{2,1,0:T(8,128)S(1)} %get-tuple-element.27), channel_id=1, source_target_pairs={{0,10},{1,11},{2,8},{3,9},{4,14},{5,15},{6,12},{7,13},{8,2},{9,3},... | collective-permute-start | bytes 86024 | tf_op jit(solution)/shard_map/ppermute | solution.py:234
  9.6 2.0 %shard_map.49 = (bf16[640,1280]{1,0:T(8,128)(2,1)S(1)}, bf16[640,1280]{1,0:T(8,128)(2,1)S(1)}, f32[8,128]{1,0:T(8,128)S(1)}) custom-call(f32[7,8,128]{2,1,0:T(8,128)S(1)} %get-tuple-element.24._.own_ref, f32[2,320,1280]{2,1,0:T(8,128)} %w_hbm.1), custom_call_target="tpu_custom_call" | custom-call | flops 6553600 | bytes 6553600 | tf_op jit(solution)/shard_map/pallas_call | solution.py:303
  11.6 1.6 %collective-permute-done.2.refs_1_ = f32[7,8,128]{2,1,0:T(8,128)S(1)} collective-permute-done((f32[7,8,128]{2,1,0:T(8,128)S(1)}, f32[7,8,128]{2,1,0:T(8,128)S(1)}, u32[]{:S(2)}, u32[]{:S(2)}) %collective-permute-start.2) | collective-permute-done | bytes 28704 | tf_op jit(solution)/shard_map/ppermute | solution.py:234
  13.2 2.4 %collective-permute-start.4 = (f32[7,8,128]{2,1,0:T(8,128)S(1)}, f32[7,8,128]{2,1,0:T(8,128)S(1)}, u32[]{:S(2)}, u32[]{:S(2)}) collective-permute-start(f32[7,8,128]{2,1,0:T(8,128)S(1)} %shard_map.50._.own_ref), channel_id=1, source_target_pairs={{0,7},{1,6},{2,5},{3,4},{4,3},{5,2},{6,1},{7,0},{8,15},{9,14},{10,... | collective-permute-start | bytes 86024 | tf_op jit(solution)/shard_map/ppermute | solution.py:234
  16.0 0.5 %collective-permute-start.6 = (f32[7,8,128]{2,1,0:T(8,128)S(1)}, f32[7,8,128]{2,1,0:T(8,128)S(1)}, u32[]{:S(2)}, u32[]{:S(2)}) collective-permute-start(f32[7,8,128]{2,1,0:T(8,128)S(1)} %shard_map.50._.own_ref), channel_id=1, source_target_pairs={{0,3},{1,2},{2,1},{3,0},{4,7},{5,6},{6,5},{7,4},{8,11},{9,10},{10,... | collective-permute-start | bytes 86024 | tf_op jit(solution)/shard_map/ppermute | solution.py:234
  16.4 0.9 %shard_map.51 = (bf16[1280,640]{1,0:T(8,128)(2,1)S(1)}, bf16[1280,640]{1,0:T(8,128)(2,1)S(1)}, f32[8,128]{1,0:T(8,128)S(1)}) custom-call(f32[7,8,128]{2,1,0:T(8,128)S(1)} %shard_map.50._.own_ref, f32[2,320,1280]{2,1,0:T(8,128)S(1)} %get-tuple-element.29.w_ref), custom_call_target="tpu_custom_call" | custom-call | flops 6553600 | bytes 6553600 | tf_op jit(solution)/shard_map/pallas_call | solution.py:315
  17.5 1.5 %collective-permute-done.5.refs_1_ = f32[7,8,128]{2,1,0:T(8,128)S(1)} collective-permute-done((f32[7,8,128]{2,1,0:T(8,128)S(1)}, f32[7,8,128]{2,1,0:T(8,128)S(1)}, u32[]{:S(2)}, u32[]{:S(2)}) %collective-permute-start.5) | collective-permute-done | bytes 28704 | tf_op jit(solution)/shard_map/ppermute | solution.py:234
  19.7 0.9 %collective-permute-done.7.got_ref = f32[2,7,8,128]{3,2,1,0:T(8,128)S(1)} collective-permute-done((f32[2,7,8,128]{3,2,1,0:T(8,128)S(1)}, f32[2,7,8,128]{3,2,1,0:T(8,128)S(1)}, u32[]{:S(2)}, u32[]{:S(2)}) %collective-permute-start.7) | collective-permute-done | bytes 57376 | tf_op jit(solution)/shard_map/ppermute | solution.py:234
  20.6 1.0 %shard_map.53.mine_ref = f32[10,8,128]{2,1,0:T(8,128)S(1)} custom-call(f32[2,7,8,128]{3,2,1,0:T(8,128)S(1)} %shard_map.52.sent_ref, f32[2,7,8,128]{3,2,1,0:T(8,128)S(1)} %collective-permute-done.7.got_ref, bf16[1280,640]{1,0:T(8,128)(2,1)S(1)} %get-tuple-element.31.in_high_ref, bf16[1280,640]{1,0:T(8,128)(2,1)S(1)} %get-tuple-element.32.in_low_ref, ...), custom_call_target="tpu_custom_call" | custom-call | tf_op jit(solution)/shard_map/pallas_call | solution.py:293
  22.0 0.9 %collective-permute-done.8.theirs_ref = f32[10,8,128]{2,1,0:T(8,128)S(1)} collective-permute-done((f32[10,8,128]{2,1,0:T(8,128)S(1)}, f32[10,8,128]{2,1,0:T(8,128)S(1)}, u32[]{:S(2)}, u32[]{:S(2)}) %collective-permute-start.8) | collective-permute-done | bytes 40992 | tf_op jit(solution)/shard_map/ppermute | solution.py:234
  22.8 1.4 %collective-permute-start.10 = (f32[5,8,128]{2,1,0:T(8,128)S(1)}, f32[5,8,128]{2,1,0:T(8,128)S(1)}, u32[]{:S(2)}, u32[]{:S(2)}) collective-permute-start(f32[5,8,128]{2,1,0:T(8,128)S(1)} %get-tuple-element.36), channel_id=1, source_target_pairs={{0,7},{1,6},{2,5},{3,4},{4,3},{5,2},{6,1},{7,0},{8,15},{9,14},{10,... | collective-permute-start | bytes 61448 | tf_op jit(solution)/shard_map/ppermute | solution.py:234
  24.6 1.4 %collective-permute-start.9 = (f32[5,8,128]{2,1,0:T(8,128)S(1)}, f32[5,8,128]{2,1,0:T(8,128)S(1)}, u32[]{:S(2)}, u32[]{:S(2)}) collective-permute-start(f32[5,8,128]{2,1,0:T(8,128)S(1)} %get-tuple-element.36), channel_id=1, source_target_pairs={{0,3},{1,2},{2,1},{3,0},{4,7},{5,6},{6,5},{7,4},{8,11},{9,10},{10,... | collective-permute-start | bytes 61448 | tf_op jit(solution)/shard_map/ppermute | solution.py:234
  26.0 0.9 %collective-permute-done.10.refs_1_ = f32[5,8,128]{2,1,0:T(8,128)S(1)} collective-permute-done((f32[5,8,128]{2,1,0:T(8,128)S(1)}, f32[5,8,128]{2,1,0:T(8,128)S(1)}, u32[]{:S(2)}, u32[]{:S(2)}) %collective-permute-start.10) | collective-permute-done | bytes 20512 | tf_op jit(solution)/shard_map/ppermute | solution.py:234
  26.9 0.5 %collective-permute-done.11.refs_2_ = f32[5,8,128]{2,1,0:T(8,128)S(1)} collective-permute-done((f32[5,8,128]{2,1,0:T(8,128)S(1)}, f32[5,8,128]{2,1,0:T(8,128)S(1)}, u32[]{:S(2)}, u32[]{:S(2)}) %collective-permute-start.11) | collective-permute-done | bytes 20512 | tf_op jit(solution)/shard_map/ppermute | solution.py:234
  27.8 1.9 %collective-permute-start.12 = (f32[5,8,128]{2,1,0:T(8,128)S(1)}, f32[5,8,128]{2,1,0:T(8,128)S(1)}, u32[]{:S(2)}, u32[]{:S(2)}) collective-permute-start(f32[5,8,128]{2,1,0:T(8,128)S(1)} %shard_map.55.own_ref), channel_id=1, source_target_pairs={{0,26},{1,27},{2,24},{3,25},{4,30},{5,31},{6,28},{7,29},{8,18},{9,... | collective-permute-start | bytes 61448 | tf_op jit(solution)/shard_map/ppermute | solution.py:234
  29.7 2.1 %collective-permute-start.14 = (f32[5,8,128]{2,1,0:T(8,128)S(1)}, f32[5,8,128]{2,1,0:T(8,128)S(1)}, u32[]{:S(2)}, u32[]{:S(2)}) collective-permute-start(f32[5,8,128]{2,1,0:T(8,128)S(1)} %shard_map.55.own_ref), channel_id=1, source_target_pairs={{0,10},{1,11},{2,8},{3,9},{4,14},{5,15},{6,12},{7,13},{8,2},{9,3},... | collective-permute-start | bytes 61448 | tf_op jit(solution)/shard_map/ppermute | solution.py:234
  32.3 0.6 %collective-permute-done.12.refs_1_ = f32[5,8,128]{2,1,0:T(8,128)S(1)} collective-permute-done((f32[5,8,128]{2,1,0:T(8,128)S(1)}, f32[5,8,128]{2,1,0:T(8,128)S(1)}, u32[]{:S(2)}, u32[]{:S(2)}) %collective-permute-start.12) | collective-permute-done | bytes 20512 | tf_op jit(solution)/shard_map/ppermute | solution.py:234
  32.9 1.1 %collective-permute-done.13.refs_2_ = f32[5,8,128]{2,1,0:T(8,128)S(1)} collective-permute-done((f32[5,8,128]{2,1,0:T(8,128)S(1)}, f32[5,8,128]{2,1,0:T(8,128)S(1)}, u32[]{:S(2)}, u32[]{:S(2)}) %collective-permute-start.13) | collective-permute-done | bytes 20512 | tf_op jit(solution)/shard_map/ppermute | solution.py:234
  34.3 1.0 %shard_map.57.refs_0_ = f32[224,1280]{1,0:T(8,128)} custom-call(bf16[224,96]{1,0:T(8,128)(2,1)S(1)} %shard_map.47.refs_0_.combine_ref, f32[5,8,128]{2,1,0:T(8,128)S(1)} %collective-permute-done.15.refs_4_.own_ref, f32[3,5,8,128]{3,2,1,0:T(8,128)S(1)} %shard_map.56.others_ref), custom_call_target="tpu_custom_call" | custom-call | tf_op jit(solution)/shard_map/pallas_call | solution.py:337
  35.3 1.0 %shard_map.58 = f32[224,1280]{1,0:T(8,128)} custom-call(bf16[224,96]{1,0:T(8,128)(2,1)S(1)} %shard_map.47.refs_0_.combine_ref, f32[5,8,128]{2,1,0:T(8,128)S(1)} %shard_map.55.own_ref, f32[3,5,8,128]{3,2,1,0:T(8,128)S(1)} %collective-permute-done.16.others_ref, f32[224,1280]{1,0:T(8,128)} %shard_map.57.refs_0_), custom_call_target="tpu_custom_call", output_to_operand_aliasing={{}: (3, {})} | custom-call | tf_op jit(solution)/shard_map/pallas_call | solution.py:337
  (23 shorter events, 3.1 us)
Async XLA Ops:
  2.7 1.5 %collective-permute-start = (f32[4,7,8,128]{3,2,1,0:T(8,128)S(1)}, f32[4,7,8,128]{3,2,1,0:T(8,128)S(1)}, u32[]{:S(2)}, u32[]{:S(2)}) collective-permute-start(f32[4,7,8,128]{3,2,1,0:T(8,128)S(1)} %get-tuple-element.23), channel_id=1, source_target_pairs={{0,2},{1,3},{2,0},{3,1},{4,6},{5,7},{6,4},{7,5},{8,10},{9,11},{10,... | collective-permute-start | bytes 344072 | tf_op jit(solution)/shard_map/ppermute | solution.py:234
  4.2 7.4 %collective-permute-start.1 = (f32[7,8,128]{2,1,0:T(8,128)S(1)}, f32[7,8,128]{2,1,0:T(8,128)S(1)}, u32[]{:S(2)}, u32[]{:S(2)}) collective-permute-start(f32[7,8,128]{2,1,0:T(8,128)S(1)} %get-tuple-element.25), channel_id=1, source_target_pairs={{0,26},{1,27},{2,24},{3,25},{4,30},{5,31},{6,28},{7,29},{8,18},{9,... | collective-permute-start | bytes 86024 | tf_op jit(solution)/shard_map/ppermute | solution.py:234
  9.0 4.2 %collective-permute-start.2 = (f32[7,8,128]{2,1,0:T(8,128)S(1)}, f32[7,8,128]{2,1,0:T(8,128)S(1)}, u32[]{:S(2)}, u32[]{:S(2)}) collective-permute-start(f32[7,8,128]{2,1,0:T(8,128)S(1)} %get-tuple-element.26), channel_id=1, source_target_pairs={{0,18},{1,19},{2,16},{3,17},{4,22},{5,23},{6,20},{7,21},{8,26},{9,... | collective-permute-start | bytes 86024 | tf_op jit(solution)/shard_map/ppermute | solution.py:234
  9.0 4.2 %collective-permute-start.3 = (f32[7,8,128]{2,1,0:T(8,128)S(1)}, f32[7,8,128]{2,1,0:T(8,128)S(1)}, u32[]{:S(2)}, u32[]{:S(2)}) collective-permute-start(f32[7,8,128]{2,1,0:T(8,128)S(1)} %get-tuple-element.27), channel_id=1, source_target_pairs={{0,10},{1,11},{2,8},{3,9},{4,14},{5,15},{6,12},{7,13},{8,2},{9,3},... | collective-permute-start | bytes 86024 | tf_op jit(solution)/shard_map/ppermute | solution.py:234
  13.2 4.3 %collective-permute-start.4 = (f32[7,8,128]{2,1,0:T(8,128)S(1)}, f32[7,8,128]{2,1,0:T(8,128)S(1)}, u32[]{:S(2)}, u32[]{:S(2)}) collective-permute-start(f32[7,8,128]{2,1,0:T(8,128)S(1)} %shard_map.50._.own_ref), channel_id=1, source_target_pairs={{0,7},{1,6},{2,5},{3,4},{4,3},{5,2},{6,1},{7,0},{8,15},{9,14},{10,... | collective-permute-start | bytes 86024 | tf_op jit(solution)/shard_map/ppermute | solution.py:234
  15.7 3.3 %collective-permute-start.5 = (f32[7,8,128]{2,1,0:T(8,128)S(1)}, f32[7,8,128]{2,1,0:T(8,128)S(1)}, u32[]{:S(2)}, u32[]{:S(2)}) collective-permute-start(f32[7,8,128]{2,1,0:T(8,128)S(1)} %shard_map.50._.own_ref), channel_id=1, source_target_pairs={{0,6},{1,7},{2,4},{3,5},{4,2},{5,3},{6,0},{7,1},{8,14},{9,15},{10,... | collective-permute-start | bytes 86024 | tf_op jit(solution)/shard_map/ppermute | solution.py:234
  16.0 3.3 %collective-permute-start.6 = (f32[7,8,128]{2,1,0:T(8,128)S(1)}, f32[7,8,128]{2,1,0:T(8,128)S(1)}, u32[]{:S(2)}, u32[]{:S(2)}) collective-permute-start(f32[7,8,128]{2,1,0:T(8,128)S(1)} %shard_map.50._.own_ref), channel_id=1, source_target_pairs={{0,3},{1,2},{2,1},{3,0},{4,7},{5,6},{6,5},{7,4},{8,11},{9,10},{10,... | collective-permute-start | bytes 86024 | tf_op jit(solution)/shard_map/ppermute | solution.py:234
  19.3 1.3 %collective-permute-start.7 = (f32[2,7,8,128]{3,2,1,0:T(8,128)S(1)}, f32[2,7,8,128]{3,2,1,0:T(8,128)S(1)}, u32[]{:S(2)}, u32[]{:S(2)}) collective-permute-start(f32[2,7,8,128]{3,2,1,0:T(8,128)S(1)} %shard_map.52.sent_ref), channel_id=1, source_target_pairs={{0,2},{1,3},{2,0},{3,1},{4,6},{5,7},{6,4},{7,5},{8,10},{9,11},{10,... | collective-permute-start | bytes 172040 | tf_op jit(solution)/shard_map/ppermute | solution.py:234
  21.6 1.2 %collective-permute-start.8 = (f32[10,8,128]{2,1,0:T(8,128)S(1)}, f32[10,8,128]{2,1,0:T(8,128)S(1)}, u32[]{:S(2)}, u32[]{:S(2)}) collective-permute-start(f32[10,8,128]{2,1,0:T(8,128)S(1)} %shard_map.53.mine_ref), channel_id=1, source_target_pairs={{0,2},{1,3},{2,0},{3,1},{4,6},{5,7},{6,4},{7,5},{8,10},{9,11},{10,... | collective-permute-start | bytes 122888 | tf_op jit(solution)/shard_map/ppermute | solution.py:234
  22.8 4.1 %collective-permute-start.10 = (f32[5,8,128]{2,1,0:T(8,128)S(1)}, f32[5,8,128]{2,1,0:T(8,128)S(1)}, u32[]{:S(2)}, u32[]{:S(2)}) collective-permute-start(f32[5,8,128]{2,1,0:T(8,128)S(1)} %get-tuple-element.36), channel_id=1, source_target_pairs={{0,7},{1,6},{2,5},{3,4},{4,3},{5,2},{6,1},{7,0},{8,15},{9,14},{10,... | collective-permute-start | bytes 61448 | tf_op jit(solution)/shard_map/ppermute | solution.py:234
  24.2 3.2 %collective-permute-start.11 = (f32[5,8,128]{2,1,0:T(8,128)S(1)}, f32[5,8,128]{2,1,0:T(8,128)S(1)}, u32[]{:S(2)}, u32[]{:S(2)}) collective-permute-start(f32[5,8,128]{2,1,0:T(8,128)S(1)} %get-tuple-element.36), channel_id=1, source_target_pairs={{0,6},{1,7},{2,4},{3,5},{4,2},{5,3},{6,0},{7,1},{8,14},{9,15},{10,... | collective-permute-start | bytes 61448 | tf_op jit(solution)/shard_map/ppermute | solution.py:234
  24.6 3.2 %collective-permute-start.9 = (f32[5,8,128]{2,1,0:T(8,128)S(1)}, f32[5,8,128]{2,1,0:T(8,128)S(1)}, u32[]{:S(2)}, u32[]{:S(2)}) collective-permute-start(f32[5,8,128]{2,1,0:T(8,128)S(1)} %get-tuple-element.36), channel_id=1, source_target_pairs={{0,3},{1,2},{2,1},{3,0},{4,7},{5,6},{6,5},{7,4},{8,11},{9,10},{10,... | collective-permute-start | bytes 61448 | tf_op jit(solution)/shard_map/ppermute | solution.py:234
  27.8 5.1 %collective-permute-start.12 = (f32[5,8,128]{2,1,0:T(8,128)S(1)}, f32[5,8,128]{2,1,0:T(8,128)S(1)}, u32[]{:S(2)}, u32[]{:S(2)}) collective-permute-start(f32[5,8,128]{2,1,0:T(8,128)S(1)} %shard_map.55.own_ref), channel_id=1, source_target_pairs={{0,26},{1,27},{2,24},{3,25},{4,30},{5,31},{6,28},{7,29},{8,18},{9,... | collective-permute-start | bytes 61448 | tf_op jit(solution)/shard_map/ppermute | solution.py:234
  29.7 4.2 %collective-permute-start.13 = (f32[5,8,128]{2,1,0:T(8,128)S(1)}, f32[5,8,128]{2,1,0:T(8,128)S(1)}, u32[]{:S(2)}, u32[]{:S(2)}) collective-permute-start(f32[5,8,128]{2,1,0:T(8,128)S(1)} %shard_map.55.own_ref), channel_id=1, source_target_pairs={{0,18},{1,19},{2,16},{3,17},{4,22},{5,23},{6,20},{7,21},{8,26},{9,... | collective-permute-start | bytes 61448 | tf_op jit(solution)/shard_map/ppermute | solution.py:234
  29.7 4.2 %collective-permute-start.14 = (f32[5,8,128]{2,1,0:T(8,128)S(1)}, f32[5,8,128]{2,1,0:T(8,128)S(1)}, u32[]{:S(2)}, u32[]{:S(2)}) collective-permute-start(f32[5,8,128]{2,1,0:T(8,128)S(1)} %shard_map.55.own_ref), channel_id=1, source_target_pairs={{0,10},{1,11},{2,8},{3,9},{4,14},{5,15},{6,12},{7,13},{8,2},{9,3},... | collective-permute-start | bytes 61448 | tf_op jit(solution)/shard_map/ppermute | solution.py:234
  31.9 2.0 %collective-permute-start.15 = (f32[5,8,128]{2,1,0:T(8,128)S(1)}, f32[5,8,128]{2,1,0:T(8,128)S(1)}, u32[]{:S(2)}, u32[]{:S(2)}) collective-permute-start(f32[5,8,128]{2,1,0:T(8,128)S(1)} %shard_map.55.own_ref), channel_id=1, source_target_pairs={{0,2},{1,3},{2,0},{3,1},{4,6},{5,7},{6,4},{7,5},{8,10},{9,11},{10,... | collective-permute-start | bytes 61448 | tf_op jit(solution)/shard_map/ppermute | solution.py:234
  33.9 1.4 %collective-permute-start.16 = (f32[3,5,8,128]{3,2,1,0:T(8,128)S(1)}, f32[3,5,8,128]{3,2,1,0:T(8,128)S(1)}, u32[]{:S(2)}, u32[]{:S(2)}) collective-permute-start(f32[3,5,8,128]{3,2,1,0:T(8,128)S(1)} %shard_map.56.others_ref), channel_id=1, source_target_pairs={{0,2},{1,3},{2,0},{3,1},{4,6},{5,7},{6,4},{7,5},{8,10},{9,11},{10,... | collective-permute-start | bytes 184328 | tf_op jit(solution)/shard_map/ppermute | solution.py:234

commit v7 on v6

--- a/solution.py
+++ b/solution.py
@@ -57,26 +57,22 @@
         copy.start()
     copies[0].wait()
     params = jnp.concatenate(pieces(params_ref[...], 3), axis=0)
-    highs, lows, logits = [], [], []
+    for copy in copies[1:-1]:
+        copy.wait()
+    token_high, token_low, rest = pieces(tokens_ref[...], 3)
     nt = ((1,), (1,))
-    for (start, stop), copy in zip(chunks, copies[1:]):
-        copy.wait()
-        high, low, rest = pieces(tokens_ref[start:stop], 3)
-        highs.append(high)
-        lows.append(low)
-        a = mm(params, high, nt)
-        b = mm(params[:2 * slots], low, nt)
-        c = mm(params[:slots], rest, nt)
-        small = a[2 * slots:] + b[slots:] + c
-        logits.append((small + (a[slots:2 * slots] + b[:slots])) + a[:slots])
-    logits = jnp.concatenate(logits, axis=1)
+    a = mm(params, token_high, nt)
+    b = mm(params[:2 * slots], token_low, nt)
+    c = mm(params[:slots], rest, nt)
+    small = a[2 * slots:] + b[slots:] + c
+    logits = (small + (a[slots:2 * slots] + b[:slots])) + a[:slots]
     logits_ref[...] = logits
     peak = jnp.max(logits, axis=1, keepdims=True)
     weights = jnp.exp(logits - peak)
     mass = jnp.sum(weights, axis=1, keepdims=True)
     weight_high, weight_low = pieces(weights, 2)
-    high = mm(jnp.concatenate([weight_high, weight_low], axis=0), jnp.concatenate(highs, axis=0))
-    low = mm(weight_high, jnp.concatenate(lows, axis=0))
+    high = mm(jnp.concatenate([weight_high, weight_low], axis=0), token_high)
+    low = mm(weight_high, token_low)
     sums_ref[:, :width] = high[:slots] + (high[slots:] + low)
     sums_ref[:, width:width + LANES] = jnp.broadcast_to(mass, (slots, LANES))
     sums_ref[:, width + LANES:] = jnp.broadcast_to(peak, (slots, LANES))
@@ -150,7 +146,7 @@
 
 def stack_kernel(*refs):
     _, *others, _, out_ref = refs
-    for k, r in enumerate(reversed(others)):
+    for k, r in enumerate(others):
         out_ref[k] = r[...]
 
 
@@ -200,7 +196,7 @@
     half, rows, _ = own_ref.shape
     groups = others_ref.shape[0] + 1
     for k in range(groups):
-        place = pl.ds(pl.multiple_of((expert ^ k) * rows, rows), rows)
+        place = pl.ds(pl.multiple_of(lax.rem(expert - k + groups, groups) * rows, rows), rows)
         for t in range(half):
             slots_ref[place, t * LANES:(t + 1) * LANES] = others_ref[k - 1, t] if k else own_ref[t]
     high, low = pieces(slots_ref[...], 2)
@@ -239,6 +235,9 @@
     def along_expert(value, k):
         return permute(value, lambda e, x, c, f: (e ^ k, x, 1 - c, f))
 
+    def around_expert(value, k):
+        return permute(value, lambda e, x, c, f: ((e + k) % n_expert, x, 1 - c, f))
+
     def plane(value):
         return [
             permute(value, lambda e, x, c, f, dx=dx, df=df: (e, (x + dx) % n_x, 1 - c, (f + df) % n_fsdp))
@@ -253,7 +252,8 @@
         f32 = jnp.float32
         params = pltpu.CompilerParams(vmem_limit_bytes=24 * 1024 * 1024)
         core = lax.axis_index("seq") % 2
-        chunks = [(0, count)]
+        step = count // 4 if count % 32 == 0 else count
+        chunks = [(i, i + step) for i in range(0, count, step)]
         in_hbm = lambda value: pltpu.with_memory_space_constraint(value, pltpu.HBM)
         shape = pltpu.VMEM((n_expert, half + 2, rows, LANES), f32)
         logits, mine, theirs, w_in = pl.pallas_call(
@@ -328,7 +328,7 @@
         keep, send = local(halves_kernel, (shape, shape), partial, other_core(partial))
         around = plane(send)
         own = local(add_kernel, shape, keep, *around[-1:], *around[:-1])
-        arrived = [along_expert(own, k) for k in order]
+        arrived = [around_expert(own, k) for k in range(1, n_expert)]
         own_near = other_core(own)
         shape = pltpu.VMEM((n_expert - 1, half, rows, LANES), f32)
         others = local(stack_kernel, shape, combine, *arrived, own_near)

time: 36.5 us -> 36.1 us (0.989)
  waiting for transfers between devices: 9.66 us -> 9.17 us
    ppermute x17, waiting for transfers between devices: 9.66 us -> 9.17 us  [permute(): return lax.ppermute(value, AXES, pairs)]
  transfers between devices with their start and end apart: 17 -> 17, of which waited for: 12 -> 13; matrix products, arithmetic and copies ran while one was open for 0% -> 0% of each run, Pallas kernels for 11% -> 11%
where the time goes in v7:
time: 36.1 us; the launch traced here: 36 us
  starting transfers between devices  17.9 us (50%)
  waiting for transfers between devices  9.17 us (25%)
  Pallas kernels  8.87 us (25%)
    ppermute x17, starting transfers between devices, permute(): return lax.ppermute(value, AXES, pairs)  17.9 us
    ppermute x17, waiting for transfers between devices, permute(): return lax.ppermute(value, AXES, pairs)  9.17 us
    pallas_call x1, Pallas kernels, body(): pl.pallas_call(functools.partial(dispatch_kernel, chunks), out_shape=(plt...  2.64 us
    pallas_call x2, Pallas kernels, mix(): pl.pallas_call(functools.partial(mix_kernel, near), out_shape=jax.ShapeDt...  2.03 us
    pallas_call x1, Pallas kernels, body(): pl.pallas_call(split_out_kernel, out_shape=(part, part, flag), in_specs=[...  2 us
    pallas_call x6, Pallas kernels, local(): pl.pallas_call(kernel, out_shape=out, in_specs=[VMEM] * len(args), out_sp...  1.07 us
    pallas_call x1, Pallas kernels, body(): pl.pallas_call(split_in_kernel, out_shape=(part, part, flag), in_specs=[V...  0.89 us
  transfers between devices with their start and end apart: 17, of which 13 were waited for; matrix products, arithmetic and copies ran while one was open for 0% of the time, Pallas kernels for 11%

profile of v7, /device:TPU:0, one launch (start us, length us, event | category | flops | bytes accessed | tf_op | source)
XLA Modules:
  0.0 36.0 jit_solution(8904767065378881973)
XLA Ops:
  0.0 2.6 %shard_map.46 = (f32[32,224]{1,0:T(8,128)S(1)}, f32[4,7,8,128]{3,2,1,0:T(8,128)S(1)}, f32[4,7,8,128]{3,2,1,0:T(8,128)S(1)}, f32[2,320,1280]{2,1,0:T(8,128)S(1)}) custom-call(f32[224,1280]{1,0:T(8,128)} %tokens_hbm.1, f32[32,1280]{1,0:T(8,128)} %bitcast.1, f32[2,320,1280]{2,1,0:T(8,128)} %w_in_hbm.1), custom_call_target="tpu_custom_call" | custom-call | tf_op jit(solution)/shard_map/pallas_call | solution.py:259
  2.7 0.5 %collective-permute-start = (f32[4,7,8,128]{3,2,1,0:T(8,128)S(1)}, f32[4,7,8,128]{3,2,1,0:T(8,128)S(1)}, u32[]{:S(2)}, u32[]{:S(2)}) collective-permute-start(f32[4,7,8,128]{3,2,1,0:T(8,128)S(1)} %get-tuple-element.23), channel_id=1, source_target_pairs={{0,2},{1,3},{2,0},{3,1},{4,6},{5,7},{6,4},{7,5},{8,10},{9,11},{10,... | collective-permute-start | bytes 344072 | tf_op jit(solution)/shard_map/ppermute | solution.py:230
  3.2 1.0 %collective-permute-done.theirs_ref = f32[4,7,8,128]{3,2,1,0:T(8,128)S(1)} collective-permute-done((f32[4,7,8,128]{3,2,1,0:T(8,128)S(1)}, f32[4,7,8,128]{3,2,1,0:T(8,128)S(1)}, u32[]{:S(2)}, u32[]{:S(2)}) %collective-permute-start) | collective-permute-done | bytes 114720 | tf_op jit(solution)/shard_map/ppermute | solution.py:230
  4.2 4.8 %collective-permute-start.1 = (f32[7,8,128]{2,1,0:T(8,128)S(1)}, f32[7,8,128]{2,1,0:T(8,128)S(1)}, u32[]{:S(2)}, u32[]{:S(2)}) collective-permute-start(f32[7,8,128]{2,1,0:T(8,128)S(1)} %get-tuple-element.25), channel_id=1, source_target_pairs={{0,26},{1,27},{2,24},{3,25},{4,30},{5,31},{6,28},{7,29},{8,18},{9,... | collective-permute-start | bytes 86024 | tf_op jit(solution)/shard_map/ppermute | solution.py:230
  8.9 0.6 %collective-permute-start.3 = (f32[7,8,128]{2,1,0:T(8,128)S(1)}, f32[7,8,128]{2,1,0:T(8,128)S(1)}, u32[]{:S(2)}, u32[]{:S(2)}) collective-permute-start(f32[7,8,128]{2,1,0:T(8,128)S(1)} %get-tuple-element.27), channel_id=1, source_target_pairs={{0,10},{1,11},{2,8},{3,9},{4,14},{5,15},{6,12},{7,13},{8,2},{9,3},... | collective-permute-start | bytes 86024 | tf_op jit(solution)/shard_map/ppermute | solution.py:230
  9.6 2.0 %shard_map.49 = (bf16[640,1280]{1,0:T(8,128)(2,1)S(1)}, bf16[640,1280]{1,0:T(8,128)(2,1)S(1)}, f32[8,128]{1,0:T(8,128)S(1)}) custom-call(f32[7,8,128]{2,1,0:T(8,128)S(1)} %get-tuple-element.24._.own_ref, f32[2,320,1280]{2,1,0:T(8,128)} %w_hbm.1), custom_call_target="tpu_custom_call" | custom-call | flops 6553600 | bytes 6553600 | tf_op jit(solution)/shard_map/pallas_call | solution.py:303
  11.6 1.6 %collective-permute-done.2.refs_1_ = f32[7,8,128]{2,1,0:T(8,128)S(1)} collective-permute-done((f32[7,8,128]{2,1,0:T(8,128)S(1)}, f32[7,8,128]{2,1,0:T(8,128)S(1)}, u32[]{:S(2)}, u32[]{:S(2)}) %collective-permute-start.2) | collective-permute-done | bytes 28704 | tf_op jit(solution)/shard_map/ppermute | solution.py:230
  13.2 2.5 %collective-permute-start.4 = (f32[7,8,128]{2,1,0:T(8,128)S(1)}, f32[7,8,128]{2,1,0:T(8,128)S(1)}, u32[]{:S(2)}, u32[]{:S(2)}) collective-permute-start(f32[7,8,128]{2,1,0:T(8,128)S(1)} %shard_map.50._.own_ref), channel_id=1, source_target_pairs={{0,7},{1,6},{2,5},{3,4},{4,3},{5,2},{6,1},{7,0},{8,15},{9,14},{10,... | collective-permute-start | bytes 86024 | tf_op jit(solution)/shard_map/ppermute | solution.py:230
  16.0 0.5 %collective-permute-start.6 = (f32[7,8,128]{2,1,0:T(8,128)S(1)}, f32[7,8,128]{2,1,0:T(8,128)S(1)}, u32[]{:S(2)}, u32[]{:S(2)}) collective-permute-start(f32[7,8,128]{2,1,0:T(8,128)S(1)} %shard_map.50._.own_ref), channel_id=1, source_target_pairs={{0,3},{1,2},{2,1},{3,0},{4,7},{5,6},{6,5},{7,4},{8,11},{9,10},{10,... | collective-permute-start | bytes 86024 | tf_op jit(solution)/shard_map/ppermute | solution.py:230
  16.4 0.9 %shard_map.51 = (bf16[1280,640]{1,0:T(8,128)(2,1)S(1)}, bf16[1280,640]{1,0:T(8,128)(2,1)S(1)}, f32[8,128]{1,0:T(8,128)S(1)}) custom-call(f32[7,8,128]{2,1,0:T(8,128)S(1)} %shard_map.50._.own_ref, f32[2,320,1280]{2,1,0:T(8,128)S(1)} %get-tuple-element.29.w_ref), custom_call_target="tpu_custom_call" | custom-call | flops 6553600 | bytes 6553600 | tf_op jit(solution)/shard_map/pallas_call | solution.py:315
  17.4 1.5 %collective-permute-done.5.refs_1_ = f32[7,8,128]{2,1,0:T(8,128)S(1)} collective-permute-done((f32[7,8,128]{2,1,0:T(8,128)S(1)}, f32[7,8,128]{2,1,0:T(8,128)S(1)}, u32[]{:S(2)}, u32[]{:S(2)}) %collective-permute-start.5) | collective-permute-done | bytes 28704 | tf_op jit(solution)/shard_map/ppermute | solution.py:230
  19.3 0.4 %collective-permute-start.7 = (f32[2,7,8,128]{3,2,1,0:T(8,128)S(1)}, f32[2,7,8,128]{3,2,1,0:T(8,128)S(1)}, u32[]{:S(2)}, u32[]{:S(2)}) collective-permute-start(f32[2,7,8,128]{3,2,1,0:T(8,128)S(1)} %shard_map.52.sent_ref), channel_id=1, source_target_pairs={{0,2},{1,3},{2,0},{3,1},{4,6},{5,7},{6,4},{7,5},{8,10},{9,11},{10,... | collective-permute-start | bytes 172040 | tf_op jit(solution)/shard_map/ppermute | solution.py:230
  19.7 0.9 %collective-permute-done.7.got_ref = f32[2,7,8,128]{3,2,1,0:T(8,128)S(1)} collective-permute-done((f32[2,7,8,128]{3,2,1,0:T(8,128)S(1)}, f32[2,7,8,128]{3,2,1,0:T(8,128)S(1)}, u32[]{:S(2)}, u32[]{:S(2)}) %collective-permute-start.7) | collective-permute-done | bytes 57376 | tf_op jit(solution)/shard_map/ppermute | solution.py:230
  20.6 1.0 %shard_map.53.mine_ref = f32[10,8,128]{2,1,0:T(8,128)S(1)} custom-call(f32[2,7,8,128]{3,2,1,0:T(8,128)S(1)} %shard_map.52.sent_ref, f32[2,7,8,128]{3,2,1,0:T(8,128)S(1)} %collective-permute-done.7.got_ref, bf16[1280,640]{1,0:T(8,128)(2,1)S(1)} %get-tuple-element.31.in_high_ref, bf16[1280,640]{1,0:T(8,128)(2,1)S(1)} %get-tuple-element.32.in_low_ref, ...), custom_call_target="tpu_custom_call" | custom-call | tf_op jit(solution)/shard_map/pallas_call | solution.py:293
  21.9 0.9 %collective-permute-done.8.theirs_ref = f32[10,8,128]{2,1,0:T(8,128)S(1)} collective-permute-done((f32[10,8,128]{2,1,0:T(8,128)S(1)}, f32[10,8,128]{2,1,0:T(8,128)S(1)}, u32[]{:S(2)}, u32[]{:S(2)}) %collective-permute-start.8) | collective-permute-done | bytes 40992 | tf_op jit(solution)/shard_map/ppermute | solution.py:230
  22.8 1.4 %collective-permute-start.10 = (f32[5,8,128]{2,1,0:T(8,128)S(1)}, f32[5,8,128]{2,1,0:T(8,128)S(1)}, u32[]{:S(2)}, u32[]{:S(2)}) collective-permute-start(f32[5,8,128]{2,1,0:T(8,128)S(1)} %get-tuple-element.36), channel_id=1, source_target_pairs={{0,7},{1,6},{2,5},{3,4},{4,3},{5,2},{6,1},{7,0},{8,15},{9,14},{10,... | collective-permute-start | bytes 61448 | tf_op jit(solution)/shard_map/ppermute | solution.py:230
  24.6 1.4 %collective-permute-start.9 = (f32[5,8,128]{2,1,0:T(8,128)S(1)}, f32[5,8,128]{2,1,0:T(8,128)S(1)}, u32[]{:S(2)}, u32[]{:S(2)}) collective-permute-start(f32[5,8,128]{2,1,0:T(8,128)S(1)} %get-tuple-element.36), channel_id=1, source_target_pairs={{0,3},{1,2},{2,1},{3,0},{4,7},{5,6},{6,5},{7,4},{8,11},{9,10},{10,... | collective-permute-start | bytes 61448 | tf_op jit(solution)/shard_map/ppermute | solution.py:230
  26.0 0.9 %collective-permute-done.10.refs_1_ = f32[5,8,128]{2,1,0:T(8,128)S(1)} collective-permute-done((f32[5,8,128]{2,1,0:T(8,128)S(1)}, f32[5,8,128]{2,1,0:T(8,128)S(1)}, u32[]{:S(2)}, u32[]{:S(2)}) %collective-permute-start.10) | collective-permute-done | bytes 20512 | tf_op jit(solution)/shard_map/ppermute | solution.py:230
  26.9 0.5 %collective-permute-done.11.refs_2_ = f32[5,8,128]{2,1,0:T(8,128)S(1)} collective-permute-done((f32[5,8,128]{2,1,0:T(8,128)S(1)}, f32[5,8,128]{2,1,0:T(8,128)S(1)}, u32[]{:S(2)}, u32[]{:S(2)}) %collective-permute-start.11) | collective-permute-done | bytes 20512 | tf_op jit(solution)/shard_map/ppermute | solution.py:230
  28.1 2.0 %collective-permute-start.13 = (f32[5,8,128]{2,1,0:T(8,128)S(1)}, f32[5,8,128]{2,1,0:T(8,128)S(1)}, u32[]{:S(2)}, u32[]{:S(2)}) collective-permute-start(f32[5,8,128]{2,1,0:T(8,128)S(1)} %shard_map.55.own_ref), channel_id=1, source_target_pairs={{0,18},{1,19},{2,16},{3,17},{4,22},{5,23},{6,20},{7,21},{8,26},{9,... | collective-permute-start | bytes 61448 | tf_op jit(solution)/shard_map/ppermute | solution.py:230
  30.1 2.1 %collective-permute-start.14 = (f32[5,8,128]{2,1,0:T(8,128)S(1)}, f32[5,8,128]{2,1,0:T(8,128)S(1)}, u32[]{:S(2)}, u32[]{:S(2)}) collective-permute-start(f32[5,8,128]{2,1,0:T(8,128)S(1)} %shard_map.55.own_ref), channel_id=1, source_target_pairs={{0,26},{1,27},{2,24},{3,25},{4,30},{5,31},{6,28},{7,29},{8,2},{9,3... | collective-permute-start | bytes 61448 | tf_op jit(solution)/shard_map/ppermute | solution.py:230
  32.9 0.7 %collective-permute-done.14.refs_3_ = f32[5,8,128]{2,1,0:T(8,128)S(1)} collective-permute-done((f32[5,8,128]{2,1,0:T(8,128)S(1)}, f32[5,8,128]{2,1,0:T(8,128)S(1)}, u32[]{:S(2)}, u32[]{:S(2)}) %collective-permute-start.14) | collective-permute-done | bytes 20512 | tf_op jit(solution)/shard_map/ppermute | solution.py:230
  33.7 1.0 %shard_map.57.refs_0_ = f32[224,1280]{1,0:T(8,128)} custom-call(bf16[224,96]{1,0:T(8,128)(2,1)S(1)} %shard_map.47.refs_0_.combine_ref, f32[5,8,128]{2,1,0:T(8,128)S(1)} %collective-permute-done.15.refs_4_.own_ref, f32[3,5,8,128]{3,2,1,0:T(8,128)S(1)} %shard_map.56.others_ref), custom_call_target="tpu_custom_call" | custom-call | tf_op jit(solution)/shard_map/pallas_call | solution.py:337
  35.0 1.0 %shard_map.58 = f32[224,1280]{1,0:T(8,128)} custom-call(bf16[224,96]{1,0:T(8,128)(2,1)S(1)} %shard_map.47.refs_0_.combine_ref, f32[5,8,128]{2,1,0:T(8,128)S(1)} %shard_map.55.own_ref, f32[3,5,8,128]{3,2,1,0:T(8,128)S(1)} %collective-permute-done.16.others_ref, f32[224,1280]{1,0:T(8,128)} %shard_map.57.refs_0_), custom_call_target="tpu_custom_call", output_to_operand_aliasing={{}: (3, {})} | custom-call | tf_op jit(solution)/shard_map/pallas_call | solution.py:337
  (23 shorter events, 3.2 us)
Async XLA Ops:
  2.7 1.5 %collective-permute-start = (f32[4,7,8,128]{3,2,1,0:T(8,128)S(1)}, f32[4,7,8,128]{3,2,1,0:T(8,128)S(1)}, u32[]{:S(2)}, u32[]{:S(2)}) collective-permute-start(f32[4,7,8,128]{3,2,1,0:T(8,128)S(1)} %get-tuple-element.23), channel_id=1, source_target_pairs={{0,2},{1,3},{2,0},{3,1},{4,6},{5,7},{6,4},{7,5},{8,10},{9,11},{10,... | collective-permute-start | bytes 344072 | tf_op jit(solution)/shard_map/ppermute | solution.py:230
  4.2 7.4 %collective-permute-start.1 = (f32[7,8,128]{2,1,0:T(8,128)S(1)}, f32[7,8,128]{2,1,0:T(8,128)S(1)}, u32[]{:S(2)}, u32[]{:S(2)}) collective-permute-start(f32[7,8,128]{2,1,0:T(8,128)S(1)} %get-tuple-element.25), channel_id=1, source_target_pairs={{0,26},{1,27},{2,24},{3,25},{4,30},{5,31},{6,28},{7,29},{8,18},{9,... | collective-permute-start | bytes 86024 | tf_op jit(solution)/shard_map/ppermute | solution.py:230
  8.9 4.2 %collective-permute-start.2 = (f32[7,8,128]{2,1,0:T(8,128)S(1)}, f32[7,8,128]{2,1,0:T(8,128)S(1)}, u32[]{:S(2)}, u32[]{:S(2)}) collective-permute-start(f32[7,8,128]{2,1,0:T(8,128)S(1)} %get-tuple-element.26), channel_id=1, source_target_pairs={{0,18},{1,19},{2,16},{3,17},{4,22},{5,23},{6,20},{7,21},{8,26},{9,... | collective-permute-start | bytes 86024 | tf_op jit(solution)/shard_map/ppermute | solution.py:230
  8.9 4.2 %collective-permute-start.3 = (f32[7,8,128]{2,1,0:T(8,128)S(1)}, f32[7,8,128]{2,1,0:T(8,128)S(1)}, u32[]{:S(2)}, u32[]{:S(2)}) collective-permute-start(f32[7,8,128]{2,1,0:T(8,128)S(1)} %get-tuple-element.27), channel_id=1, source_target_pairs={{0,10},{1,11},{2,8},{3,9},{4,14},{5,15},{6,12},{7,13},{8,2},{9,3},... | collective-permute-start | bytes 86024 | tf_op jit(solution)/shard_map/ppermute | solution.py:230
  13.2 4.3 %collective-permute-start.4 = (f32[7,8,128]{2,1,0:T(8,128)S(1)}, f32[7,8,128]{2,1,0:T(8,128)S(1)}, u32[]{:S(2)}, u32[]{:S(2)}) collective-permute-start(f32[7,8,128]{2,1,0:T(8,128)S(1)} %shard_map.50._.own_ref), channel_id=1, source_target_pairs={{0,7},{1,6},{2,5},{3,4},{4,3},{5,2},{6,1},{7,0},{8,15},{9,14},{10,... | collective-permute-start | bytes 86024 | tf_op jit(solution)/shard_map/ppermute | solution.py:230
  15.6 3.3 %collective-permute-start.5 = (f32[7,8,128]{2,1,0:T(8,128)S(1)}, f32[7,8,128]{2,1,0:T(8,128)S(1)}, u32[]{:S(2)}, u32[]{:S(2)}) collective-permute-start(f32[7,8,128]{2,1,0:T(8,128)S(1)} %shard_map.50._.own_ref), channel_id=1, source_target_pairs={{0,6},{1,7},{2,4},{3,5},{4,2},{5,3},{6,0},{7,1},{8,14},{9,15},{10,... | collective-permute-start | bytes 86024 | tf_op jit(solution)/shard_map/ppermute | solution.py:230
  16.0 3.3 %collective-permute-start.6 = (f32[7,8,128]{2,1,0:T(8,128)S(1)}, f32[7,8,128]{2,1,0:T(8,128)S(1)}, u32[]{:S(2)}, u32[]{:S(2)}) collective-permute-start(f32[7,8,128]{2,1,0:T(8,128)S(1)} %shard_map.50._.own_ref), channel_id=1, source_target_pairs={{0,3},{1,2},{2,1},{3,0},{4,7},{5,6},{6,5},{7,4},{8,11},{9,10},{10,... | collective-permute-start | bytes 86024 | tf_op jit(solution)/shard_map/ppermute | solution.py:230
  19.3 1.3 %collective-permute-start.7 = (f32[2,7,8,128]{3,2,1,0:T(8,128)S(1)}, f32[2,7,8,128]{3,2,1,0:T(8,128)S(1)}, u32[]{:S(2)}, u32[]{:S(2)}) collective-permute-start(f32[2,7,8,128]{3,2,1,0:T(8,128)S(1)} %shard_map.52.sent_ref), channel_id=1, source_target_pairs={{0,2},{1,3},{2,0},{3,1},{4,6},{5,7},{6,4},{7,5},{8,10},{9,11},{10,... | collective-permute-start | bytes 172040 | tf_op jit(solution)/shard_map/ppermute | solution.py:230
  21.6 1.2 %collective-permute-start.8 = (f32[10,8,128]{2,1,0:T(8,128)S(1)}, f32[10,8,128]{2,1,0:T(8,128)S(1)}, u32[]{:S(2)}, u32[]{:S(2)}) collective-permute-start(f32[10,8,128]{2,1,0:T(8,128)S(1)} %shard_map.53.mine_ref), channel_id=1, source_target_pairs={{0,2},{1,3},{2,0},{3,1},{4,6},{5,7},{6,4},{7,5},{8,10},{9,11},{10,... | collective-permute-start | bytes 122888 | tf_op jit(solution)/shard_map/ppermute | solution.py:230
  22.8 4.1 %collective-permute-start.10 = (f32[5,8,128]{2,1,0:T(8,128)S(1)}, f32[5,8,128]{2,1,0:T(8,128)S(1)}, u32[]{:S(2)}, u32[]{:S(2)}) collective-permute-start(f32[5,8,128]{2,1,0:T(8,128)S(1)} %get-tuple-element.36), channel_id=1, source_target_pairs={{0,7},{1,6},{2,5},{3,4},{4,3},{5,2},{6,1},{7,0},{8,15},{9,14},{10,... | collective-permute-start | bytes 61448 | tf_op jit(solution)/shard_map/ppermute | solution.py:230
  24.2 3.2 %collective-permute-start.11 = (f32[5,8,128]{2,1,0:T(8,128)S(1)}, f32[5,8,128]{2,1,0:T(8,128)S(1)}, u32[]{:S(2)}, u32[]{:S(2)}) collective-permute-start(f32[5,8,128]{2,1,0:T(8,128)S(1)} %get-tuple-element.36), channel_id=1, source_target_pairs={{0,6},{1,7},{2,4},{3,5},{4,2},{5,3},{6,0},{7,1},{8,14},{9,15},{10,... | collective-permute-start | bytes 61448 | tf_op jit(solution)/shard_map/ppermute | solution.py:230
  24.6 3.2 %collective-permute-start.9 = (f32[5,8,128]{2,1,0:T(8,128)S(1)}, f32[5,8,128]{2,1,0:T(8,128)S(1)}, u32[]{:S(2)}, u32[]{:S(2)}) collective-permute-start(f32[5,8,128]{2,1,0:T(8,128)S(1)} %get-tuple-element.36), channel_id=1, source_target_pairs={{0,3},{1,2},{2,1},{3,0},{4,7},{5,6},{6,5},{7,4},{8,11},{9,10},{10,... | collective-permute-start | bytes 61448 | tf_op jit(solution)/shard_map/ppermute | solution.py:230
  27.8 5.2 %collective-permute-start.12 = (f32[5,8,128]{2,1,0:T(8,128)S(1)}, f32[5,8,128]{2,1,0:T(8,128)S(1)}, u32[]{:S(2)}, u32[]{:S(2)}) collective-permute-start(f32[5,8,128]{2,1,0:T(8,128)S(1)} %shard_map.55.own_ref), channel_id=1, source_target_pairs={{0,10},{1,11},{2,8},{3,9},{4,14},{5,15},{6,12},{7,13},{8,18},{9,19... | collective-permute-start | bytes 61448 | tf_op jit(solution)/shard_map/ppermute | solution.py:230
  28.1 4.9 %collective-permute-start.13 = (f32[5,8,128]{2,1,0:T(8,128)S(1)}, f32[5,8,128]{2,1,0:T(8,128)S(1)}, u32[]{:S(2)}, u32[]{:S(2)}) collective-permute-start(f32[5,8,128]{2,1,0:T(8,128)S(1)} %shard_map.55.own_ref), channel_id=1, source_target_pairs={{0,18},{1,19},{2,16},{3,17},{4,22},{5,23},{6,20},{7,21},{8,26},{9,... | collective-permute-start | bytes 61448 | tf_op jit(solution)/shard_map/ppermute | solution.py:230
  30.1 3.6 %collective-permute-start.14 = (f32[5,8,128]{2,1,0:T(8,128)S(1)}, f32[5,8,128]{2,1,0:T(8,128)S(1)}, u32[]{:S(2)}, u32[]{:S(2)}) collective-permute-start(f32[5,8,128]{2,1,0:T(8,128)S(1)} %shard_map.55.own_ref), channel_id=1, source_target_pairs={{0,26},{1,27},{2,24},{3,25},{4,30},{5,31},{6,28},{7,29},{8,2},{9,3... | collective-permute-start | bytes 61448 | tf_op jit(solution)/shard_map/ppermute | solution.py:230
  32.2 1.5 %collective-permute-start.15 = (f32[5,8,128]{2,1,0:T(8,128)S(1)}, f32[5,8,128]{2,1,0:T(8,128)S(1)}, u32[]{:S(2)}, u32[]{:S(2)}) collective-permute-start(f32[5,8,128]{2,1,0:T(8,128)S(1)} %shard_map.55.own_ref), channel_id=1, source_target_pairs={{0,2},{1,3},{2,0},{3,1},{4,6},{5,7},{6,4},{7,5},{8,10},{9,11},{10,... | collective-permute-start | bytes 61448 | tf_op jit(solution)/shard_map/ppermute | solution.py:230
  33.7 1.3 %collective-permute-start.16 = (f32[3,5,8,128]{3,2,1,0:T(8,128)S(1)}, f32[3,5,8,128]{3,2,1,0:T(8,128)S(1)}, u32[]{:S(2)}, u32[]{:S(2)}) collective-permute-start(f32[3,5,8,128]{3,2,1,0:T(8,128)S(1)} %shard_map.56.others_ref), channel_id=1, source_target_pairs={{0,2},{1,3},{2,0},{3,1},{4,6},{5,7},{6,4},{7,5},{8,10},{9,11},{10,... | collective-permute-start | bytes 184328 | tf_op jit(solution)/shard_map/ppermute | solution.py:230

commit v8 on v7

--- a/solution.py
+++ b/solution.py
@@ -34,6 +34,12 @@
 
 def pick(core, when_zero, when_one):
     return jnp.where(core == 0, when_zero, when_one)
+
+
+def ring_step(e, k, n, where=lambda c, a, b: a if c else b):
+    place = where(e % 2 == 1, (e + 1) // 2, n - e // 2) + k
+    place = where(place >= n, place - n, place)
+    return where(place == 0, 0, where(place <= n // 2, 2 * place - 1, 2 * (n - place)))
 
 
 def join(parts):
@@ -77,7 +83,8 @@
     sums_ref[:, width:width + LANES] = jnp.broadcast_to(mass, (slots, LANES))
     sums_ref[:, width + LANES:] = jnp.broadcast_to(peak, (slots, LANES))
     for k in range(groups):
-        own = pl.ds(pl.multiple_of((expert ^ k) * rows, rows), rows)
+        target = ring_step(expert, k, groups, jnp.where)
+        own = pl.ds(pl.multiple_of(target * rows, rows), rows)
         sides = (core, 1 - core) if k else (1 - core, core)
         for ref, side in zip((mine_ref, theirs_ref), sides):
             for t in range(half):
@@ -190,28 +197,38 @@
         out_ref[t] = out[:, t * LANES:(t + 1) * LANES]
 
 
-def mix_kernel(near, combine_ref, own_ref, others_ref, *refs):
-    out_hbm, slots_ref, out_ref, sems = refs[-4:]
-    core, expert = lax.axis_index("seq") % 2, lax.axis_index("expert")
-    half, rows, _ = own_ref.shape
-    groups = others_ref.shape[0] + 1
-    for k in range(groups):
+def slot_pieces(parts, slots_ref):
+    expert = lax.axis_index("expert")
+    groups, (tiles, rows, _) = len(parts), parts[0].shape
+    for k, part in enumerate(parts):
         place = pl.ds(pl.multiple_of(lax.rem(expert - k + groups, groups) * rows, rows), rows)
-        for t in range(half):
-            slots_ref[place, t * LANES:(t + 1) * LANES] = others_ref[k - 1, t] if k else own_ref[t]
+        for t in range(tiles):
+            slots_ref[place, t * LANES:(t + 1) * LANES] = part[t]
     high, low = pieces(slots_ref[...], 2)
-    slots = jnp.concatenate([high, high, low], axis=0)
-    side = core if near else 1 - core
-    columns = pl.ds(pl.multiple_of(side * (half * LANES), LANES), half * LANES)
-    count = combine_ref.shape[0]
-    step = pl.cdiv(count, 16 * sems.shape[0]) * 16
-    copies = []
+    return jnp.concatenate([high, high, low], axis=0)
+
+
+def near_kernel(combine_ref, *refs):
+    own_ref, others_ref, out_ref, slots_ref = refs
+    parts = [own_ref[...]] + [others_ref[k] for k in range(others_ref.shape[0])]
+    out_ref[...] = mm(combine_ref[...], slot_pieces(parts, slots_ref))
+
+
+def far_kernel(combine_ref, own_ref, others_ref, near_ref, out_hbm, slots_ref, far_ref, sems):
+    core = lax.axis_index("seq") % 2
+    count, half = near_ref.shape
+    columns = [pl.ds(pl.multiple_of(side * half, LANES), half) for side in (core, 1 - core)]
+    copies = [pltpu.make_async_copy(near_ref, out_hbm.at[:, columns[0]], sems.at[0])]
+    copies[0].start()
+    parts = [own_ref[...]] + [others_ref[k] for k in range(others_ref.shape[0])]
+    slots = slot_pieces(parts, slots_ref)
+    step = pl.cdiv(count, 16 * (sems.shape[0] - 1)) * 16
     for i, start in enumerate(range(0, count, step)):
         size = min(step, count - start)
-        out_ref[start:start + size] = mm(combine_ref[start:start + size], slots)
+        far_ref[start:start + size] = mm(combine_ref[start:start + size], slots)
         place = pl.ds(start, size)
-        copies.append(pltpu.make_async_copy(out_ref.at[place], out_hbm.at[place, columns], sems.at[i]))
-        copies[i].start()
+        copies.append(pltpu.make_async_copy(far_ref.at[place], out_hbm.at[place, columns[1]], sems.at[i + 1]))
+        copies[-1].start()
     for copy in copies:
         copy.wait()
 
@@ -232,8 +249,8 @@
     def other_core(value):
         return permute(value, lambda e, x, c, f: (e, x, 1 - c, f))
 
-    def along_expert(value, k):
-        return permute(value, lambda e, x, c, f: (e ^ k, x, 1 - c, f))
+    def along_ring(value, k):
+        return permute(value, lambda e, x, c, f: (ring_step(e, k, n_expert), x, 1 - c, f))
 
     def around_expert(value, k):
         return permute(value, lambda e, x, c, f: ((e + k) % n_expert, x, 1 - c, f))
@@ -284,7 +301,6 @@
             out_specs=(VMEM,) * n_expert,
             compiler_params=params,
         )(mine, other_core(theirs))
-        order = list(range(n_expert - 1, 0, -1))
         flag = pltpu.VMEM((8, LANES), f32)
         experts, units, _ = w_in.shape
         cost = pl.CostEstimate(flops=8 * w_in.size, bytes_accessed=8 * w_in.size, transcendentals=0)
@@ -310,7 +326,7 @@
             compiler_params=params,
         )(chip[0], in_hbm(w_out))
         shape = pltpu.VMEM((half + 2, rows, LANES), f32)
-        total = local(total_kernel, shape, chip[0], *[along_expert(chip[k], k) for k in order], ready)
+        total = local(total_kernel, shape, chip[0], *[along_ring(chip[k], k) for k in range(1, n_expert)], ready)
         part = pltpu.VMEM((width, experts * units), jnp.bfloat16)
         in_high, in_low, ready = pl.pallas_call(
             split_in_kernel,
@@ -332,24 +348,24 @@
         own_near = other_core(own)
         shape = pltpu.VMEM((n_expert - 1, half, rows, LANES), f32)
         others = local(stack_kernel, shape, combine, *arrived, own_near)
-
-        def mix(near, own, others, *out):
-            return pl.pallas_call(
-                functools.partial(mix_kernel, near),
-                out_shape=jax.ShapeDtypeStruct((count, width), f32),
-                in_specs=[VMEM, VMEM, VMEM] + [HBM] * len(out),
-                out_specs=HBM,
-                scratch_shapes=[
-                    pltpu.VMEM((slots, half * LANES), f32),
-                    pltpu.VMEM((count, half * LANES), f32),
-                    pltpu.SemaphoreType.DMA((4,)),
-                ],
-                input_output_aliases={3: 0} if out else {},
-                compiler_params=params,
-            )(combine, own, others, *out)
-
-        mixed = mix(True, own_near, others)
-        return mix(False, own, other_core(others), mixed)
+        whole = pltpu.VMEM((count, half * LANES), f32)
+        slot_values = pltpu.VMEM((slots, half * LANES), f32)
+        near = pl.pallas_call(
+            near_kernel,
+            out_shape=whole,
+            in_specs=[VMEM] * 3,
+            out_specs=VMEM,
+            scratch_shapes=[slot_values],
+            compiler_params=params,
+        )(combine, own_near, others)
+        return pl.pallas_call(
+            far_kernel,
+            out_shape=jax.ShapeDtypeStruct((count, width), f32),
+            in_specs=[VMEM] * 4,
+            out_specs=HBM,
+            scratch_shapes=[slot_values, whole, pltpu.SemaphoreType.DMA((5,))],
+            compiler_params=params,
+        )(combine, own, other_core(others), near)
 
     return jax.shard_map(
         body,

time: 36.1 us -> 36.1 us (level)
  Pallas kernels: 8.87 us -> 8.13 us
  waiting for transfers between devices: 9.17 us -> 9.57 us
    pallas_call x2, Pallas kernels: 2.03 us -> 1.29 us  [the longest x1 1.05 us: body(): pl.pallas_call(far_kernel, out_shape=jax.ShapeDtypeStruct((count, width),...]
    ppermute x17, waiting for transfers between devices: 9.17 us -> 9.57 us  [permute(): return lax.ppermute(value, AXES, pairs)]
  transfers between devices with their start and end apart: 17 -> 17, of which waited for: 13 -> 13; matrix products, arithmetic and copies ran while one was open for 0% -> 0% of each run, Pallas kernels for 11% -> 9%
where the time goes in v8:
time: 36.1 us; the launch traced here: 36 us
  starting transfers between devices  18.2 us (50%)
  waiting for transfers between devices  9.57 us (27%)
  Pallas kernels  8.13 us (23%)
    ppermute x17, starting transfers between devices, permute(): return lax.ppermute(value, AXES, pairs)  18.2 us
    ppermute x17, waiting for transfers between devices, permute(): return lax.ppermute(value, AXES, pairs)  9.57 us
    pallas_call x1, Pallas kernels, body(): pl.pallas_call(functools.partial(dispatch_kernel, chunks), out_shape=(plt...  2.65 us
    pallas_call x1, Pallas kernels, body(): pl.pallas_call(split_out_kernel, out_shape=(part, part, flag), in_specs=[...  2 us
    pallas_call x6, Pallas kernels, local(): pl.pallas_call(kernel, out_shape=out, in_specs=[VMEM] * len(args), out_sp...  1.07 us
    pallas_call x1, Pallas kernels, body(): pl.pallas_call(far_kernel, out_shape=jax.ShapeDtypeStruct((count, width),...  1.05 us
    pallas_call x1, Pallas kernels, body(): pl.pallas_call(split_in_kernel, out_shape=(part, part, flag), in_specs=[V...  0.89 us
  transfers between devices with their start and end apart: 17, of which 13 were waited for; matrix products, arithmetic and copies ran while one was open for 0% of the time, Pallas kernels for 9%

profile of v8, /device:TPU:0, one launch (start us, length us, event | category | flops | bytes accessed | tf_op | source)
XLA Modules:
  0.0 36.0 jit_solution(14377585115562355087)
XLA Ops:
  0.0 2.6 %shard_map.46 = (f32[32,224]{1,0:T(8,128)S(1)}, f32[4,7,8,128]{3,2,1,0:T(8,128)S(1)}, f32[4,7,8,128]{3,2,1,0:T(8,128)S(1)}, f32[2,320,1280]{2,1,0:T(8,128)S(1)}) custom-call(f32[224,1280]{1,0:T(8,128)} %tokens_hbm.1, f32[32,1280]{1,0:T(8,128)} %bitcast.1, f32[2,320,1280]{2,1,0:T(8,128)} %w_in_hbm.1), custom_call_target="tpu_custom_call" | custom-call | tf_op jit(solution)/shard_map/pallas_call | solution.py:276
  2.7 0.5 %collective-permute-start = (f32[4,7,8,128]{3,2,1,0:T(8,128)S(1)}, f32[4,7,8,128]{3,2,1,0:T(8,128)S(1)}, u32[]{:S(2)}, u32[]{:S(2)}) collective-permute-start(f32[4,7,8,128]{3,2,1,0:T(8,128)S(1)} %get-tuple-element.23), channel_id=1, source_target_pairs={{0,2},{1,3},{2,0},{3,1},{4,6},{5,7},{6,4},{7,5},{8,10},{9,11},{10,... | collective-permute-start | bytes 344072 | tf_op jit(solution)/shard_map/ppermute | solution.py:247
  3.2 1.0 %collective-permute-done.theirs_ref = f32[4,7,8,128]{3,2,1,0:T(8,128)S(1)} collective-permute-done((f32[4,7,8,128]{3,2,1,0:T(8,128)S(1)}, f32[4,7,8,128]{3,2,1,0:T(8,128)S(1)}, u32[]{:S(2)}, u32[]{:S(2)}) %collective-permute-start) | collective-permute-done | bytes 114720 | tf_op jit(solution)/shard_map/ppermute | solution.py:247
  4.2 2.7 %collective-permute-start.1 = (f32[7,8,128]{2,1,0:T(8,128)S(1)}, f32[7,8,128]{2,1,0:T(8,128)S(1)}, u32[]{:S(2)}, u32[]{:S(2)}) collective-permute-start(f32[7,8,128]{2,1,0:T(8,128)S(1)} %get-tuple-element.25), channel_id=1, source_target_pairs={{0,10},{1,11},{2,8},{3,9},{4,14},{5,15},{6,12},{7,13},{8,26},{9,27... | collective-permute-start | bytes 86024 | tf_op jit(solution)/shard_map/ppermute | solution.py:247
  6.9 2.4 %collective-permute-start.2 = (f32[7,8,128]{2,1,0:T(8,128)S(1)}, f32[7,8,128]{2,1,0:T(8,128)S(1)}, u32[]{:S(2)}, u32[]{:S(2)}) collective-permute-start(f32[7,8,128]{2,1,0:T(8,128)S(1)} %get-tuple-element.26), channel_id=1, source_target_pairs={{0,26},{1,27},{2,24},{3,25},{4,30},{5,31},{6,28},{7,29},{8,18},{9,... | collective-permute-start | bytes 86024 | tf_op jit(solution)/shard_map/ppermute | solution.py:247
  9.3 1.3 %collective-permute-start.3 = (f32[7,8,128]{2,1,0:T(8,128)S(1)}, f32[7,8,128]{2,1,0:T(8,128)S(1)}, u32[]{:S(2)}, u32[]{:S(2)}) collective-permute-start(f32[7,8,128]{2,1,0:T(8,128)S(1)} %get-tuple-element.27), channel_id=1, source_target_pairs={{0,18},{1,19},{2,16},{3,17},{4,22},{5,23},{6,20},{7,21},{8,2},{9,3... | collective-permute-start | bytes 86024 | tf_op jit(solution)/shard_map/ppermute | solution.py:247
  10.7 2.0 %shard_map.49 = (bf16[640,1280]{1,0:T(8,128)(2,1)S(1)}, bf16[640,1280]{1,0:T(8,128)(2,1)S(1)}, f32[8,128]{1,0:T(8,128)S(1)}) custom-call(f32[7,8,128]{2,1,0:T(8,128)S(1)} %get-tuple-element.24._.own_ref, f32[2,320,1280]{2,1,0:T(8,128)} %w_hbm.1), custom_call_target="tpu_custom_call" | custom-call | flops 6553600 | bytes 6553600 | tf_op jit(solution)/shard_map/pallas_call | solution.py:319
  13.1 2.2 %collective-permute-start.4 = (f32[7,8,128]{2,1,0:T(8,128)S(1)}, f32[7,8,128]{2,1,0:T(8,128)S(1)}, u32[]{:S(2)}, u32[]{:S(2)}) collective-permute-start(f32[7,8,128]{2,1,0:T(8,128)S(1)} %shard_map.50._.own_ref), channel_id=1, source_target_pairs={{0,7},{1,6},{2,5},{3,4},{4,3},{5,2},{6,1},{7,0},{8,15},{9,14},{10,... | collective-permute-start | bytes 86024 | tf_op jit(solution)/shard_map/ppermute | solution.py:247
  15.3 0.6 %collective-permute-start.5 = (f32[7,8,128]{2,1,0:T(8,128)S(1)}, f32[7,8,128]{2,1,0:T(8,128)S(1)}, u32[]{:S(2)}, u32[]{:S(2)}) collective-permute-start(f32[7,8,128]{2,1,0:T(8,128)S(1)} %shard_map.50._.own_ref), channel_id=1, source_target_pairs={{0,6},{1,7},{2,4},{3,5},{4,2},{5,3},{6,0},{7,1},{8,14},{9,15},{10,... | collective-permute-start | bytes 86024 | tf_op jit(solution)/shard_map/ppermute | solution.py:247
  16.1 0.9 %shard_map.51 = (bf16[1280,640]{1,0:T(8,128)(2,1)S(1)}, bf16[1280,640]{1,0:T(8,128)(2,1)S(1)}, f32[8,128]{1,0:T(8,128)S(1)}) custom-call(f32[7,8,128]{2,1,0:T(8,128)S(1)} %shard_map.50._.own_ref, f32[2,320,1280]{2,1,0:T(8,128)S(1)} %get-tuple-element.29.w_ref), custom_call_target="tpu_custom_call" | custom-call | flops 6553600 | bytes 6553600 | tf_op jit(solution)/shard_map/pallas_call | solution.py:331
  17.3 1.2 %collective-permute-done.5.refs_1_ = f32[7,8,128]{2,1,0:T(8,128)S(1)} collective-permute-done((f32[7,8,128]{2,1,0:T(8,128)S(1)}, f32[7,8,128]{2,1,0:T(8,128)S(1)}, u32[]{:S(2)}, u32[]{:S(2)}) %collective-permute-start.5) | collective-permute-done | bytes 28704 | tf_op jit(solution)/shard_map/ppermute | solution.py:247
  18.6 0.6 %collective-permute-done.6.refs_2_ = f32[7,8,128]{2,1,0:T(8,128)S(1)} collective-permute-done((f32[7,8,128]{2,1,0:T(8,128)S(1)}, f32[7,8,128]{2,1,0:T(8,128)S(1)}, u32[]{:S(2)}, u32[]{:S(2)}) %collective-permute-start.6) | collective-permute-done | bytes 28704 | tf_op jit(solution)/shard_map/ppermute | solution.py:247
  19.4 1.1 %collective-permute-done.7.got_ref = f32[2,7,8,128]{3,2,1,0:T(8,128)S(1)} collective-permute-done((f32[2,7,8,128]{3,2,1,0:T(8,128)S(1)}, f32[2,7,8,128]{3,2,1,0:T(8,128)S(1)}, u32[]{:S(2)}, u32[]{:S(2)}) %collective-permute-start.7) | collective-permute-done | bytes 57376 | tf_op jit(solution)/shard_map/ppermute | solution.py:247
  20.5 1.0 %shard_map.53.mine_ref = f32[10,8,128]{2,1,0:T(8,128)S(1)} custom-call(f32[2,7,8,128]{3,2,1,0:T(8,128)S(1)} %shard_map.52.sent_ref, f32[2,7,8,128]{3,2,1,0:T(8,128)S(1)} %collective-permute-done.7.got_ref, bf16[1280,640]{1,0:T(8,128)(2,1)S(1)} %get-tuple-element.31.in_high_ref, bf16[1280,640]{1,0:T(8,128)(2,1)S(1)} %get-tuple-element.32.in_low_ref, ...), custom_call_target="tpu_custom_call" | custom-call | tf_op jit(solution)/shard_map/pallas_call | solution.py:309
  21.7 1.1 %collective-permute-done.8.theirs_ref = f32[10,8,128]{2,1,0:T(8,128)S(1)} collective-permute-done((f32[10,8,128]{2,1,0:T(8,128)S(1)}, f32[10,8,128]{2,1,0:T(8,128)S(1)}, u32[]{:S(2)}, u32[]{:S(2)}) %collective-permute-start.8) | collective-permute-done | bytes 40992 | tf_op jit(solution)/shard_map/ppermute | solution.py:247
  22.8 1.3 %collective-permute-start.10 = (f32[5,8,128]{2,1,0:T(8,128)S(1)}, f32[5,8,128]{2,1,0:T(8,128)S(1)}, u32[]{:S(2)}, u32[]{:S(2)}) collective-permute-start(f32[5,8,128]{2,1,0:T(8,128)S(1)} %get-tuple-element.36), channel_id=1, source_target_pairs={{0,7},{1,6},{2,5},{3,4},{4,3},{5,2},{6,1},{7,0},{8,15},{9,14},{10,... | collective-permute-start | bytes 61448 | tf_op jit(solution)/shard_map/ppermute | solution.py:247
  24.5 1.3 %collective-permute-start.9 = (f32[5,8,128]{2,1,0:T(8,128)S(1)}, f32[5,8,128]{2,1,0:T(8,128)S(1)}, u32[]{:S(2)}, u32[]{:S(2)}) collective-permute-start(f32[5,8,128]{2,1,0:T(8,128)S(1)} %get-tuple-element.36), channel_id=1, source_target_pairs={{0,3},{1,2},{2,1},{3,0},{4,7},{5,6},{6,5},{7,4},{8,11},{9,10},{10,... | collective-permute-start | bytes 61448 | tf_op jit(solution)/shard_map/ppermute | solution.py:247
  25.7 1.1 %collective-permute-done.10.refs_1_ = f32[5,8,128]{2,1,0:T(8,128)S(1)} collective-permute-done((f32[5,8,128]{2,1,0:T(8,128)S(1)}, f32[5,8,128]{2,1,0:T(8,128)S(1)}, u32[]{:S(2)}, u32[]{:S(2)}) %collective-permute-start.10) | collective-permute-done | bytes 20512 | tf_op jit(solution)/shard_map/ppermute | solution.py:247
  27.7 0.6 %collective-permute-start.12 = (f32[5,8,128]{2,1,0:T(8,128)S(1)}, f32[5,8,128]{2,1,0:T(8,128)S(1)}, u32[]{:S(2)}, u32[]{:S(2)}) collective-permute-start(f32[5,8,128]{2,1,0:T(8,128)S(1)} %shard_map.55.own_ref), channel_id=1, source_target_pairs={{0,10},{1,11},{2,8},{3,9},{4,14},{5,15},{6,12},{7,13},{8,18},{9,19... | collective-permute-start | bytes 61448 | tf_op jit(solution)/shard_map/ppermute | solution.py:247
  28.3 1.3 %collective-permute-start.13 = (f32[5,8,128]{2,1,0:T(8,128)S(1)}, f32[5,8,128]{2,1,0:T(8,128)S(1)}, u32[]{:S(2)}, u32[]{:S(2)}) collective-permute-start(f32[5,8,128]{2,1,0:T(8,128)S(1)} %shard_map.55.own_ref), channel_id=1, source_target_pairs={{0,18},{1,19},{2,16},{3,17},{4,22},{5,23},{6,20},{7,21},{8,26},{9,... | collective-permute-start | bytes 61448 | tf_op jit(solution)/shard_map/ppermute | solution.py:247
  29.6 2.6 %collective-permute-start.14 = (f32[5,8,128]{2,1,0:T(8,128)S(1)}, f32[5,8,128]{2,1,0:T(8,128)S(1)}, u32[]{:S(2)}, u32[]{:S(2)}) collective-permute-start(f32[5,8,128]{2,1,0:T(8,128)S(1)} %shard_map.55.own_ref), channel_id=1, source_target_pairs={{0,26},{1,27},{2,24},{3,25},{4,30},{5,31},{6,28},{7,29},{8,2},{9,3... | collective-permute-start | bytes 61448 | tf_op jit(solution)/shard_map/ppermute | solution.py:247
  32.8 0.9 %collective-permute-done.14.refs_3_ = f32[5,8,128]{2,1,0:T(8,128)S(1)} collective-permute-done((f32[5,8,128]{2,1,0:T(8,128)S(1)}, f32[5,8,128]{2,1,0:T(8,128)S(1)}, u32[]{:S(2)}, u32[]{:S(2)}) %collective-permute-start.14) | collective-permute-done | bytes 20512 | tf_op jit(solution)/shard_map/ppermute | solution.py:247
  34.0 1.0 %collective-permute-done.16.others_ref = f32[3,5,8,128]{3,2,1,0:T(8,128)S(1)} collective-permute-done((f32[3,5,8,128]{3,2,1,0:T(8,128)S(1)}, f32[3,5,8,128]{3,2,1,0:T(8,128)S(1)}, u32[]{:S(2)}, u32[]{:S(2)}) %collective-permute-start.16) | collective-permute-done | bytes 61472 | tf_op jit(solution)/shard_map/ppermute | solution.py:247
  35.0 1.0 %shard_map.58 = f32[224,1280]{1,0:T(8,128)} custom-call(bf16[224,96]{1,0:T(8,128)(2,1)S(1)} %shard_map.47.refs_0_.combine_ref, f32[5,8,128]{2,1,0:T(8,128)S(1)} %shard_map.55.own_ref, f32[3,5,8,128]{3,2,1,0:T(8,128)S(1)} %collective-permute-done.16.others_ref, f32[224,640]{1,0:T(8,128)S(1)} %shard_map.57.near_ref), custom_call_target="tpu_custom_call" | custom-call | tf_op jit(solution)/shard_map/pallas_call | solution.py:361
  (23 shorter events, 3.5 us)
Async XLA Ops:
  2.7 1.5 %collective-permute-start = (f32[4,7,8,128]{3,2,1,0:T(8,128)S(1)}, f32[4,7,8,128]{3,2,1,0:T(8,128)S(1)}, u32[]{:S(2)}, u32[]{:S(2)}) collective-permute-start(f32[4,7,8,128]{3,2,1,0:T(8,128)S(1)} %get-tuple-element.23), channel_id=1, source_target_pairs={{0,2},{1,3},{2,0},{3,1},{4,6},{5,7},{6,4},{7,5},{8,10},{9,11},{10,... | collective-permute-start | bytes 344072 | tf_op jit(solution)/shard_map/ppermute | solution.py:247
  4.2 8.5 %collective-permute-start.1 = (f32[7,8,128]{2,1,0:T(8,128)S(1)}, f32[7,8,128]{2,1,0:T(8,128)S(1)}, u32[]{:S(2)}, u32[]{:S(2)}) collective-permute-start(f32[7,8,128]{2,1,0:T(8,128)S(1)} %get-tuple-element.25), channel_id=1, source_target_pairs={{0,10},{1,11},{2,8},{3,9},{4,14},{5,15},{6,12},{7,13},{8,26},{9,27... | collective-permute-start | bytes 86024 | tf_op jit(solution)/shard_map/ppermute | solution.py:247
  6.9 5.8 %collective-permute-start.2 = (f32[7,8,128]{2,1,0:T(8,128)S(1)}, f32[7,8,128]{2,1,0:T(8,128)S(1)}, u32[]{:S(2)}, u32[]{:S(2)}) collective-permute-start(f32[7,8,128]{2,1,0:T(8,128)S(1)} %get-tuple-element.26), channel_id=1, source_target_pairs={{0,26},{1,27},{2,24},{3,25},{4,30},{5,31},{6,28},{7,29},{8,18},{9,... | collective-permute-start | bytes 86024 | tf_op jit(solution)/shard_map/ppermute | solution.py:247
  9.3 3.7 %collective-permute-start.3 = (f32[7,8,128]{2,1,0:T(8,128)S(1)}, f32[7,8,128]{2,1,0:T(8,128)S(1)}, u32[]{:S(2)}, u32[]{:S(2)}) collective-permute-start(f32[7,8,128]{2,1,0:T(8,128)S(1)} %get-tuple-element.27), channel_id=1, source_target_pairs={{0,18},{1,19},{2,16},{3,17},{4,22},{5,23},{6,20},{7,21},{8,2},{9,3... | collective-permute-start | bytes 86024 | tf_op jit(solution)/shard_map/ppermute | solution.py:247
  13.1 4.3 %collective-permute-start.4 = (f32[7,8,128]{2,1,0:T(8,128)S(1)}, f32[7,8,128]{2,1,0:T(8,128)S(1)}, u32[]{:S(2)}, u32[]{:S(2)}) collective-permute-start(f32[7,8,128]{2,1,0:T(8,128)S(1)} %shard_map.50._.own_ref), channel_id=1, source_target_pairs={{0,7},{1,6},{2,5},{3,4},{4,3},{5,2},{6,1},{7,0},{8,15},{9,14},{10,... | collective-permute-start | bytes 86024 | tf_op jit(solution)/shard_map/ppermute | solution.py:247
  15.3 3.3 %collective-permute-start.5 = (f32[7,8,128]{2,1,0:T(8,128)S(1)}, f32[7,8,128]{2,1,0:T(8,128)S(1)}, u32[]{:S(2)}, u32[]{:S(2)}) collective-permute-start(f32[7,8,128]{2,1,0:T(8,128)S(1)} %shard_map.50._.own_ref), channel_id=1, source_target_pairs={{0,6},{1,7},{2,4},{3,5},{4,2},{5,3},{6,0},{7,1},{8,14},{9,15},{10,... | collective-permute-start | bytes 86024 | tf_op jit(solution)/shard_map/ppermute | solution.py:247
  15.8 3.3 %collective-permute-start.6 = (f32[7,8,128]{2,1,0:T(8,128)S(1)}, f32[7,8,128]{2,1,0:T(8,128)S(1)}, u32[]{:S(2)}, u32[]{:S(2)}) collective-permute-start(f32[7,8,128]{2,1,0:T(8,128)S(1)} %shard_map.50._.own_ref), channel_id=1, source_target_pairs={{0,3},{1,2},{2,1},{3,0},{4,7},{5,6},{6,5},{7,4},{8,11},{9,10},{10,... | collective-permute-start | bytes 86024 | tf_op jit(solution)/shard_map/ppermute | solution.py:247
  19.2 1.3 %collective-permute-start.7 = (f32[2,7,8,128]{3,2,1,0:T(8,128)S(1)}, f32[2,7,8,128]{3,2,1,0:T(8,128)S(1)}, u32[]{:S(2)}, u32[]{:S(2)}) collective-permute-start(f32[2,7,8,128]{3,2,1,0:T(8,128)S(1)} %shard_map.52.sent_ref), channel_id=1, source_target_pairs={{0,2},{1,3},{2,0},{3,1},{4,6},{5,7},{6,4},{7,5},{8,10},{9,11},{10,... | collective-permute-start | bytes 172040 | tf_op jit(solution)/shard_map/ppermute | solution.py:247
  21.5 1.2 %collective-permute-start.8 = (f32[10,8,128]{2,1,0:T(8,128)S(1)}, f32[10,8,128]{2,1,0:T(8,128)S(1)}, u32[]{:S(2)}, u32[]{:S(2)}) collective-permute-start(f32[10,8,128]{2,1,0:T(8,128)S(1)} %shard_map.53.mine_ref), channel_id=1, source_target_pairs={{0,2},{1,3},{2,0},{3,1},{4,6},{5,7},{6,4},{7,5},{8,10},{9,11},{10,... | collective-permute-start | bytes 122888 | tf_op jit(solution)/shard_map/ppermute | solution.py:247
  22.8 4.1 %collective-permute-start.10 = (f32[5,8,128]{2,1,0:T(8,128)S(1)}, f32[5,8,128]{2,1,0:T(8,128)S(1)}, u32[]{:S(2)}, u32[]{:S(2)}) collective-permute-start(f32[5,8,128]{2,1,0:T(8,128)S(1)} %get-tuple-element.36), channel_id=1, source_target_pairs={{0,7},{1,6},{2,5},{3,4},{4,3},{5,2},{6,1},{7,0},{8,15},{9,14},{10,... | collective-permute-start | bytes 61448 | tf_op jit(solution)/shard_map/ppermute | solution.py:247
  24.0 3.2 %collective-permute-start.11 = (f32[5,8,128]{2,1,0:T(8,128)S(1)}, f32[5,8,128]{2,1,0:T(8,128)S(1)}, u32[]{:S(2)}, u32[]{:S(2)}) collective-permute-start(f32[5,8,128]{2,1,0:T(8,128)S(1)} %get-tuple-element.36), channel_id=1, source_target_pairs={{0,6},{1,7},{2,4},{3,5},{4,2},{5,3},{6,0},{7,1},{8,14},{9,15},{10,... | collective-permute-start | bytes 61448 | tf_op jit(solution)/shard_map/ppermute | solution.py:247
  24.5 3.2 %collective-permute-start.9 = (f32[5,8,128]{2,1,0:T(8,128)S(1)}, f32[5,8,128]{2,1,0:T(8,128)S(1)}, u32[]{:S(2)}, u32[]{:S(2)}) collective-permute-start(f32[5,8,128]{2,1,0:T(8,128)S(1)} %get-tuple-element.36), channel_id=1, source_target_pairs={{0,3},{1,2},{2,1},{3,0},{4,7},{5,6},{6,5},{7,4},{8,11},{9,10},{10,... | collective-permute-start | bytes 61448 | tf_op jit(solution)/shard_map/ppermute | solution.py:247
  27.7 5.1 %collective-permute-start.12 = (f32[5,8,128]{2,1,0:T(8,128)S(1)}, f32[5,8,128]{2,1,0:T(8,128)S(1)}, u32[]{:S(2)}, u32[]{:S(2)}) collective-permute-start(f32[5,8,128]{2,1,0:T(8,128)S(1)} %shard_map.55.own_ref), channel_id=1, source_target_pairs={{0,10},{1,11},{2,8},{3,9},{4,14},{5,15},{6,12},{7,13},{8,18},{9,19... | collective-permute-start | bytes 61448 | tf_op jit(solution)/shard_map/ppermute | solution.py:247
  28.3 4.5 %collective-permute-start.13 = (f32[5,8,128]{2,1,0:T(8,128)S(1)}, f32[5,8,128]{2,1,0:T(8,128)S(1)}, u32[]{:S(2)}, u32[]{:S(2)}) collective-permute-start(f32[5,8,128]{2,1,0:T(8,128)S(1)} %shard_map.55.own_ref), channel_id=1, source_target_pairs={{0,18},{1,19},{2,16},{3,17},{4,22},{5,23},{6,20},{7,21},{8,26},{9,... | collective-permute-start | bytes 61448 | tf_op jit(solution)/shard_map/ppermute | solution.py:247
  29.6 4.0 %collective-permute-start.14 = (f32[5,8,128]{2,1,0:T(8,128)S(1)}, f32[5,8,128]{2,1,0:T(8,128)S(1)}, u32[]{:S(2)}, u32[]{:S(2)}) collective-permute-start(f32[5,8,128]{2,1,0:T(8,128)S(1)} %shard_map.55.own_ref), channel_id=1, source_target_pairs={{0,26},{1,27},{2,24},{3,25},{4,30},{5,31},{6,28},{7,29},{8,2},{9,3... | collective-permute-start | bytes 61448 | tf_op jit(solution)/shard_map/ppermute | solution.py:247
  32.1 1.5 %collective-permute-start.15 = (f32[5,8,128]{2,1,0:T(8,128)S(1)}, f32[5,8,128]{2,1,0:T(8,128)S(1)}, u32[]{:S(2)}, u32[]{:S(2)}) collective-permute-start(f32[5,8,128]{2,1,0:T(8,128)S(1)} %shard_map.55.own_ref), channel_id=1, source_target_pairs={{0,2},{1,3},{2,0},{3,1},{4,6},{5,7},{6,4},{7,5},{8,10},{9,11},{10,... | collective-permute-start | bytes 61448 | tf_op jit(solution)/shard_map/ppermute | solution.py:247
  33.6 1.3 %collective-permute-start.16 = (f32[3,5,8,128]{3,2,1,0:T(8,128)S(1)}, f32[3,5,8,128]{3,2,1,0:T(8,128)S(1)}, u32[]{:S(2)}, u32[]{:S(2)}) collective-permute-start(f32[3,5,8,128]{3,2,1,0:T(8,128)S(1)} %shard_map.56.refs_1_), channel_id=1, source_target_pairs={{0,2},{1,3},{2,0},{3,1},{4,6},{5,7},{6,4},{7,5},{8,10},{9,11},{10,... | collective-permute-start | bytes 184328 | tf_op jit(solution)/shard_map/ppermute | solution.py:247

commit v9 on v7

--- a/solution.py
+++ b/solution.py
@@ -284,7 +284,7 @@
             out_specs=(VMEM,) * n_expert,
             compiler_params=params,
         )(mine, other_core(theirs))
-        order = list(range(n_expert - 1, 0, -1))
+        order = sorted(range(n_expert - 1, 0, -1), key=lambda k: k != n_expert // 2)
         flag = pltpu.VMEM((8, LANES), f32)
         experts, units, _ = w_in.shape
         cost = pl.CostEstimate(flops=8 * w_in.size, bytes_accessed=8 * w_in.size, transcendentals=0)

time: 36.1 us -> 36.1 us (level)
  starting transfers between devices: 17.9 us -> 17.5 us
  waiting for transfers between devices: 9.17 us -> 9.56 us
    ppermute x17, waiting for transfers between devices: 9.17 us -> 9.56 us  [permute(): return lax.ppermute(value, AXES, pairs)]
    ppermute x17, starting transfers between devices: 17.9 us -> 17.5 us  [permute(): return lax.ppermute(value, AXES, pairs)]
  transfers between devices with their start and end apart: 17 -> 17, of which waited for: 13 -> 12; matrix products, arithmetic and copies ran while one was open for 0% -> 0% of each run, Pallas kernels for 11% -> 11%
where the time goes in v9:
time: 36.1 us; the launch traced here: 36 us
  starting transfers between devices  17.5 us (48%)
  waiting for transfers between devices  9.56 us (26%)
  Pallas kernels  8.85 us (25%)
    ppermute x17, starting transfers between devices, permute(): return lax.ppermute(value, AXES, pairs)  17.5 us
    ppermute x17, waiting for transfers between devices, permute(): return lax.ppermute(value, AXES, pairs)  9.56 us
    pallas_call x1, Pallas kernels, body(): pl.pallas_call(functools.partial(dispatch_kernel, chunks), out_shape=(plt...  2.64 us
    pallas_call x2, Pallas kernels, mix(): pl.pallas_call(functools.partial(mix_kernel, near), out_shape=jax.ShapeDt...  2.02 us
    pallas_call x1, Pallas kernels, body(): pl.pallas_call(split_out_kernel, out_shape=(part, part, flag), in_specs=[...  2 us
    pallas_call x6, Pallas kernels, local(): pl.pallas_call(kernel, out_shape=out, in_specs=[VMEM] * len(args), out_sp...  1.07 us
    pallas_call x1, Pallas kernels, body(): pl.pallas_call(split_in_kernel, out_shape=(part, part, flag), in_specs=[V...  0.89 us
  transfers between devices with their start and end apart: 17, of which 12 were waited for; matrix products, arithmetic and copies ran while one was open for 0% of the time, Pallas kernels for 11%

profile of v9, /device:TPU:0, one launch (start us, length us, event | category | flops | bytes accessed | tf_op | source)
XLA Modules:
  0.0 36.0 jit_solution(14252017158861274434)
XLA Ops:
  0.0 2.6 %shard_map.46 = (f32[32,224]{1,0:T(8,128)S(1)}, f32[4,7,8,128]{3,2,1,0:T(8,128)S(1)}, f32[4,7,8,128]{3,2,1,0:T(8,128)S(1)}, f32[2,320,1280]{2,1,0:T(8,128)S(1)}) custom-call(f32[224,1280]{1,0:T(8,128)} %tokens_hbm.1, f32[32,1280]{1,0:T(8,128)} %bitcast.1, f32[2,320,1280]{2,1,0:T(8,128)} %w_in_hbm.1), custom_call_target="tpu_custom_call" | custom-call | tf_op jit(solution)/shard_map/pallas_call | solution.py:259
  2.7 0.5 %collective-permute-start = (f32[4,7,8,128]{3,2,1,0:T(8,128)S(1)}, f32[4,7,8,128]{3,2,1,0:T(8,128)S(1)}, u32[]{:S(2)}, u32[]{:S(2)}) collective-permute-start(f32[4,7,8,128]{3,2,1,0:T(8,128)S(1)} %get-tuple-element.23), channel_id=1, source_target_pairs={{0,2},{1,3},{2,0},{3,1},{4,6},{5,7},{6,4},{7,5},{8,10},{9,11},{10,... | collective-permute-start | bytes 344072 | tf_op jit(solution)/shard_map/ppermute | solution.py:230
  3.2 1.0 %collective-permute-done.theirs_ref = f32[4,7,8,128]{3,2,1,0:T(8,128)S(1)} collective-permute-done((f32[4,7,8,128]{3,2,1,0:T(8,128)S(1)}, f32[4,7,8,128]{3,2,1,0:T(8,128)S(1)}, u32[]{:S(2)}, u32[]{:S(2)}) %collective-permute-start) | collective-permute-done | bytes 114720 | tf_op jit(solution)/shard_map/ppermute | solution.py:230
  4.2 3.8 %collective-permute-start.1 = (f32[7,8,128]{2,1,0:T(8,128)S(1)}, f32[7,8,128]{2,1,0:T(8,128)S(1)}, u32[]{:S(2)}, u32[]{:S(2)}) collective-permute-start(f32[7,8,128]{2,1,0:T(8,128)S(1)} %get-tuple-element.25), channel_id=1, source_target_pairs={{0,18},{1,19},{2,16},{3,17},{4,22},{5,23},{6,20},{7,21},{8,26},{9,... | collective-permute-start | bytes 86024 | tf_op jit(solution)/shard_map/ppermute | solution.py:230
  7.9 1.3 %collective-permute-start.2 = (f32[7,8,128]{2,1,0:T(8,128)S(1)}, f32[7,8,128]{2,1,0:T(8,128)S(1)}, u32[]{:S(2)}, u32[]{:S(2)}) collective-permute-start(f32[7,8,128]{2,1,0:T(8,128)S(1)} %get-tuple-element.26), channel_id=1, source_target_pairs={{0,26},{1,27},{2,24},{3,25},{4,30},{5,31},{6,28},{7,29},{8,18},{9,... | collective-permute-start | bytes 86024 | tf_op jit(solution)/shard_map/ppermute | solution.py:230
  9.5 2.0 %shard_map.49 = (bf16[640,1280]{1,0:T(8,128)(2,1)S(1)}, bf16[640,1280]{1,0:T(8,128)(2,1)S(1)}, f32[8,128]{1,0:T(8,128)S(1)}) custom-call(f32[7,8,128]{2,1,0:T(8,128)S(1)} %get-tuple-element.24._.own_ref, f32[2,320,1280]{2,1,0:T(8,128)} %w_hbm.1), custom_call_target="tpu_custom_call" | custom-call | flops 6553600 | bytes 6553600 | tf_op jit(solution)/shard_map/pallas_call | solution.py:303
  11.5 1.6 %collective-permute-done.2.refs_1_ = f32[7,8,128]{2,1,0:T(8,128)S(1)} collective-permute-done((f32[7,8,128]{2,1,0:T(8,128)S(1)}, f32[7,8,128]{2,1,0:T(8,128)S(1)}, u32[]{:S(2)}, u32[]{:S(2)}) %collective-permute-start.2) | collective-permute-done | bytes 28704 | tf_op jit(solution)/shard_map/ppermute | solution.py:230
  13.2 2.6 %collective-permute-start.4 = (f32[7,8,128]{2,1,0:T(8,128)S(1)}, f32[7,8,128]{2,1,0:T(8,128)S(1)}, u32[]{:S(2)}, u32[]{:S(2)}) collective-permute-start(f32[7,8,128]{2,1,0:T(8,128)S(1)} %shard_map.50._.own_ref), channel_id=1, source_target_pairs={{0,7},{1,6},{2,5},{3,4},{4,3},{5,2},{6,1},{7,0},{8,15},{9,14},{10,... | collective-permute-start | bytes 86024 | tf_op jit(solution)/shard_map/ppermute | solution.py:230
  15.9 0.6 %collective-permute-start.6 = (f32[7,8,128]{2,1,0:T(8,128)S(1)}, f32[7,8,128]{2,1,0:T(8,128)S(1)}, u32[]{:S(2)}, u32[]{:S(2)}) collective-permute-start(f32[7,8,128]{2,1,0:T(8,128)S(1)} %shard_map.50._.own_ref), channel_id=1, source_target_pairs={{0,3},{1,2},{2,1},{3,0},{4,7},{5,6},{6,5},{7,4},{8,11},{9,10},{10,... | collective-permute-start | bytes 86024 | tf_op jit(solution)/shard_map/ppermute | solution.py:230
  16.5 0.9 %shard_map.51 = (bf16[1280,640]{1,0:T(8,128)(2,1)S(1)}, bf16[1280,640]{1,0:T(8,128)(2,1)S(1)}, f32[8,128]{1,0:T(8,128)S(1)}) custom-call(f32[7,8,128]{2,1,0:T(8,128)S(1)} %shard_map.50._.own_ref, f32[2,320,1280]{2,1,0:T(8,128)S(1)} %get-tuple-element.29.w_ref), custom_call_target="tpu_custom_call" | custom-call | flops 6553600 | bytes 6553600 | tf_op jit(solution)/shard_map/pallas_call | solution.py:315
  17.4 1.7 %collective-permute-done.5.refs_1_ = f32[7,8,128]{2,1,0:T(8,128)S(1)} collective-permute-done((f32[7,8,128]{2,1,0:T(8,128)S(1)}, f32[7,8,128]{2,1,0:T(8,128)S(1)}, u32[]{:S(2)}, u32[]{:S(2)}) %collective-permute-start.5) | collective-permute-done | bytes 28704 | tf_op jit(solution)/shard_map/ppermute | solution.py:230
  19.3 0.5 %collective-permute-start.7 = (f32[2,7,8,128]{3,2,1,0:T(8,128)S(1)}, f32[2,7,8,128]{3,2,1,0:T(8,128)S(1)}, u32[]{:S(2)}, u32[]{:S(2)}) collective-permute-start(f32[2,7,8,128]{3,2,1,0:T(8,128)S(1)} %shard_map.52.sent_ref), channel_id=1, source_target_pairs={{0,2},{1,3},{2,0},{3,1},{4,6},{5,7},{6,4},{7,5},{8,10},{9,11},{10,... | collective-permute-start | bytes 172040 | tf_op jit(solution)/shard_map/ppermute | solution.py:230
  19.8 0.9 %collective-permute-done.7.got_ref = f32[2,7,8,128]{3,2,1,0:T(8,128)S(1)} collective-permute-done((f32[2,7,8,128]{3,2,1,0:T(8,128)S(1)}, f32[2,7,8,128]{3,2,1,0:T(8,128)S(1)}, u32[]{:S(2)}, u32[]{:S(2)}) %collective-permute-start.7) | collective-permute-done | bytes 57376 | tf_op jit(solution)/shard_map/ppermute | solution.py:230
  20.7 1.0 %shard_map.53.mine_ref = f32[10,8,128]{2,1,0:T(8,128)S(1)} custom-call(f32[2,7,8,128]{3,2,1,0:T(8,128)S(1)} %shard_map.52.sent_ref, f32[2,7,8,128]{3,2,1,0:T(8,128)S(1)} %collective-permute-done.7.got_ref, bf16[1280,640]{1,0:T(8,128)(2,1)S(1)} %get-tuple-element.31.in_high_ref, bf16[1280,640]{1,0:T(8,128)(2,1)S(1)} %get-tuple-element.32.in_low_ref, ...), custom_call_target="tpu_custom_call" | custom-call | tf_op jit(solution)/shard_map/pallas_call | solution.py:293
  22.0 0.9 %collective-permute-done.8.theirs_ref = f32[10,8,128]{2,1,0:T(8,128)S(1)} collective-permute-done((f32[10,8,128]{2,1,0:T(8,128)S(1)}, f32[10,8,128]{2,1,0:T(8,128)S(1)}, u32[]{:S(2)}, u32[]{:S(2)}) %collective-permute-start.8) | collective-permute-done | bytes 40992 | tf_op jit(solution)/shard_map/ppermute | solution.py:230
  22.9 1.4 %collective-permute-start.10 = (f32[5,8,128]{2,1,0:T(8,128)S(1)}, f32[5,8,128]{2,1,0:T(8,128)S(1)}, u32[]{:S(2)}, u32[]{:S(2)}) collective-permute-start(f32[5,8,128]{2,1,0:T(8,128)S(1)} %get-tuple-element.36), channel_id=1, source_target_pairs={{0,7},{1,6},{2,5},{3,4},{4,3},{5,2},{6,1},{7,0},{8,15},{9,14},{10,... | collective-permute-start | bytes 61448 | tf_op jit(solution)/shard_map/ppermute | solution.py:230
  24.6 1.4 %collective-permute-start.9 = (f32[5,8,128]{2,1,0:T(8,128)S(1)}, f32[5,8,128]{2,1,0:T(8,128)S(1)}, u32[]{:S(2)}, u32[]{:S(2)}) collective-permute-start(f32[5,8,128]{2,1,0:T(8,128)S(1)} %get-tuple-element.36), channel_id=1, source_target_pairs={{0,3},{1,2},{2,1},{3,0},{4,7},{5,6},{6,5},{7,4},{8,11},{9,10},{10,... | collective-permute-start | bytes 61448 | tf_op jit(solution)/shard_map/ppermute | solution.py:230
  26.1 0.9 %collective-permute-done.10.refs_1_ = f32[5,8,128]{2,1,0:T(8,128)S(1)} collective-permute-done((f32[5,8,128]{2,1,0:T(8,128)S(1)}, f32[5,8,128]{2,1,0:T(8,128)S(1)}, u32[]{:S(2)}, u32[]{:S(2)}) %collective-permute-start.10) | collective-permute-done | bytes 20512 | tf_op jit(solution)/shard_map/ppermute | solution.py:230
  27.9 2.4 %collective-permute-start.13 = (f32[5,8,128]{2,1,0:T(8,128)S(1)}, f32[5,8,128]{2,1,0:T(8,128)S(1)}, u32[]{:S(2)}, u32[]{:S(2)}) collective-permute-start(f32[5,8,128]{2,1,0:T(8,128)S(1)} %shard_map.55.own_ref), channel_id=1, source_target_pairs={{0,18},{1,19},{2,16},{3,17},{4,22},{5,23},{6,20},{7,21},{8,26},{9,... | collective-permute-start | bytes 61448 | tf_op jit(solution)/shard_map/ppermute | solution.py:230
  30.3 1.3 %collective-permute-start.14 = (f32[5,8,128]{2,1,0:T(8,128)S(1)}, f32[5,8,128]{2,1,0:T(8,128)S(1)}, u32[]{:S(2)}, u32[]{:S(2)}) collective-permute-start(f32[5,8,128]{2,1,0:T(8,128)S(1)} %shard_map.55.own_ref), channel_id=1, source_target_pairs={{0,26},{1,27},{2,24},{3,25},{4,30},{5,31},{6,28},{7,29},{8,2},{9,3... | collective-permute-start | bytes 61448 | tf_op jit(solution)/shard_map/ppermute | solution.py:230
  32.2 0.7 %collective-permute-done.12.refs_1_ = f32[5,8,128]{2,1,0:T(8,128)S(1)} collective-permute-done((f32[5,8,128]{2,1,0:T(8,128)S(1)}, f32[5,8,128]{2,1,0:T(8,128)S(1)}, u32[]{:S(2)}, u32[]{:S(2)}) %collective-permute-start.12) | collective-permute-done | bytes 20512 | tf_op jit(solution)/shard_map/ppermute | solution.py:230
  32.9 0.7 %collective-permute-done.14.refs_3_ = f32[5,8,128]{2,1,0:T(8,128)S(1)} collective-permute-done((f32[5,8,128]{2,1,0:T(8,128)S(1)}, f32[5,8,128]{2,1,0:T(8,128)S(1)}, u32[]{:S(2)}, u32[]{:S(2)}) %collective-permute-start.14) | collective-permute-done | bytes 20512 | tf_op jit(solution)/shard_map/ppermute | solution.py:230
  33.9 1.0 %shard_map.57.refs_0_ = f32[224,1280]{1,0:T(8,128)} custom-call(bf16[224,96]{1,0:T(8,128)(2,1)S(1)} %shard_map.47.refs_0_.combine_ref, f32[5,8,128]{2,1,0:T(8,128)S(1)} %collective-permute-done.15.refs_4_.own_ref, f32[3,5,8,128]{3,2,1,0:T(8,128)S(1)} %shard_map.56.others_ref), custom_call_target="tpu_custom_call" | custom-call | tf_op jit(solution)/shard_map/pallas_call | solution.py:337
  35.0 1.0 %shard_map.58 = f32[224,1280]{1,0:T(8,128)} custom-call(bf16[224,96]{1,0:T(8,128)(2,1)S(1)} %shard_map.47.refs_0_.combine_ref, f32[5,8,128]{2,1,0:T(8,128)S(1)} %shard_map.55.own_ref, f32[3,5,8,128]{3,2,1,0:T(8,128)S(1)} %collective-permute-done.16.others_ref, f32[224,1280]{1,0:T(8,128)} %shard_map.57.refs_0_), custom_call_target="tpu_custom_call", output_to_operand_aliasing={{}: (3, {})} | custom-call | tf_op jit(solution)/shard_map/pallas_call | solution.py:337
  (23 shorter events, 3.2 us)
Async XLA Ops:
  2.7 1.5 %collective-permute-start = (f32[4,7,8,128]{3,2,1,0:T(8,128)S(1)}, f32[4,7,8,128]{3,2,1,0:T(8,128)S(1)}, u32[]{:S(2)}, u32[]{:S(2)}) collective-permute-start(f32[4,7,8,128]{3,2,1,0:T(8,128)S(1)} %get-tuple-element.23), channel_id=1, source_target_pairs={{0,2},{1,3},{2,0},{3,1},{4,6},{5,7},{6,4},{7,5},{8,10},{9,11},{10,... | collective-permute-start | bytes 344072 | tf_op jit(solution)/shard_map/ppermute | solution.py:230
  4.2 7.3 %collective-permute-start.1 = (f32[7,8,128]{2,1,0:T(8,128)S(1)}, f32[7,8,128]{2,1,0:T(8,128)S(1)}, u32[]{:S(2)}, u32[]{:S(2)}) collective-permute-start(f32[7,8,128]{2,1,0:T(8,128)S(1)} %get-tuple-element.25), channel_id=1, source_target_pairs={{0,18},{1,19},{2,16},{3,17},{4,22},{5,23},{6,20},{7,21},{8,26},{9,... | collective-permute-start | bytes 86024 | tf_op jit(solution)/shard_map/ppermute | solution.py:230
  7.9 5.2 %collective-permute-start.2 = (f32[7,8,128]{2,1,0:T(8,128)S(1)}, f32[7,8,128]{2,1,0:T(8,128)S(1)}, u32[]{:S(2)}, u32[]{:S(2)}) collective-permute-start(f32[7,8,128]{2,1,0:T(8,128)S(1)} %get-tuple-element.26), channel_id=1, source_target_pairs={{0,26},{1,27},{2,24},{3,25},{4,30},{5,31},{6,28},{7,29},{8,18},{9,... | collective-permute-start | bytes 86024 | tf_op jit(solution)/shard_map/ppermute | solution.py:230
  9.2 3.9 %collective-permute-start.3 = (f32[7,8,128]{2,1,0:T(8,128)S(1)}, f32[7,8,128]{2,1,0:T(8,128)S(1)}, u32[]{:S(2)}, u32[]{:S(2)}) collective-permute-start(f32[7,8,128]{2,1,0:T(8,128)S(1)} %get-tuple-element.27), channel_id=1, source_target_pairs={{0,10},{1,11},{2,8},{3,9},{4,14},{5,15},{6,12},{7,13},{8,2},{9,3},... | collective-permute-start | bytes 86024 | tf_op jit(solution)/shard_map/ppermute | solution.py:230
  13.2 4.3 %collective-permute-start.4 = (f32[7,8,128]{2,1,0:T(8,128)S(1)}, f32[7,8,128]{2,1,0:T(8,128)S(1)}, u32[]{:S(2)}, u32[]{:S(2)}) collective-permute-start(f32[7,8,128]{2,1,0:T(8,128)S(1)} %shard_map.50._.own_ref), channel_id=1, source_target_pairs={{0,7},{1,6},{2,5},{3,4},{4,3},{5,2},{6,1},{7,0},{8,15},{9,14},{10,... | collective-permute-start | bytes 86024 | tf_op jit(solution)/shard_map/ppermute | solution.py:230
  15.7 3.4 %collective-permute-start.5 = (f32[7,8,128]{2,1,0:T(8,128)S(1)}, f32[7,8,128]{2,1,0:T(8,128)S(1)}, u32[]{:S(2)}, u32[]{:S(2)}) collective-permute-start(f32[7,8,128]{2,1,0:T(8,128)S(1)} %shard_map.50._.own_ref), channel_id=1, source_target_pairs={{0,6},{1,7},{2,4},{3,5},{4,2},{5,3},{6,0},{7,1},{8,14},{9,15},{10,... | collective-permute-start | bytes 86024 | tf_op jit(solution)/shard_map/ppermute | solution.py:230
  15.9 3.3 %collective-permute-start.6 = (f32[7,8,128]{2,1,0:T(8,128)S(1)}, f32[7,8,128]{2,1,0:T(8,128)S(1)}, u32[]{:S(2)}, u32[]{:S(2)}) collective-permute-start(f32[7,8,128]{2,1,0:T(8,128)S(1)} %shard_map.50._.own_ref), channel_id=1, source_target_pairs={{0,3},{1,2},{2,1},{3,0},{4,7},{5,6},{6,5},{7,4},{8,11},{9,10},{10,... | collective-permute-start | bytes 86024 | tf_op jit(solution)/shard_map/ppermute | solution.py:230
  19.3 1.4 %collective-permute-start.7 = (f32[2,7,8,128]{3,2,1,0:T(8,128)S(1)}, f32[2,7,8,128]{3,2,1,0:T(8,128)S(1)}, u32[]{:S(2)}, u32[]{:S(2)}) collective-permute-start(f32[2,7,8,128]{3,2,1,0:T(8,128)S(1)} %shard_map.52.sent_ref), channel_id=1, source_target_pairs={{0,2},{1,3},{2,0},{3,1},{4,6},{5,7},{6,4},{7,5},{8,10},{9,11},{10,... | collective-permute-start | bytes 172040 | tf_op jit(solution)/shard_map/ppermute | solution.py:230
  21.7 1.2 %collective-permute-start.8 = (f32[10,8,128]{2,1,0:T(8,128)S(1)}, f32[10,8,128]{2,1,0:T(8,128)S(1)}, u32[]{:S(2)}, u32[]{:S(2)}) collective-permute-start(f32[10,8,128]{2,1,0:T(8,128)S(1)} %shard_map.53.mine_ref), channel_id=1, source_target_pairs={{0,2},{1,3},{2,0},{3,1},{4,6},{5,7},{6,4},{7,5},{8,10},{9,11},{10,... | collective-permute-start | bytes 122888 | tf_op jit(solution)/shard_map/ppermute | solution.py:230
  22.9 4.1 %collective-permute-start.10 = (f32[5,8,128]{2,1,0:T(8,128)S(1)}, f32[5,8,128]{2,1,0:T(8,128)S(1)}, u32[]{:S(2)}, u32[]{:S(2)}) collective-permute-start(f32[5,8,128]{2,1,0:T(8,128)S(1)} %get-tuple-element.36), channel_id=1, source_target_pairs={{0,7},{1,6},{2,5},{3,4},{4,3},{5,2},{6,1},{7,0},{8,15},{9,14},{10,... | collective-permute-start | bytes 61448 | tf_op jit(solution)/shard_map/ppermute | solution.py:230
  24.3 3.2 %collective-permute-start.11 = (f32[5,8,128]{2,1,0:T(8,128)S(1)}, f32[5,8,128]{2,1,0:T(8,128)S(1)}, u32[]{:S(2)}, u32[]{:S(2)}) collective-permute-start(f32[5,8,128]{2,1,0:T(8,128)S(1)} %get-tuple-element.36), channel_id=1, source_target_pairs={{0,6},{1,7},{2,4},{3,5},{4,2},{5,3},{6,0},{7,1},{8,14},{9,15},{10,... | collective-permute-start | bytes 61448 | tf_op jit(solution)/shard_map/ppermute | solution.py:230
  24.6 3.2 %collective-permute-start.9 = (f32[5,8,128]{2,1,0:T(8,128)S(1)}, f32[5,8,128]{2,1,0:T(8,128)S(1)}, u32[]{:S(2)}, u32[]{:S(2)}) collective-permute-start(f32[5,8,128]{2,1,0:T(8,128)S(1)} %get-tuple-element.36), channel_id=1, source_target_pairs={{0,3},{1,2},{2,1},{3,0},{4,7},{5,6},{6,5},{7,4},{8,11},{9,10},{10,... | collective-permute-start | bytes 61448 | tf_op jit(solution)/shard_map/ppermute | solution.py:230
  27.9 5.1 %collective-permute-start.12 = (f32[5,8,128]{2,1,0:T(8,128)S(1)}, f32[5,8,128]{2,1,0:T(8,128)S(1)}, u32[]{:S(2)}, u32[]{:S(2)}) collective-permute-start(f32[5,8,128]{2,1,0:T(8,128)S(1)} %shard_map.55.own_ref), channel_id=1, source_target_pairs={{0,10},{1,11},{2,8},{3,9},{4,14},{5,15},{6,12},{7,13},{8,18},{9,19... | collective-permute-start | bytes 61448 | tf_op jit(solution)/shard_map/ppermute | solution.py:230
  27.9 5.0 %collective-permute-start.13 = (f32[5,8,128]{2,1,0:T(8,128)S(1)}, f32[5,8,128]{2,1,0:T(8,128)S(1)}, u32[]{:S(2)}, u32[]{:S(2)}) collective-permute-start(f32[5,8,128]{2,1,0:T(8,128)S(1)} %shard_map.55.own_ref), channel_id=1, source_target_pairs={{0,18},{1,19},{2,16},{3,17},{4,22},{5,23},{6,20},{7,21},{8,26},{9,... | collective-permute-start | bytes 61448 | tf_op jit(solution)/shard_map/ppermute | solution.py:230
  30.3 3.3 %collective-permute-start.14 = (f32[5,8,128]{2,1,0:T(8,128)S(1)}, f32[5,8,128]{2,1,0:T(8,128)S(1)}, u32[]{:S(2)}, u32[]{:S(2)}) collective-permute-start(f32[5,8,128]{2,1,0:T(8,128)S(1)} %shard_map.55.own_ref), channel_id=1, source_target_pairs={{0,26},{1,27},{2,24},{3,25},{4,30},{5,31},{6,28},{7,29},{8,2},{9,3... | collective-permute-start | bytes 61448 | tf_op jit(solution)/shard_map/ppermute | solution.py:230
  31.7 2.0 %collective-permute-start.15 = (f32[5,8,128]{2,1,0:T(8,128)S(1)}, f32[5,8,128]{2,1,0:T(8,128)S(1)}, u32[]{:S(2)}, u32[]{:S(2)}) collective-permute-start(f32[5,8,128]{2,1,0:T(8,128)S(1)} %shard_map.55.own_ref), channel_id=1, source_target_pairs={{0,2},{1,3},{2,0},{3,1},{4,6},{5,7},{6,4},{7,5},{8,10},{9,11},{10,... | collective-permute-start | bytes 61448 | tf_op jit(solution)/shard_map/ppermute | solution.py:230
  33.7 1.3 %collective-permute-start.16 = (f32[3,5,8,128]{3,2,1,0:T(8,128)S(1)}, f32[3,5,8,128]{3,2,1,0:T(8,128)S(1)}, u32[]{:S(2)}, u32[]{:S(2)}) collective-permute-start(f32[3,5,8,128]{3,2,1,0:T(8,128)S(1)} %shard_map.56.others_ref), channel_id=1, source_target_pairs={{0,2},{1,3},{2,0},{3,1},{4,6},{5,7},{6,4},{7,5},{8,10},{9,11},{10,... | collective-permute-start | bytes 184328 | tf_op jit(solution)/shard_map/ppermute | solution.py:230

commit v10 on v7

--- a/solution.py
+++ b/solution.py
@@ -244,6 +244,13 @@
             for dx in range(n_x)[::-1] for df in range(n_fsdp)[::-1] if dx or df
         ]
 
+    def turned(value):
+        return [
+            permute(value, lambda e, x, c, f: (e, 1 - x, 1 - c, 1 - f)),
+            permute(value, lambda e, x, c, f: (e, f, 1 - c, 1 - x)),
+            permute(value, lambda e, x, c, f: (e, 1 - f, 1 - c, x)),
+        ]
+
     def body(tokens, slot_params, w_in, w_out):
         count, width = tokens.shape
         slots = slot_params.shape[1]
@@ -326,7 +333,7 @@
         partial = local(expert_kernel, shape, sent, other_core(sent), in_high, in_low, out_high, out_low)
         shape = pltpu.VMEM((half, rows, LANES), f32)
         keep, send = local(halves_kernel, (shape, shape), partial, other_core(partial))
-        around = plane(send)
+        around = turned(send) if n_x == n_fsdp == 2 else plane(send)
         own = local(add_kernel, shape, keep, *around[-1:], *around[:-1])
         arrived = [around_expert(own, k) for k in range(1, n_expert)]
         own_near = other_core(own)

time: 36.1 us -> 37.1 us (1.028)
  waiting for transfers between devices: 9.17 us -> 10.1 us
    ppermute x17, waiting for transfers between devices: 9.17 us -> 10.1 us  [permute(): return lax.ppermute(value, AXES, pairs)]
where the time goes in v10:
time: 37.1 us; the launch traced here: 37 us
  starting transfers between devices  17.9 us (48%)
  waiting for transfers between devices  10.1 us (27%)
  Pallas kernels  8.87 us (24%)
    ppermute x17, starting transfers between devices, permute(): return lax.ppermute(value, AXES, pairs)  17.9 us
    ppermute x17, waiting for transfers between devices, permute(): return lax.ppermute(value, AXES, pairs)  10.1 us
    pallas_call x1, Pallas kernels, body(): pl.pallas_call(functools.partial(dispatch_kernel, chunks), out_shape=(plt...  2.64 us
    pallas_call x2, Pallas kernels, mix(): pl.pallas_call(functools.partial(mix_kernel, near), out_shape=jax.ShapeDt...  2.03 us
    pallas_call x1, Pallas kernels, body(): pl.pallas_call(split_out_kernel, out_shape=(part, part, flag), in_specs=[...  2 us
    pallas_call x6, Pallas kernels, local(): pl.pallas_call(kernel, out_shape=out, in_specs=[VMEM] * len(args), out_sp...  1.07 us
    pallas_call x1, Pallas kernels, body(): pl.pallas_call(split_in_kernel, out_shape=(part, part, flag), in_specs=[V...  0.89 us
  transfers between devices with their start and end apart: 17, of which 13 were waited for; matrix products, arithmetic and copies ran while one was open for 0% of the time, Pallas kernels for 11%

profile of v10, /device:TPU:0, one launch (start us, length us, event | category | flops | bytes accessed | tf_op | source)
XLA Modules:
  0.0 37.0 jit_solution(6994932250413269216)
XLA Ops:
  0.0 2.6 %shard_map.46 = (f32[32,224]{1,0:T(8,128)S(1)}, f32[4,7,8,128]{3,2,1,0:T(8,128)S(1)}, f32[4,7,8,128]{3,2,1,0:T(8,128)S(1)}, f32[2,320,1280]{2,1,0:T(8,128)S(1)}) custom-call(f32[224,1280]{1,0:T(8,128)} %tokens_hbm.1, f32[32,1280]{1,0:T(8,128)} %bitcast.1, f32[2,320,1280]{2,1,0:T(8,128)} %w_in_hbm.1), custom_call_target="tpu_custom_call" | custom-call | tf_op jit(solution)/shard_map/pallas_call | solution.py:266
  2.7 0.5 %collective-permute-start = (f32[4,7,8,128]{3,2,1,0:T(8,128)S(1)}, f32[4,7,8,128]{3,2,1,0:T(8,128)S(1)}, u32[]{:S(2)}, u32[]{:S(2)}) collective-permute-start(f32[4,7,8,128]{3,2,1,0:T(8,128)S(1)} %get-tuple-element.23), channel_id=1, source_target_pairs={{0,2},{1,3},{2,0},{3,1},{4,6},{5,7},{6,4},{7,5},{8,10},{9,11},{10,... | collective-permute-start | bytes 344072 | tf_op jit(solution)/shard_map/ppermute | solution.py:230
  3.2 1.0 %collective-permute-done.theirs_ref = f32[4,7,8,128]{3,2,1,0:T(8,128)S(1)} collective-permute-done((f32[4,7,8,128]{3,2,1,0:T(8,128)S(1)}, f32[4,7,8,128]{3,2,1,0:T(8,128)S(1)}, u32[]{:S(2)}, u32[]{:S(2)}) %collective-permute-start) | collective-permute-done | bytes 114720 | tf_op jit(solution)/shard_map/ppermute | solution.py:230
  4.2 4.8 %collective-permute-start.1 = (f32[7,8,128]{2,1,0:T(8,128)S(1)}, f32[7,8,128]{2,1,0:T(8,128)S(1)}, u32[]{:S(2)}, u32[]{:S(2)}) collective-permute-start(f32[7,8,128]{2,1,0:T(8,128)S(1)} %get-tuple-element.25), channel_id=1, source_target_pairs={{0,26},{1,27},{2,24},{3,25},{4,30},{5,31},{6,28},{7,29},{8,18},{9,... | collective-permute-start | bytes 86024 | tf_op jit(solution)/shard_map/ppermute | solution.py:230
  8.9 0.6 %collective-permute-start.3 = (f32[7,8,128]{2,1,0:T(8,128)S(1)}, f32[7,8,128]{2,1,0:T(8,128)S(1)}, u32[]{:S(2)}, u32[]{:S(2)}) collective-permute-start(f32[7,8,128]{2,1,0:T(8,128)S(1)} %get-tuple-element.27), channel_id=1, source_target_pairs={{0,10},{1,11},{2,8},{3,9},{4,14},{5,15},{6,12},{7,13},{8,2},{9,3},... | collective-permute-start | bytes 86024 | tf_op jit(solution)/shard_map/ppermute | solution.py:230
  9.6 2.0 %shard_map.49 = (bf16[640,1280]{1,0:T(8,128)(2,1)S(1)}, bf16[640,1280]{1,0:T(8,128)(2,1)S(1)}, f32[8,128]{1,0:T(8,128)S(1)}) custom-call(f32[7,8,128]{2,1,0:T(8,128)S(1)} %get-tuple-element.24._.own_ref, f32[2,320,1280]{2,1,0:T(8,128)} %w_hbm.1), custom_call_target="tpu_custom_call" | custom-call | flops 6553600 | bytes 6553600 | tf_op jit(solution)/shard_map/pallas_call | solution.py:310
  11.6 1.6 %collective-permute-done.2.refs_1_ = f32[7,8,128]{2,1,0:T(8,128)S(1)} collective-permute-done((f32[7,8,128]{2,1,0:T(8,128)S(1)}, f32[7,8,128]{2,1,0:T(8,128)S(1)}, u32[]{:S(2)}, u32[]{:S(2)}) %collective-permute-start.2) | collective-permute-done | bytes 28704 | tf_op jit(solution)/shard_map/ppermute | solution.py:230
  13.2 2.5 %collective-permute-start.4 = (f32[7,8,128]{2,1,0:T(8,128)S(1)}, f32[7,8,128]{2,1,0:T(8,128)S(1)}, u32[]{:S(2)}, u32[]{:S(2)}) collective-permute-start(f32[7,8,128]{2,1,0:T(8,128)S(1)} %shard_map.50._.own_ref), channel_id=1, source_target_pairs={{0,7},{1,6},{2,5},{3,4},{4,3},{5,2},{6,1},{7,0},{8,15},{9,14},{10,... | collective-permute-start | bytes 86024 | tf_op jit(solution)/shard_map/ppermute | solution.py:230
  16.4 0.9 %shard_map.51 = (bf16[1280,640]{1,0:T(8,128)(2,1)S(1)}, bf16[1280,640]{1,0:T(8,128)(2,1)S(1)}, f32[8,128]{1,0:T(8,128)S(1)}) custom-call(f32[7,8,128]{2,1,0:T(8,128)S(1)} %shard_map.50._.own_ref, f32[2,320,1280]{2,1,0:T(8,128)S(1)} %get-tuple-element.29.w_ref), custom_call_target="tpu_custom_call" | custom-call | flops 6553600 | bytes 6553600 | tf_op jit(solution)/shard_map/pallas_call | solution.py:322
  17.4 1.5 %collective-permute-done.5.refs_1_ = f32[7,8,128]{2,1,0:T(8,128)S(1)} collective-permute-done((f32[7,8,128]{2,1,0:T(8,128)S(1)}, f32[7,8,128]{2,1,0:T(8,128)S(1)}, u32[]{:S(2)}, u32[]{:S(2)}) %collective-permute-start.5) | collective-permute-done | bytes 28704 | tf_op jit(solution)/shard_map/ppermute | solution.py:230
  19.7 0.9 %collective-permute-done.7.got_ref = f32[2,7,8,128]{3,2,1,0:T(8,128)S(1)} collective-permute-done((f32[2,7,8,128]{3,2,1,0:T(8,128)S(1)}, f32[2,7,8,128]{3,2,1,0:T(8,128)S(1)}, u32[]{:S(2)}, u32[]{:S(2)}) %collective-permute-start.7) | collective-permute-done | bytes 57376 | tf_op jit(solution)/shard_map/ppermute | solution.py:230
  20.6 1.0 %shard_map.53.mine_ref = f32[10,8,128]{2,1,0:T(8,128)S(1)} custom-call(f32[2,7,8,128]{3,2,1,0:T(8,128)S(1)} %shard_map.52.sent_ref, f32[2,7,8,128]{3,2,1,0:T(8,128)S(1)} %collective-permute-done.7.got_ref, bf16[1280,640]{1,0:T(8,128)(2,1)S(1)} %get-tuple-element.31.in_high_ref, bf16[1280,640]{1,0:T(8,128)(2,1)S(1)} %get-tuple-element.32.in_low_ref, ...), custom_call_target="tpu_custom_call" | custom-call | tf_op jit(solution)/shard_map/pallas_call | solution.py:300
  21.9 0.9 %collective-permute-done.8.theirs_ref = f32[10,8,128]{2,1,0:T(8,128)S(1)} collective-permute-done((f32[10,8,128]{2,1,0:T(8,128)S(1)}, f32[10,8,128]{2,1,0:T(8,128)S(1)}, u32[]{:S(2)}, u32[]{:S(2)}) %collective-permute-start.8) | collective-permute-done | bytes 40992 | tf_op jit(solution)/shard_map/ppermute | solution.py:230
  22.8 1.4 %collective-permute-start.10 = (f32[5,8,128]{2,1,0:T(8,128)S(1)}, f32[5,8,128]{2,1,0:T(8,128)S(1)}, u32[]{:S(2)}, u32[]{:S(2)}) collective-permute-start(f32[5,8,128]{2,1,0:T(8,128)S(1)} %get-tuple-element.36), channel_id=1, source_target_pairs={{0,7},{1,6},{2,5},{3,4},{4,3},{5,2},{6,1},{7,0},{8,15},{9,14},{10,... | collective-permute-start | bytes 61448 | tf_op jit(solution)/shard_map/ppermute | solution.py:230
  24.2 1.3 %collective-permute-start.11 = (f32[5,8,128]{2,1,0:T(8,128)S(1)}, f32[5,8,128]{2,1,0:T(8,128)S(1)}, u32[]{:S(2)}, u32[]{:S(2)}) collective-permute-start(f32[5,8,128]{2,1,0:T(8,128)S(1)} %get-tuple-element.36), channel_id=1, source_target_pairs={{0,3},{1,7},{2,1},{3,5},{4,2},{5,6},{6,0},{7,4},{8,11},{9,15},{10,... | collective-permute-start | bytes 61448 | tf_op jit(solution)/shard_map/ppermute | solution.py:230
  25.5 0.5 %collective-permute-start.9 = (f32[5,8,128]{2,1,0:T(8,128)S(1)}, f32[5,8,128]{2,1,0:T(8,128)S(1)}, u32[]{:S(2)}, u32[]{:S(2)}) collective-permute-start(f32[5,8,128]{2,1,0:T(8,128)S(1)} %get-tuple-element.36), channel_id=1, source_target_pairs={{0,6},{1,2},{2,4},{3,0},{4,7},{5,3},{6,5},{7,1},{8,14},{9,10},{10,... | collective-permute-start | bytes 61448 | tf_op jit(solution)/shard_map/ppermute | solution.py:230
  26.0 1.0 %collective-permute-done.10.refs_1_ = f32[5,8,128]{2,1,0:T(8,128)S(1)} collective-permute-done((f32[5,8,128]{2,1,0:T(8,128)S(1)}, f32[5,8,128]{2,1,0:T(8,128)S(1)}, u32[]{:S(2)}, u32[]{:S(2)}) %collective-permute-start.10) | collective-permute-done | bytes 20512 | tf_op jit(solution)/shard_map/ppermute | solution.py:230
  26.9 0.5 %collective-permute-done.11.refs_2_ = f32[5,8,128]{2,1,0:T(8,128)S(1)} collective-permute-done((f32[5,8,128]{2,1,0:T(8,128)S(1)}, f32[5,8,128]{2,1,0:T(8,128)S(1)}, u32[]{:S(2)}, u32[]{:S(2)}) %collective-permute-start.11) | collective-permute-done | bytes 20512 | tf_op jit(solution)/shard_map/ppermute | solution.py:230
  27.4 1.3 %collective-permute-done.9.refs_0_ = f32[5,8,128]{2,1,0:T(8,128)S(1)} collective-permute-done((f32[5,8,128]{2,1,0:T(8,128)S(1)}, f32[5,8,128]{2,1,0:T(8,128)S(1)}, u32[]{:S(2)}, u32[]{:S(2)}) %collective-permute-start.9) | collective-permute-done | bytes 20512 | tf_op jit(solution)/shard_map/ppermute | solution.py:230
  29.1 1.9 %collective-permute-start.13 = (f32[5,8,128]{2,1,0:T(8,128)S(1)}, f32[5,8,128]{2,1,0:T(8,128)S(1)}, u32[]{:S(2)}, u32[]{:S(2)}) collective-permute-start(f32[5,8,128]{2,1,0:T(8,128)S(1)} %shard_map.55.own_ref), channel_id=1, source_target_pairs={{0,18},{1,19},{2,16},{3,17},{4,22},{5,23},{6,20},{7,21},{8,26},{9,... | collective-permute-start | bytes 61448 | tf_op jit(solution)/shard_map/ppermute | solution.py:230
  31.0 2.1 %collective-permute-start.14 = (f32[5,8,128]{2,1,0:T(8,128)S(1)}, f32[5,8,128]{2,1,0:T(8,128)S(1)}, u32[]{:S(2)}, u32[]{:S(2)}) collective-permute-start(f32[5,8,128]{2,1,0:T(8,128)S(1)} %shard_map.55.own_ref), channel_id=1, source_target_pairs={{0,26},{1,27},{2,24},{3,25},{4,30},{5,31},{6,28},{7,29},{8,2},{9,3... | collective-permute-start | bytes 61448 | tf_op jit(solution)/shard_map/ppermute | solution.py:230
  33.9 0.8 %collective-permute-done.14.refs_3_ = f32[5,8,128]{2,1,0:T(8,128)S(1)} collective-permute-done((f32[5,8,128]{2,1,0:T(8,128)S(1)}, f32[5,8,128]{2,1,0:T(8,128)S(1)}, u32[]{:S(2)}, u32[]{:S(2)}) %collective-permute-start.14) | collective-permute-done | bytes 20512 | tf_op jit(solution)/shard_map/ppermute | solution.py:230
  34.7 1.0 %shard_map.57.refs_0_ = f32[224,1280]{1,0:T(8,128)} custom-call(bf16[224,96]{1,0:T(8,128)(2,1)S(1)} %shard_map.47.refs_0_.combine_ref, f32[5,8,128]{2,1,0:T(8,128)S(1)} %collective-permute-done.15.refs_4_.own_ref, f32[3,5,8,128]{3,2,1,0:T(8,128)S(1)} %shard_map.56.others_ref), custom_call_target="tpu_custom_call" | custom-call | tf_op jit(solution)/shard_map/pallas_call | solution.py:344
  36.0 1.0 %shard_map.58 = f32[224,1280]{1,0:T(8,128)} custom-call(bf16[224,96]{1,0:T(8,128)(2,1)S(1)} %shard_map.47.refs_0_.combine_ref, f32[5,8,128]{2,1,0:T(8,128)S(1)} %shard_map.55.own_ref, f32[3,5,8,128]{3,2,1,0:T(8,128)S(1)} %collective-permute-done.16.others_ref, f32[224,1280]{1,0:T(8,128)} %shard_map.57.refs_0_), custom_call_target="tpu_custom_call", output_to_operand_aliasing={{}: (3, {})} | custom-call | tf_op jit(solution)/shard_map/pallas_call | solution.py:344
  (23 shorter events, 3.4 us)
Async XLA Ops:
  2.7 1.5 %collective-permute-start = (f32[4,7,8,128]{3,2,1,0:T(8,128)S(1)}, f32[4,7,8,128]{3,2,1,0:T(8,128)S(1)}, u32[]{:S(2)}, u32[]{:S(2)}) collective-permute-start(f32[4,7,8,128]{3,2,1,0:T(8,128)S(1)} %get-tuple-element.23), channel_id=1, source_target_pairs={{0,2},{1,3},{2,0},{3,1},{4,6},{5,7},{6,4},{7,5},{8,10},{9,11},{10,... | collective-permute-start | bytes 344072 | tf_op jit(solution)/shard_map/ppermute | solution.py:230
  4.2 7.4 %collective-permute-start.1 = (f32[7,8,128]{2,1,0:T(8,128)S(1)}, f32[7,8,128]{2,1,0:T(8,128)S(1)}, u32[]{:S(2)}, u32[]{:S(2)}) collective-permute-start(f32[7,8,128]{2,1,0:T(8,128)S(1)} %get-tuple-element.25), channel_id=1, source_target_pairs={{0,26},{1,27},{2,24},{3,25},{4,30},{5,31},{6,28},{7,29},{8,18},{9,... | collective-permute-start | bytes 86024 | tf_op jit(solution)/shard_map/ppermute | solution.py:230
  8.9 4.2 %collective-permute-start.2 = (f32[7,8,128]{2,1,0:T(8,128)S(1)}, f32[7,8,128]{2,1,0:T(8,128)S(1)}, u32[]{:S(2)}, u32[]{:S(2)}) collective-permute-start(f32[7,8,128]{2,1,0:T(8,128)S(1)} %get-tuple-element.26), channel_id=1, source_target_pairs={{0,18},{1,19},{2,16},{3,17},{4,22},{5,23},{6,20},{7,21},{8,26},{9,... | collective-permute-start | bytes 86024 | tf_op jit(solution)/shard_map/ppermute | solution.py:230
  8.9 4.2 %collective-permute-start.3 = (f32[7,8,128]{2,1,0:T(8,128)S(1)}, f32[7,8,128]{2,1,0:T(8,128)S(1)}, u32[]{:S(2)}, u32[]{:S(2)}) collective-permute-start(f32[7,8,128]{2,1,0:T(8,128)S(1)} %get-tuple-element.27), channel_id=1, source_target_pairs={{0,10},{1,11},{2,8},{3,9},{4,14},{5,15},{6,12},{7,13},{8,2},{9,3},... | collective-permute-start | bytes 86024 | tf_op jit(solution)/shard_map/ppermute | solution.py:230
  13.2 4.3 %collective-permute-start.4 = (f32[7,8,128]{2,1,0:T(8,128)S(1)}, f32[7,8,128]{2,1,0:T(8,128)S(1)}, u32[]{:S(2)}, u32[]{:S(2)}) collective-permute-start(f32[7,8,128]{2,1,0:T(8,128)S(1)} %shard_map.50._.own_ref), channel_id=1, source_target_pairs={{0,7},{1,6},{2,5},{3,4},{4,3},{5,2},{6,1},{7,0},{8,15},{9,14},{10,... | collective-permute-start | bytes 86024 | tf_op jit(solution)/shard_map/ppermute | solution.py:230
  15.6 3.3 %collective-permute-start.5 = (f32[7,8,128]{2,1,0:T(8,128)S(1)}, f32[7,8,128]{2,1,0:T(8,128)S(1)}, u32[]{:S(2)}, u32[]{:S(2)}) collective-permute-start(f32[7,8,128]{2,1,0:T(8,128)S(1)} %shard_map.50._.own_ref), channel_id=1, source_target_pairs={{0,6},{1,7},{2,4},{3,5},{4,2},{5,3},{6,0},{7,1},{8,14},{9,15},{10,... | collective-permute-start | bytes 86024 | tf_op jit(solution)/shard_map/ppermute | solution.py:230
  16.0 3.3 %collective-permute-start.6 = (f32[7,8,128]{2,1,0:T(8,128)S(1)}, f32[7,8,128]{2,1,0:T(8,128)S(1)}, u32[]{:S(2)}, u32[]{:S(2)}) collective-permute-start(f32[7,8,128]{2,1,0:T(8,128)S(1)} %shard_map.50._.own_ref), channel_id=1, source_target_pairs={{0,3},{1,2},{2,1},{3,0},{4,7},{5,6},{6,5},{7,4},{8,11},{9,10},{10,... | collective-permute-start | bytes 86024 | tf_op jit(solution)/shard_map/ppermute | solution.py:230
  19.3 1.3 %collective-permute-start.7 = (f32[2,7,8,128]{3,2,1,0:T(8,128)S(1)}, f32[2,7,8,128]{3,2,1,0:T(8,128)S(1)}, u32[]{:S(2)}, u32[]{:S(2)}) collective-permute-start(f32[2,7,8,128]{3,2,1,0:T(8,128)S(1)} %shard_map.52.sent_ref), channel_id=1, source_target_pairs={{0,2},{1,3},{2,0},{3,1},{4,6},{5,7},{6,4},{7,5},{8,10},{9,11},{10,... | collective-permute-start | bytes 172040 | tf_op jit(solution)/shard_map/ppermute | solution.py:230
  21.6 1.2 %collective-permute-start.8 = (f32[10,8,128]{2,1,0:T(8,128)S(1)}, f32[10,8,128]{2,1,0:T(8,128)S(1)}, u32[]{:S(2)}, u32[]{:S(2)}) collective-permute-start(f32[10,8,128]{2,1,0:T(8,128)S(1)} %shard_map.53.mine_ref), channel_id=1, source_target_pairs={{0,2},{1,3},{2,0},{3,1},{4,6},{5,7},{6,4},{7,5},{8,10},{9,11},{10,... | collective-permute-start | bytes 122888 | tf_op jit(solution)/shard_map/ppermute | solution.py:230
  22.8 4.1 %collective-permute-start.10 = (f32[5,8,128]{2,1,0:T(8,128)S(1)}, f32[5,8,128]{2,1,0:T(8,128)S(1)}, u32[]{:S(2)}, u32[]{:S(2)}) collective-permute-start(f32[5,8,128]{2,1,0:T(8,128)S(1)} %get-tuple-element.36), channel_id=1, source_target_pairs={{0,7},{1,6},{2,5},{3,4},{4,3},{5,2},{6,1},{7,0},{8,15},{9,14},{10,... | collective-permute-start | bytes 61448 | tf_op jit(solution)/shard_map/ppermute | solution.py:230
  24.2 3.2 %collective-permute-start.11 = (f32[5,8,128]{2,1,0:T(8,128)S(1)}, f32[5,8,128]{2,1,0:T(8,128)S(1)}, u32[]{:S(2)}, u32[]{:S(2)}) collective-permute-start(f32[5,8,128]{2,1,0:T(8,128)S(1)} %get-tuple-element.36), channel_id=1, source_target_pairs={{0,3},{1,7},{2,1},{3,5},{4,2},{5,6},{6,0},{7,4},{8,11},{9,15},{10,... | collective-permute-start | bytes 61448 | tf_op jit(solution)/shard_map/ppermute | solution.py:230
  25.5 3.2 %collective-permute-start.9 = (f32[5,8,128]{2,1,0:T(8,128)S(1)}, f32[5,8,128]{2,1,0:T(8,128)S(1)}, u32[]{:S(2)}, u32[]{:S(2)}) collective-permute-start(f32[5,8,128]{2,1,0:T(8,128)S(1)} %get-tuple-element.36), channel_id=1, source_target_pairs={{0,6},{1,2},{2,4},{3,0},{4,7},{5,3},{6,5},{7,1},{8,14},{9,10},{10,... | collective-permute-start | bytes 61448 | tf_op jit(solution)/shard_map/ppermute | solution.py:230
  28.7 5.2 %collective-permute-start.12 = (f32[5,8,128]{2,1,0:T(8,128)S(1)}, f32[5,8,128]{2,1,0:T(8,128)S(1)}, u32[]{:S(2)}, u32[]{:S(2)}) collective-permute-start(f32[5,8,128]{2,1,0:T(8,128)S(1)} %shard_map.55.own_ref), channel_id=1, source_target_pairs={{0,10},{1,11},{2,8},{3,9},{4,14},{5,15},{6,12},{7,13},{8,18},{9,19... | collective-permute-start | bytes 61448 | tf_op jit(solution)/shard_map/ppermute | solution.py:230
  29.1 4.8 %collective-permute-start.13 = (f32[5,8,128]{2,1,0:T(8,128)S(1)}, f32[5,8,128]{2,1,0:T(8,128)S(1)}, u32[]{:S(2)}, u32[]{:S(2)}) collective-permute-start(f32[5,8,128]{2,1,0:T(8,128)S(1)} %shard_map.55.own_ref), channel_id=1, source_target_pairs={{0,18},{1,19},{2,16},{3,17},{4,22},{5,23},{6,20},{7,21},{8,26},{9,... | collective-permute-start | bytes 61448 | tf_op jit(solution)/shard_map/ppermute | solution.py:230
  31.0 3.6 %collective-permute-start.14 = (f32[5,8,128]{2,1,0:T(8,128)S(1)}, f32[5,8,128]{2,1,0:T(8,128)S(1)}, u32[]{:S(2)}, u32[]{:S(2)}) collective-permute-start(f32[5,8,128]{2,1,0:T(8,128)S(1)} %shard_map.55.own_ref), channel_id=1, source_target_pairs={{0,26},{1,27},{2,24},{3,25},{4,30},{5,31},{6,28},{7,29},{8,2},{9,3... | collective-permute-start | bytes 61448 | tf_op jit(solution)/shard_map/ppermute | solution.py:230
  33.1 1.5 %collective-permute-start.15 = (f32[5,8,128]{2,1,0:T(8,128)S(1)}, f32[5,8,128]{2,1,0:T(8,128)S(1)}, u32[]{:S(2)}, u32[]{:S(2)}) collective-permute-start(f32[5,8,128]{2,1,0:T(8,128)S(1)} %shard_map.55.own_ref), channel_id=1, source_target_pairs={{0,2},{1,3},{2,0},{3,1},{4,6},{5,7},{6,4},{7,5},{8,10},{9,11},{10,... | collective-permute-start | bytes 61448 | tf_op jit(solution)/shard_map/ppermute | solution.py:230
  34.6 1.3 %collective-permute-start.16 = (f32[3,5,8,128]{3,2,1,0:T(8,128)S(1)}, f32[3,5,8,128]{3,2,1,0:T(8,128)S(1)}, u32[]{:S(2)}, u32[]{:S(2)}) collective-permute-start(f32[3,5,8,128]{3,2,1,0:T(8,128)S(1)} %shard_map.56.others_ref), channel_id=1, source_target_pairs={{0,2},{1,3},{2,0},{3,1},{4,6},{5,7},{6,4},{7,5},{8,10},{9,11},{10,... | collective-permute-start | bytes 184328 | tf_op jit(solution)/shard_map/ppermute | solution.py:230

commit v11 on v9

--- a/solution.py
+++ b/solution.py
@@ -34,6 +34,12 @@
 
 def pick(core, when_zero, when_one):
     return jnp.where(core == 0, when_zero, when_one)
+
+
+def ring_step(e, k, n, where=lambda c, a, b: a if c else b):
+    place = where(e % 2 == 1, (e + 1) // 2, n - e // 2) + k
+    place = where(place >= n, place - n, place)
+    return where(place == 0, 0, where(place <= n // 2, 2 * place - 1, 2 * (n - place)))
 
 
 def join(parts):
@@ -77,7 +83,8 @@
     sums_ref[:, width:width + LANES] = jnp.broadcast_to(mass, (slots, LANES))
     sums_ref[:, width + LANES:] = jnp.broadcast_to(peak, (slots, LANES))
     for k in range(groups):
-        own = pl.ds(pl.multiple_of((expert ^ k) * rows, rows), rows)
+        target = ring_step(expert, k, groups, jnp.where)
+        own = pl.ds(pl.multiple_of(target * rows, rows), rows)
         sides = (core, 1 - core) if k else (1 - core, core)
         for ref, side in zip((mine_ref, theirs_ref), sides):
             for t in range(half):
@@ -232,8 +239,8 @@
     def other_core(value):
         return permute(value, lambda e, x, c, f: (e, x, 1 - c, f))
 
-    def along_expert(value, k):
-        return permute(value, lambda e, x, c, f: (e ^ k, x, 1 - c, f))
+    def along_ring(value, k):
+        return permute(value, lambda e, x, c, f: (ring_step(e, k, n_expert), x, 1 - c, f))
 
     def around_expert(value, k):
         return permute(value, lambda e, x, c, f: ((e + k) % n_expert, x, 1 - c, f))
@@ -284,7 +291,6 @@
             out_specs=(VMEM,) * n_expert,
             compiler_params=params,
         )(mine, other_core(theirs))
-        order = sorted(range(n_expert - 1, 0, -1), key=lambda k: k != n_expert // 2)
         flag = pltpu.VMEM((8, LANES), f32)
         experts, units, _ = w_in.shape
         cost = pl.CostEstimate(flops=8 * w_in.size, bytes_accessed=8 * w_in.size, transcendentals=0)
@@ -310,7 +316,7 @@
             compiler_params=params,
         )(chip[0], in_hbm(w_out))
         shape = pltpu.VMEM((half + 2, rows, LANES), f32)
-        total = local(total_kernel, shape, chip[0], *[along_expert(chip[k], k) for k in order], ready)
+        total = local(total_kernel, shape, chip[0], *[along_ring(chip[k], k) for k in range(1, n_expert)], ready)
         part = pltpu.VMEM((width, experts * units), jnp.bfloat16)
         in_high, in_low, ready = pl.pallas_call(
             split_in_kernel,

time: 36.1 us -> 36.1 us (level)
  waiting for transfers between devices: 9.56 us -> 8.79 us
  starting transfers between devices: 17.5 us -> 18.2 us
    ppermute x17, waiting for transfers between devices: 9.56 us -> 8.79 us  [permute(): return lax.ppermute(value, AXES, pairs)]
    ppermute x17, starting transfers between devices: 17.5 us -> 18.2 us  [permute(): return lax.ppermute(value, AXES, pairs)]
  transfers between devices with their start and end apart: 17 -> 17, of which waited for: 12 -> 13; matrix products, arithmetic and copies ran while one was open for 0% -> 0% of each run, Pallas kernels for 11% -> 11%
where the time goes in v11:
time: 36.1 us; the launch traced here: 36 us
  starting transfers between devices  18.2 us (50%)
  Pallas kernels  8.87 us (25%)
  waiting for transfers between devices  8.79 us (24%)
    ppermute x17, starting transfers between devices, permute(): return lax.ppermute(value, AXES, pairs)  18.2 us
    ppermute x17, waiting for transfers between devices, permute(): return lax.ppermute(value, AXES, pairs)  8.79 us
    pallas_call x1, Pallas kernels, body(): pl.pallas_call(functools.partial(dispatch_kernel, chunks), out_shape=(plt...  2.65 us
    pallas_call x2, Pallas kernels, mix(): pl.pallas_call(functools.partial(mix_kernel, near), out_shape=jax.ShapeDt...  2.03 us
    pallas_call x1, Pallas kernels, body(): pl.pallas_call(split_out_kernel, out_shape=(part, part, flag), in_specs=[...  2 us
    pallas_call x6, Pallas kernels, local(): pl.pallas_call(kernel, out_shape=out, in_specs=[VMEM] * len(args), out_sp...  1.07 us
    pallas_call x1, Pallas kernels, body(): pl.pallas_call(split_in_kernel, out_shape=(part, part, flag), in_specs=[V...  0.89 us
  transfers between devices with their start and end apart: 17, of which 13 were waited for; matrix products, arithmetic and copies ran while one was open for 0% of the time, Pallas kernels for 11%

profile of v11, /device:TPU:0, one launch (start us, length us, event | category | flops | bytes accessed | tf_op | source)
XLA Modules:
  0.0 36.0 jit_solution(1618880440528384518)
XLA Ops:
  0.0 2.6 %shard_map.46 = (f32[32,224]{1,0:T(8,128)S(1)}, f32[4,7,8,128]{3,2,1,0:T(8,128)S(1)}, f32[4,7,8,128]{3,2,1,0:T(8,128)S(1)}, f32[2,320,1280]{2,1,0:T(8,128)S(1)}) custom-call(f32[224,1280]{1,0:T(8,128)} %tokens_hbm.1, f32[32,1280]{1,0:T(8,128)} %bitcast.1, f32[2,320,1280]{2,1,0:T(8,128)} %w_in_hbm.1), custom_call_target="tpu_custom_call" | custom-call | tf_op jit(solution)/shard_map/pallas_call | solution.py:266
  2.7 0.5 %collective-permute-start = (f32[4,7,8,128]{3,2,1,0:T(8,128)S(1)}, f32[4,7,8,128]{3,2,1,0:T(8,128)S(1)}, u32[]{:S(2)}, u32[]{:S(2)}) collective-permute-start(f32[4,7,8,128]{3,2,1,0:T(8,128)S(1)} %get-tuple-element.23), channel_id=1, source_target_pairs={{0,2},{1,3},{2,0},{3,1},{4,6},{5,7},{6,4},{7,5},{8,10},{9,11},{10,... | collective-permute-start | bytes 344072 | tf_op jit(solution)/shard_map/ppermute | solution.py:237
  3.2 1.0 %collective-permute-done.theirs_ref = f32[4,7,8,128]{3,2,1,0:T(8,128)S(1)} collective-permute-done((f32[4,7,8,128]{3,2,1,0:T(8,128)S(1)}, f32[4,7,8,128]{3,2,1,0:T(8,128)S(1)}, u32[]{:S(2)}, u32[]{:S(2)}) %collective-permute-start) | collective-permute-done | bytes 114720 | tf_op jit(solution)/shard_map/ppermute | solution.py:237
  4.2 2.7 %collective-permute-start.1 = (f32[7,8,128]{2,1,0:T(8,128)S(1)}, f32[7,8,128]{2,1,0:T(8,128)S(1)}, u32[]{:S(2)}, u32[]{:S(2)}) collective-permute-start(f32[7,8,128]{2,1,0:T(8,128)S(1)} %get-tuple-element.25), channel_id=1, source_target_pairs={{0,10},{1,11},{2,8},{3,9},{4,14},{5,15},{6,12},{7,13},{8,26},{9,27... | collective-permute-start | bytes 86024 | tf_op jit(solution)/shard_map/ppermute | solution.py:237
  6.9 2.4 %collective-permute-start.2 = (f32[7,8,128]{2,1,0:T(8,128)S(1)}, f32[7,8,128]{2,1,0:T(8,128)S(1)}, u32[]{:S(2)}, u32[]{:S(2)}) collective-permute-start(f32[7,8,128]{2,1,0:T(8,128)S(1)} %get-tuple-element.26), channel_id=1, source_target_pairs={{0,26},{1,27},{2,24},{3,25},{4,30},{5,31},{6,28},{7,29},{8,18},{9,... | collective-permute-start | bytes 86024 | tf_op jit(solution)/shard_map/ppermute | solution.py:237
  9.3 1.3 %collective-permute-start.3 = (f32[7,8,128]{2,1,0:T(8,128)S(1)}, f32[7,8,128]{2,1,0:T(8,128)S(1)}, u32[]{:S(2)}, u32[]{:S(2)}) collective-permute-start(f32[7,8,128]{2,1,0:T(8,128)S(1)} %get-tuple-element.27), channel_id=1, source_target_pairs={{0,18},{1,19},{2,16},{3,17},{4,22},{5,23},{6,20},{7,21},{8,2},{9,3... | collective-permute-start | bytes 86024 | tf_op jit(solution)/shard_map/ppermute | solution.py:237
  10.7 2.0 %shard_map.49 = (bf16[640,1280]{1,0:T(8,128)(2,1)S(1)}, bf16[640,1280]{1,0:T(8,128)(2,1)S(1)}, f32[8,128]{1,0:T(8,128)S(1)}) custom-call(f32[7,8,128]{2,1,0:T(8,128)S(1)} %get-tuple-element.24._.own_ref, f32[2,320,1280]{2,1,0:T(8,128)} %w_hbm.1), custom_call_target="tpu_custom_call" | custom-call | flops 6553600 | bytes 6553600 | tf_op jit(solution)/shard_map/pallas_call | solution.py:309
  13.1 2.2 %collective-permute-start.4 = (f32[7,8,128]{2,1,0:T(8,128)S(1)}, f32[7,8,128]{2,1,0:T(8,128)S(1)}, u32[]{:S(2)}, u32[]{:S(2)}) collective-permute-start(f32[7,8,128]{2,1,0:T(8,128)S(1)} %shard_map.50._.own_ref), channel_id=1, source_target_pairs={{0,7},{1,6},{2,5},{3,4},{4,3},{5,2},{6,1},{7,0},{8,15},{9,14},{10,... | collective-permute-start | bytes 86024 | tf_op jit(solution)/shard_map/ppermute | solution.py:237
  15.3 0.6 %collective-permute-start.5 = (f32[7,8,128]{2,1,0:T(8,128)S(1)}, f32[7,8,128]{2,1,0:T(8,128)S(1)}, u32[]{:S(2)}, u32[]{:S(2)}) collective-permute-start(f32[7,8,128]{2,1,0:T(8,128)S(1)} %shard_map.50._.own_ref), channel_id=1, source_target_pairs={{0,6},{1,7},{2,4},{3,5},{4,2},{5,3},{6,0},{7,1},{8,14},{9,15},{10,... | collective-permute-start | bytes 86024 | tf_op jit(solution)/shard_map/ppermute | solution.py:237
  16.1 0.9 %shard_map.51 = (bf16[1280,640]{1,0:T(8,128)(2,1)S(1)}, bf16[1280,640]{1,0:T(8,128)(2,1)S(1)}, f32[8,128]{1,0:T(8,128)S(1)}) custom-call(f32[7,8,128]{2,1,0:T(8,128)S(1)} %shard_map.50._.own_ref, f32[2,320,1280]{2,1,0:T(8,128)S(1)} %get-tuple-element.29.w_ref), custom_call_target="tpu_custom_call" | custom-call | flops 6553600 | bytes 6553600 | tf_op jit(solution)/shard_map/pallas_call | solution.py:321
  17.3 1.2 %collective-permute-done.5.refs_1_ = f32[7,8,128]{2,1,0:T(8,128)S(1)} collective-permute-done((f32[7,8,128]{2,1,0:T(8,128)S(1)}, f32[7,8,128]{2,1,0:T(8,128)S(1)}, u32[]{:S(2)}, u32[]{:S(2)}) %collective-permute-start.5) | collective-permute-done | bytes 28704 | tf_op jit(solution)/shard_map/ppermute | solution.py:237
  18.6 0.6 %collective-permute-done.6.refs_2_ = f32[7,8,128]{2,1,0:T(8,128)S(1)} collective-permute-done((f32[7,8,128]{2,1,0:T(8,128)S(1)}, f32[7,8,128]{2,1,0:T(8,128)S(1)}, u32[]{:S(2)}, u32[]{:S(2)}) %collective-permute-start.6) | collective-permute-done | bytes 28704 | tf_op jit(solution)/shard_map/ppermute | solution.py:237
  19.4 1.1 %collective-permute-done.7.got_ref = f32[2,7,8,128]{3,2,1,0:T(8,128)S(1)} collective-permute-done((f32[2,7,8,128]{3,2,1,0:T(8,128)S(1)}, f32[2,7,8,128]{3,2,1,0:T(8,128)S(1)}, u32[]{:S(2)}, u32[]{:S(2)}) %collective-permute-start.7) | collective-permute-done | bytes 57376 | tf_op jit(solution)/shard_map/ppermute | solution.py:237
  20.5 1.0 %shard_map.53.mine_ref = f32[10,8,128]{2,1,0:T(8,128)S(1)} custom-call(f32[2,7,8,128]{3,2,1,0:T(8,128)S(1)} %shard_map.52.sent_ref, f32[2,7,8,128]{3,2,1,0:T(8,128)S(1)} %collective-permute-done.7.got_ref, bf16[1280,640]{1,0:T(8,128)(2,1)S(1)} %get-tuple-element.31.in_high_ref, bf16[1280,640]{1,0:T(8,128)(2,1)S(1)} %get-tuple-element.32.in_low_ref, ...), custom_call_target="tpu_custom_call" | custom-call | tf_op jit(solution)/shard_map/pallas_call | solution.py:299
  21.7 1.1 %collective-permute-done.8.theirs_ref = f32[10,8,128]{2,1,0:T(8,128)S(1)} collective-permute-done((f32[10,8,128]{2,1,0:T(8,128)S(1)}, f32[10,8,128]{2,1,0:T(8,128)S(1)}, u32[]{:S(2)}, u32[]{:S(2)}) %collective-permute-start.8) | collective-permute-done | bytes 40992 | tf_op jit(solution)/shard_map/ppermute | solution.py:237
  22.8 1.3 %collective-permute-start.10 = (f32[5,8,128]{2,1,0:T(8,128)S(1)}, f32[5,8,128]{2,1,0:T(8,128)S(1)}, u32[]{:S(2)}, u32[]{:S(2)}) collective-permute-start(f32[5,8,128]{2,1,0:T(8,128)S(1)} %get-tuple-element.36), channel_id=1, source_target_pairs={{0,7},{1,6},{2,5},{3,4},{4,3},{5,2},{6,1},{7,0},{8,15},{9,14},{10,... | collective-permute-start | bytes 61448 | tf_op jit(solution)/shard_map/ppermute | solution.py:237
  24.5 1.3 %collective-permute-start.9 = (f32[5,8,128]{2,1,0:T(8,128)S(1)}, f32[5,8,128]{2,1,0:T(8,128)S(1)}, u32[]{:S(2)}, u32[]{:S(2)}) collective-permute-start(f32[5,8,128]{2,1,0:T(8,128)S(1)} %get-tuple-element.36), channel_id=1, source_target_pairs={{0,3},{1,2},{2,1},{3,0},{4,7},{5,6},{6,5},{7,4},{8,11},{9,10},{10,... | collective-permute-start | bytes 61448 | tf_op jit(solution)/shard_map/ppermute | solution.py:237
  25.7 1.1 %collective-permute-done.10.refs_1_ = f32[5,8,128]{2,1,0:T(8,128)S(1)} collective-permute-done((f32[5,8,128]{2,1,0:T(8,128)S(1)}, f32[5,8,128]{2,1,0:T(8,128)S(1)}, u32[]{:S(2)}, u32[]{:S(2)}) %collective-permute-start.10) | collective-permute-done | bytes 20512 | tf_op jit(solution)/shard_map/ppermute | solution.py:237
  27.7 0.6 %collective-permute-start.12 = (f32[5,8,128]{2,1,0:T(8,128)S(1)}, f32[5,8,128]{2,1,0:T(8,128)S(1)}, u32[]{:S(2)}, u32[]{:S(2)}) collective-permute-start(f32[5,8,128]{2,1,0:T(8,128)S(1)} %shard_map.55.own_ref), channel_id=1, source_target_pairs={{0,10},{1,11},{2,8},{3,9},{4,14},{5,15},{6,12},{7,13},{8,18},{9,19... | collective-permute-start | bytes 61448 | tf_op jit(solution)/shard_map/ppermute | solution.py:237
  28.3 1.3 %collective-permute-start.13 = (f32[5,8,128]{2,1,0:T(8,128)S(1)}, f32[5,8,128]{2,1,0:T(8,128)S(1)}, u32[]{:S(2)}, u32[]{:S(2)}) collective-permute-start(f32[5,8,128]{2,1,0:T(8,128)S(1)} %shard_map.55.own_ref), channel_id=1, source_target_pairs={{0,18},{1,19},{2,16},{3,17},{4,22},{5,23},{6,20},{7,21},{8,26},{9,... | collective-permute-start | bytes 61448 | tf_op jit(solution)/shard_map/ppermute | solution.py:237
  29.6 2.6 %collective-permute-start.14 = (f32[5,8,128]{2,1,0:T(8,128)S(1)}, f32[5,8,128]{2,1,0:T(8,128)S(1)}, u32[]{:S(2)}, u32[]{:S(2)}) collective-permute-start(f32[5,8,128]{2,1,0:T(8,128)S(1)} %shard_map.55.own_ref), channel_id=1, source_target_pairs={{0,26},{1,27},{2,24},{3,25},{4,30},{5,31},{6,28},{7,29},{8,2},{9,3... | collective-permute-start | bytes 61448 | tf_op jit(solution)/shard_map/ppermute | solution.py:237
  32.8 0.9 %collective-permute-done.14.refs_3_ = f32[5,8,128]{2,1,0:T(8,128)S(1)} collective-permute-done((f32[5,8,128]{2,1,0:T(8,128)S(1)}, f32[5,8,128]{2,1,0:T(8,128)S(1)}, u32[]{:S(2)}, u32[]{:S(2)}) %collective-permute-start.14) | collective-permute-done | bytes 20512 | tf_op jit(solution)/shard_map/ppermute | solution.py:237
  33.7 1.0 %shard_map.57.refs_0_ = f32[224,1280]{1,0:T(8,128)} custom-call(bf16[224,96]{1,0:T(8,128)(2,1)S(1)} %shard_map.47.refs_0_.combine_ref, f32[5,8,128]{2,1,0:T(8,128)S(1)} %collective-permute-done.15.refs_4_.own_ref, f32[3,5,8,128]{3,2,1,0:T(8,128)S(1)} %shard_map.56.others_ref), custom_call_target="tpu_custom_call" | custom-call | tf_op jit(solution)/shard_map/pallas_call | solution.py:343
  35.0 1.0 %shard_map.58 = f32[224,1280]{1,0:T(8,128)} custom-call(bf16[224,96]{1,0:T(8,128)(2,1)S(1)} %shard_map.47.refs_0_.combine_ref, f32[5,8,128]{2,1,0:T(8,128)S(1)} %shard_map.55.own_ref, f32[3,5,8,128]{3,2,1,0:T(8,128)S(1)} %collective-permute-done.16.others_ref, f32[224,1280]{1,0:T(8,128)} %shard_map.57.refs_0_), custom_call_target="tpu_custom_call", output_to_operand_aliasing={{}: (3, {})} | custom-call | tf_op jit(solution)/shard_map/pallas_call | solution.py:343
  (23 shorter events, 3.5 us)
Async XLA Ops:
  2.7 1.5 %collective-permute-start = (f32[4,7,8,128]{3,2,1,0:T(8,128)S(1)}, f32[4,7,8,128]{3,2,1,0:T(8,128)S(1)}, u32[]{:S(2)}, u32[]{:S(2)}) collective-permute-start(f32[4,7,8,128]{3,2,1,0:T(8,128)S(1)} %get-tuple-element.23), channel_id=1, source_target_pairs={{0,2},{1,3},{2,0},{3,1},{4,6},{5,7},{6,4},{7,5},{8,10},{9,11},{10,... | collective-permute-start | bytes 344072 | tf_op jit(solution)/shard_map/ppermute | solution.py:237
  4.2 8.5 %collective-permute-start.1 = (f32[7,8,128]{2,1,0:T(8,128)S(1)}, f32[7,8,128]{2,1,0:T(8,128)S(1)}, u32[]{:S(2)}, u32[]{:S(2)}) collective-permute-start(f32[7,8,128]{2,1,0:T(8,128)S(1)} %get-tuple-element.25), channel_id=1, source_target_pairs={{0,10},{1,11},{2,8},{3,9},{4,14},{5,15},{6,12},{7,13},{8,26},{9,27... | collective-permute-start | bytes 86024 | tf_op jit(solution)/shard_map/ppermute | solution.py:237
  6.9 5.8 %collective-permute-start.2 = (f32[7,8,128]{2,1,0:T(8,128)S(1)}, f32[7,8,128]{2,1,0:T(8,128)S(1)}, u32[]{:S(2)}, u32[]{:S(2)}) collective-permute-start(f32[7,8,128]{2,1,0:T(8,128)S(1)} %get-tuple-element.26), channel_id=1, source_target_pairs={{0,26},{1,27},{2,24},{3,25},{4,30},{5,31},{6,28},{7,29},{8,18},{9,... | collective-permute-start | bytes 86024 | tf_op jit(solution)/shard_map/ppermute | solution.py:237
  9.3 3.7 %collective-permute-start.3 = (f32[7,8,128]{2,1,0:T(8,128)S(1)}, f32[7,8,128]{2,1,0:T(8,128)S(1)}, u32[]{:S(2)}, u32[]{:S(2)}) collective-permute-start(f32[7,8,128]{2,1,0:T(8,128)S(1)} %get-tuple-element.27), channel_id=1, source_target_pairs={{0,18},{1,19},{2,16},{3,17},{4,22},{5,23},{6,20},{7,21},{8,2},{9,3... | collective-permute-start | bytes 86024 | tf_op jit(solution)/shard_map/ppermute | solution.py:237
  13.1 4.3 %collective-permute-start.4 = (f32[7,8,128]{2,1,0:T(8,128)S(1)}, f32[7,8,128]{2,1,0:T(8,128)S(1)}, u32[]{:S(2)}, u32[]{:S(2)}) collective-permute-start(f32[7,8,128]{2,1,0:T(8,128)S(1)} %shard_map.50._.own_ref), channel_id=1, source_target_pairs={{0,7},{1,6},{2,5},{3,4},{4,3},{5,2},{6,1},{7,0},{8,15},{9,14},{10,... | collective-permute-start | bytes 86024 | tf_op jit(solution)/shard_map/ppermute | solution.py:237
  15.3 3.3 %collective-permute-start.5 = (f32[7,8,128]{2,1,0:T(8,128)S(1)}, f32[7,8,128]{2,1,0:T(8,128)S(1)}, u32[]{:S(2)}, u32[]{:S(2)}) collective-permute-start(f32[7,8,128]{2,1,0:T(8,128)S(1)} %shard_map.50._.own_ref), channel_id=1, source_target_pairs={{0,6},{1,7},{2,4},{3,5},{4,2},{5,3},{6,0},{7,1},{8,14},{9,15},{10,... | collective-permute-start | bytes 86024 | tf_op jit(solution)/shard_map/ppermute | solution.py:237
  15.8 3.3 %collective-permute-start.6 = (f32[7,8,128]{2,1,0:T(8,128)S(1)}, f32[7,8,128]{2,1,0:T(8,128)S(1)}, u32[]{:S(2)}, u32[]{:S(2)}) collective-permute-start(f32[7,8,128]{2,1,0:T(8,128)S(1)} %shard_map.50._.own_ref), channel_id=1, source_target_pairs={{0,3},{1,2},{2,1},{3,0},{4,7},{5,6},{6,5},{7,4},{8,11},{9,10},{10,... | collective-permute-start | bytes 86024 | tf_op jit(solution)/shard_map/ppermute | solution.py:237
  19.2 1.3 %collective-permute-start.7 = (f32[2,7,8,128]{3,2,1,0:T(8,128)S(1)}, f32[2,7,8,128]{3,2,1,0:T(8,128)S(1)}, u32[]{:S(2)}, u32[]{:S(2)}) collective-permute-start(f32[2,7,8,128]{3,2,1,0:T(8,128)S(1)} %shard_map.52.sent_ref), channel_id=1, source_target_pairs={{0,2},{1,3},{2,0},{3,1},{4,6},{5,7},{6,4},{7,5},{8,10},{9,11},{10,... | collective-permute-start | bytes 172040 | tf_op jit(solution)/shard_map/ppermute | solution.py:237
  21.5 1.2 %collective-permute-start.8 = (f32[10,8,128]{2,1,0:T(8,128)S(1)}, f32[10,8,128]{2,1,0:T(8,128)S(1)}, u32[]{:S(2)}, u32[]{:S(2)}) collective-permute-start(f32[10,8,128]{2,1,0:T(8,128)S(1)} %shard_map.53.mine_ref), channel_id=1, source_target_pairs={{0,2},{1,3},{2,0},{3,1},{4,6},{5,7},{6,4},{7,5},{8,10},{9,11},{10,... | collective-permute-start | bytes 122888 | tf_op jit(solution)/shard_map/ppermute | solution.py:237
  22.8 4.1 %collective-permute-start.10 = (f32[5,8,128]{2,1,0:T(8,128)S(1)}, f32[5,8,128]{2,1,0:T(8,128)S(1)}, u32[]{:S(2)}, u32[]{:S(2)}) collective-permute-start(f32[5,8,128]{2,1,0:T(8,128)S(1)} %get-tuple-element.36), channel_id=1, source_target_pairs={{0,7},{1,6},{2,5},{3,4},{4,3},{5,2},{6,1},{7,0},{8,15},{9,14},{10,... | collective-permute-start | bytes 61448 | tf_op jit(solution)/shard_map/ppermute | solution.py:237
  24.0 3.2 %collective-permute-start.11 = (f32[5,8,128]{2,1,0:T(8,128)S(1)}, f32[5,8,128]{2,1,0:T(8,128)S(1)}, u32[]{:S(2)}, u32[]{:S(2)}) collective-permute-start(f32[5,8,128]{2,1,0:T(8,128)S(1)} %get-tuple-element.36), channel_id=1, source_target_pairs={{0,6},{1,7},{2,4},{3,5},{4,2},{5,3},{6,0},{7,1},{8,14},{9,15},{10,... | collective-permute-start | bytes 61448 | tf_op jit(solution)/shard_map/ppermute | solution.py:237
  24.5 3.2 %collective-permute-start.9 = (f32[5,8,128]{2,1,0:T(8,128)S(1)}, f32[5,8,128]{2,1,0:T(8,128)S(1)}, u32[]{:S(2)}, u32[]{:S(2)}) collective-permute-start(f32[5,8,128]{2,1,0:T(8,128)S(1)} %get-tuple-element.36), channel_id=1, source_target_pairs={{0,3},{1,2},{2,1},{3,0},{4,7},{5,6},{6,5},{7,4},{8,11},{9,10},{10,... | collective-permute-start | bytes 61448 | tf_op jit(solution)/shard_map/ppermute | solution.py:237
  27.7 5.1 %collective-permute-start.12 = (f32[5,8,128]{2,1,0:T(8,128)S(1)}, f32[5,8,128]{2,1,0:T(8,128)S(1)}, u32[]{:S(2)}, u32[]{:S(2)}) collective-permute-start(f32[5,8,128]{2,1,0:T(8,128)S(1)} %shard_map.55.own_ref), channel_id=1, source_target_pairs={{0,10},{1,11},{2,8},{3,9},{4,14},{5,15},{6,12},{7,13},{8,18},{9,19... | collective-permute-start | bytes 61448 | tf_op jit(solution)/shard_map/ppermute | solution.py:237
  28.3 4.5 %collective-permute-start.13 = (f32[5,8,128]{2,1,0:T(8,128)S(1)}, f32[5,8,128]{2,1,0:T(8,128)S(1)}, u32[]{:S(2)}, u32[]{:S(2)}) collective-permute-start(f32[5,8,128]{2,1,0:T(8,128)S(1)} %shard_map.55.own_ref), channel_id=1, source_target_pairs={{0,18},{1,19},{2,16},{3,17},{4,22},{5,23},{6,20},{7,21},{8,26},{9,... | collective-permute-start | bytes 61448 | tf_op jit(solution)/shard_map/ppermute | solution.py:237
  29.6 4.0 %collective-permute-start.14 = (f32[5,8,128]{2,1,0:T(8,128)S(1)}, f32[5,8,128]{2,1,0:T(8,128)S(1)}, u32[]{:S(2)}, u32[]{:S(2)}) collective-permute-start(f32[5,8,128]{2,1,0:T(8,128)S(1)} %shard_map.55.own_ref), channel_id=1, source_target_pairs={{0,26},{1,27},{2,24},{3,25},{4,30},{5,31},{6,28},{7,29},{8,2},{9,3... | collective-permute-start | bytes 61448 | tf_op jit(solution)/shard_map/ppermute | solution.py:237
  32.1 1.5 %collective-permute-start.15 = (f32[5,8,128]{2,1,0:T(8,128)S(1)}, f32[5,8,128]{2,1,0:T(8,128)S(1)}, u32[]{:S(2)}, u32[]{:S(2)}) collective-permute-start(f32[5,8,128]{2,1,0:T(8,128)S(1)} %shard_map.55.own_ref), channel_id=1, source_target_pairs={{0,2},{1,3},{2,0},{3,1},{4,6},{5,7},{6,4},{7,5},{8,10},{9,11},{10,... | collective-permute-start | bytes 61448 | tf_op jit(solution)/shard_map/ppermute | solution.py:237
  33.6 1.3 %collective-permute-start.16 = (f32[3,5,8,128]{3,2,1,0:T(8,128)S(1)}, f32[3,5,8,128]{3,2,1,0:T(8,128)S(1)}, u32[]{:S(2)}, u32[]{:S(2)}) collective-permute-start(f32[3,5,8,128]{3,2,1,0:T(8,128)S(1)} %shard_map.56.others_ref), channel_id=1, source_target_pairs={{0,2},{1,3},{2,0},{3,1},{4,6},{5,7},{6,4},{7,5},{8,10},{9,11},{10,... | collective-permute-start | bytes 184328 | tf_op jit(solution)/shard_map/ppermute | solution.py:237
